TPU v7x, 32 devices: a whole 2x2x4 slice. The times are simulated.
32 devices in a mesh: smp: 16 (over z, x, core), par: 2 (over y).
Axes of the slice: x: 2, y: 2, z: 4, core: 2. Of those that a mesh axis runs over, the one named last changes fastest.
Arguments:
- log_derivs: float32 [4096, 2048], P('smp', 'par'), may hold values from -40 to 40, as said below
- coefficients: float32 [4096], P('smp'), may hold values from -6 to 6
Outputs:
- gram: float32 [4096, 4096], P('smp', 'par')
- update: float32 [2048], P(('par', 'smp'))
Inputs may be any that keep to these rules, and one draw needn't show every extreme that they name: `log_derivs`: finite real values.
All inputs are finite; a program needn't handle non-finite values.
Results may differ from a plain program's by a relative error of at most 0.00014.
Values sent between devices are 32-bit elements; how exact they have to be, the bound alone decides.
No kernel may reach another device: no remote copies, remote signals or barrier semaphores. Data moves between devices by JAX's collectives and lax.ppermute only.
A program may use at most 128 MiB of HBM per device.

v0:
```python
import jax
import jax.numpy as jnp
from jax import lax
from jax.sharding import PartitionSpec as P


def row_products(left_rows, right_rows):
    return lax.dot_general(
        left_rows,
        right_rows,
        (((1,), (1,)), ((), ())),
        precision=lax.Precision.HIGHEST,
        preferred_element_type=jnp.float32,
    )


def local(log_derivs, coefficients):
    samples = log_derivs.shape[0] * lax.axis_size("smp")
    column_total = lax.psum(jnp.sum(log_derivs, axis=0), "smp")
    centred = (log_derivs - column_total[None, :] / samples) / jnp.sqrt(jnp.float32(samples))
    partial_gram = row_products(centred, lax.all_gather(centred, "smp", axis=0, tiled=True))
    gram = lax.psum_scatter(partial_gram, "par", scatter_dimension=1, tiled=True)
    update_term = lax.dot_general(
        coefficients,
        centred,
        (((0,), (0,)), ((), ())),
        precision=lax.Precision.HIGHEST,
        preferred_element_type=jnp.float32,
    )
    update = lax.psum_scatter(update_term, "smp", scatter_dimension=0, tiled=True)
    return (gram, update)


def solution(mesh):
    placed = (P("smp", "par"), P("smp"))
    return jax.shard_map(
        local,
        mesh=mesh,
        in_specs=placed,
        out_specs=(P("smp", "par"), P(("par", "smp"))),
        check_vma=False,
    )
```

profile of v0, /device:TPU:0, one launch (start us, length us, event | category | flops | bytes accessed | tf_op | source)
XLA Modules:
  0.0 248.0 jit_solution(4594640960496671880)
XLA Ops:
  7.2 0.0 copy-start
  7.2 0.0 copy-start.2
  7.2 0.0 all-gather.2.cloned.1.call-start
  7.2 1.3 reduce_sum.9
  8.5 34.9 %psum.7 = f32[1024]{0:T(1024)S(1)} all-reduce(f32[1024]{0:T(1024)S(1)} %reduce_sum.9), channel_id=1, replica_groups=mesh['smp'=16,'par'=2] {'smp'}, use_global_device_ids=true, to_apply=%region_1.0 | all-reduce | flops 1024 | bytes 8192 | tf_op jit(solution)/shard_map/psum | solution.py:19
  43.5 2.4 subtract_multiply_fusion
  45.8 0.0 copy-start.1
  45.8 0.0 all-gather.2.cloned.1.call-update
  45.8 0.0 reduce-scatter.2.cloned.1.call-start
  45.9 124.3 %all-gather.2.cloned.1.call-done = f32[4096,1024]{1,0:T(8,128)} async-done(((f32[256,1024]{1,0:T(8,128)}), f32[4096,1024]{1,0:T(8,128)}) %all-gather.2.cloned.1.call-update) | async-done | bytes 16777232 | tf_op jit(solution)/shard_map/all_gather | solution.py:21
  170.2 18.3 %fusion = f32[256,4096]{1,0:T(8,128)} fusion(f32[256,1024]{1,0:T(8,128)} %subtract_multiply_fusion, f32[4096,1024]{1,0:T(8,128)} %all-gather.2.cloned.1.call-done), kind=kOutput, calls=%fused_computation.2 | convolution fusion | flops 12884901888 | bytes 22020096 | tf_op jit(solution)/shard_map/dot_general | solution.py:8
  188.5 0.0 reduce-scatter.2.cloned.1.call-update
  188.5 0.0 copy-done.2
  188.5 0.6 dynamic-slice
  189.8 0.0 copy-done
  189.8 0.0 copy-done.1
  189.8 0.6 fusion.1
  190.4 30.6 %all-reduce = f32[1024]{0:T(1024)S(1)} all-reduce(f32[1024]{0:T(1024)S(1)} %bitcast.8), channel_id=3, replica_groups=mesh['smp'=16,'par'=2] {'smp'}, use_global_device_ids=true, to_apply=%region_3.0.clone | all-reduce | flops 1024 | bytes 8192
  221.1 0.6 dynamic-slice.1
  221.7 19.5 %reduce-scatter.2.cloned.1.call-done = f32[256,2048]{1,0:T(8,128)} async-done(((f32[256,4096]{1,0:T(8,128)}), f32[256,2048]{1,0:T(8,128)}) %reduce-scatter.2.cloned.1.call-update) | async-done | bytes 2097168 | tf_op jit(solution)/shard_map/reduce_scatter | solution.py:22
  (1 shorter events, 0.0 us)
Async XLA Ops:
  7.2 182.6 %copy-start = (f32[256]{0:T(256)S(1)}, f32[256]{0:T(256)}, u32[]{:S(2)}) copy-start(f32[256]{0:T(256)} %param.3) | copy-start | bytes 3076
  7.2 181.3 %copy-start.2 = (u32[32]{0:T(128)S(1)}, u32[32]{0:T(128)}, u32[]{:S(2)}) copy-start(u32[32]{0:T(128)} %constant.10) | copy-start | bytes 388
  7.2 163.0 %all-gather.2.cloned.1.call-start = ((), (), s32[]{:S(2)}) async-start(), calls=%async_computation.1 | async-start | bytes 17825792 | tf_op jit(solution)/shard_map/all_gather | solution.py:21
  45.8 144.0 %copy-start.1 = (f32[256,1024]{1,0:T(8,128)S(1)}, f32[256,1024]{1,0:T(8,128)}, u32[]{:S(2)}) copy-start(f32[256,1024]{1,0:T(8,128)} %subtract_multiply_fusion) | copy-start | bytes 3145732
  45.8 195.3 %reduce-scatter.2.cloned.1.call-start = ((), (), s32[]{:S(2)}) async-start(), calls=%async_computation.2 | async-start | bytes 6291456 | tf_op jit(solution)/shard_map/reduce_scatter | solution.py:22
Sparse Core Ops, SparseCore 0:
  46.0 124.1 all-gather.1
  188.6 52.4 reduce-scatter.1
where the time goes:
time: 248 us
  waiting for transfers between devices  144 us (58%)
  blocking collectives  65.5 us (26%)
  matrix products  19 us (8%)
  between operations  14.7 us (6%)
  other arithmetic  3.66 us (1%)
    all_gather x1, waiting for transfers between devices, local(): lax.all_gather(centred, 'smp', axis=0, tiled=True)  124 us
    psum x1, blocking collectives, local(): column_total = lax.psum(jnp.sum(log_derivs, axis=0), 'smp')  34.9 us
    unnamed x1, blocking collectives  30.6 us
    reduce_scatter x1, waiting for transfers between devices, local(): lax.psum_scatter(partial_gram, 'par', scatter_dimension=1, tiled=True)  19.5 us
    dot_general x1, matrix products, row_products(): lax.dot_general(left_rows, right_rows, (((1,), (1,)), ((), ())), precisio...  18.3 us
  transfers between devices with their start and end apart: 2, of which 2 were waited for; matrix products, arithmetic and copies ran while one was open for 1% of the time, Pallas kernels for 0%

commit v1 on v0

--- a/solution.py
+++ b/solution.py
@@ -1,7 +1,14 @@
+import functools
+
 import jax
 import jax.numpy as jnp
 from jax import lax
+from jax.experimental import pallas as pl
+from jax.experimental.pallas import tpu as pltpu
 from jax.sharding import PartitionSpec as P
+
+BOTH = ("smp", "par")
+VMEM_LIMIT = 40 * 1024 * 1024
 
 
 def row_products(left_rows, right_rows):
@@ -14,7 +21,7 @@
     )
 
 
-def local(log_derivs, coefficients):
+def gathered(log_derivs, coefficients):
     samples = log_derivs.shape[0] * lax.axis_size("smp")
     column_total = lax.psum(jnp.sum(log_derivs, axis=0), "smp")
     centred = (log_derivs - column_total[None, :] / samples) / jnp.sqrt(jnp.float32(samples))
@@ -31,10 +38,243 @@
     return (gram, update)
 
 
+def stats_kernel(rows_ref, coef_ref, stats_ref):
+    rows = rows_ref[...]
+    coef = coef_ref[...]
+    mean = jnp.sum(rows, axis=0, keepdims=True) / rows.shape[0]
+    stats_ref[0:1, :] = mean
+    stats_ref[1:2, :] = jnp.sum(coef * (rows - mean), axis=0, keepdims=True)
+    stats_ref[2:3, :] = jnp.broadcast_to(jnp.sum(coef, axis=0, keepdims=True), mean.shape)
+
+
+def block_stats(rows, coefficients):
+    return pl.pallas_call(
+        stats_kernel,
+        out_shape=jax.ShapeDtypeStruct((8, rows.shape[1]), jnp.float32),
+        compiler_params=pltpu.CompilerParams(vmem_limit_bytes=VMEM_LIMIT),
+        name="block_stats",
+    )(rows, coefficients[:, None])
+
+
+def merge(*parts):
+    mean = sum(p[0:1] for p in parts) / len(parts)
+    product = sum(p[1:2] + p[2:3] * (p[0:1] - mean) for p in parts)
+    total = sum(p[2:3] for p in parts)
+    return jnp.concatenate([mean, product, total, jnp.zeros((5, mean.shape[1]), jnp.float32)], axis=0)
+
+
+def split(values):
+    high = values.astype(jnp.bfloat16)
+    return high, (values - high.astype(jnp.float32)).astype(jnp.bfloat16)
+
+
+def dot_nt(left, right):
+    return lax.dot_general(left, right, (((1,), (1,)), ((), ())), preferred_element_type=jnp.float32)
+
+
+def products_kernel(scale, counts, flag_ref, mean_ref, own_ref, side_ref, *refs):
+    first, second = refs[: counts[0]], refs[counts[0] : sum(counts)]
+    keep_own, keep_side, *sent = refs[sum(counts) :]
+    height = own_ref.shape[0]
+    if len(sent) == 1:
+        sent = [sent[0].at[pl.ds(0, height)], sent[0].at[pl.ds(height, height)]]
+    mean = mean_ref[0:1, :]
+    rows = [split(ref[...] - mean) for ref in (own_ref, side_ref)]
+
+    def fill(column_refs, outs):
+        at = 0
+        for ref in column_refs:
+            high, low = split(ref[...] - mean)
+            width = ref.shape[0]
+            for (row_high, row_low), out in zip(rows, outs):
+                total = dot_nt(row_high, high) + (dot_nt(row_high, low) + dot_nt(row_low, high))
+                out[:, at : at + width] = total * scale
+            at += width
+
+    @pl.when(flag_ref[0] == 1)
+    def _():
+        fill(first, (keep_own, keep_side))
+        fill(second, sent)
+
+    @pl.when(flag_ref[0] != 1)
+    def _():
+        fill(second, (keep_own, keep_side))
+        fill(first, sent)
+
+
+def products(mean, own, side, flag, first, second, samples, joined, name):
+    rows, params = own.shape
+    width = sum(block.shape[0] for block in first)
+    out = jax.ShapeDtypeStruct((rows, width), jnp.float32)
+    both = jax.ShapeDtypeStruct((2 * rows, width), jnp.float32)
+    return pl.pallas_call(
+        functools.partial(products_kernel, 1.0 / samples, (len(first), len(second))),
+        out_shape=(out, out, both) if joined else (out, out, out, out),
+        in_specs=[pl.BlockSpec(memory_space=pltpu.SMEM)]
+        + [pl.BlockSpec(memory_space=pltpu.VMEM)] * (3 + len(first) + len(second)),
+        compiler_params=pltpu.CompilerParams(vmem_limit_bytes=VMEM_LIMIT),
+        cost_estimate=pl.CostEstimate(
+            flops=24 * rows * width * params, bytes_accessed=16 * (rows + width) * params, transcendentals=0
+        ),
+        name=name,
+    )(flag, mean, own, side, *first, *second)
+
+
+def place_kernel(summands, splits, aliased, at_ref, *refs):
+    blocks = list(refs[: sum(summands)])
+    out = refs[len(blocks) + aliased]
+    *totals, sems = refs[len(blocks) + aliased + 1 :]
+    copies = []
+    for total, terms, parts in zip(totals, summands, splits):
+        taken, blocks = blocks[:terms], blocks[terms:]
+        value = taken[0][0 : total.shape[0], :]
+        for block in taken[1:]:
+            value += block[0 : total.shape[0], :]
+        total[...] = value
+        width = total.shape[1] // parts
+        for part in range(parts):
+            at = pl.multiple_of(at_ref[len(copies)] * 128, 128)
+            copy = pltpu.make_async_copy(
+                total.at[:, pl.ds(part * width, width)], out.at[:, pl.ds(at, width)], sems.at[len(copies)]
+            )
+            copy.start()
+            copies.append(copy)
+    for copy in copies:
+        copy.wait()
+
+
+def place(pieces, shape, into, name):
+    blocks = [block for terms, _ in pieces for block in terms]
+    at = jnp.stack([column for _, columns in pieces for column in columns]).astype(jnp.int32)
+    aliased = 0 if into is None else 1
+    return pl.pallas_call(
+        functools.partial(
+            place_kernel, [len(terms) for terms, _ in pieces], [len(columns) for _, columns in pieces], aliased
+        ),
+        out_shape=jax.ShapeDtypeStruct(shape, jnp.float32),
+        in_specs=[pl.BlockSpec(memory_space=pltpu.SMEM)]
+        + [pl.BlockSpec(memory_space=pltpu.VMEM)] * len(blocks)
+        + [pl.BlockSpec(memory_space=pl.ANY)] * aliased,
+        out_specs=pl.BlockSpec(memory_space=pl.ANY),
+        scratch_shapes=[pltpu.VMEM((shape[0], terms[0].shape[1]), jnp.float32) for terms, _ in pieces]
+        + [pltpu.SemaphoreType.DMA((at.shape[0],))],
+        input_output_aliases={1 + len(blocks): 0} if aliased else {},
+        compiler_params=pltpu.CompilerParams(vmem_limit_bytes=VMEM_LIMIT),
+        name=name,
+    )(at, *blocks, *([into] if aliased else []))
+
+
+def ringed(log_derivs, coefficients):
+    rows, params = log_derivs.shape
+    samples = rows * lax.axis_size("smp")
+    levels, planes = lax.axis_size("smp") // 4, lax.axis_size("par")
+    per_plane = levels // planes
+    here, plane = lax.axis_index("smp"), lax.axis_index("par")
+    level, side, core = here // 4, (here // 2) % 2, here % 2
+    half = rows // 2
+
+    def moves(to):
+        pairs = []
+        for z in range(levels):
+            for x in range(2):
+                for c in range(2):
+                    for y in range(planes):
+                        tz, tx, tc, ty = to(z, x, c, y)
+                        target = ((tz % levels) * 2 + tx) * 2 + tc
+                        pairs.append((((z * 2 + x) * 2 + c) * planes + y, target * planes + ty))
+        return pairs
+
+    ring = moves(lambda z, x, c, y: (z + 1 - 2 * c, x, c, y))
+    over_side = moves(lambda z, x, c, y: (z, 1 - x, c, y))
+    over_core = moves(lambda z, x, c, y: (z, x, 1 - c, y))
+    over_plane = moves(lambda z, x, c, y: (z, x, c, 1 - y))
+    diagonal = moves(lambda z, x, c, y: (z, 1 - x, c, 1 - y))
+    turns = [moves(lambda z, x, c, y, k=k: (z + k, x, c, y)) for k in range(1, levels)]
+
+    def send(value, pairs):
+        return lax.ppermute(value, BOTH, pairs)
+
+    one = [send(part, ring) for part in (log_derivs[:half], log_derivs[half:])]
+
+    stats = block_stats(log_derivs, coefficients)
+    stats = merge(stats, send(stats, over_core))
+    stats = merge(stats, send(stats, over_side))
+    stats = merge(stats, *[send(stats, turn) for turn in turns])
+    share = params // lax.axis_size("smp")
+    update = lax.dynamic_slice(stats, (1, here * share), (1, share))[0] / jnp.sqrt(jnp.float32(samples))
+
+    side_rows = send(log_derivs, over_side)
+    core_rows = send(log_derivs, over_core)
+    two = [send(part, ring) for part in one]
+    one_core = [send(part, over_core) for part in one]
+    three = [send(part, ring) for part in two]
+    two_core = [send(part, over_core) for part in two]
+    three_core = [send(part, over_core) for part in three]
+
+    near = (level - 1 + 2 * core + levels) % levels
+    far = (level + 1 - 2 * core + levels) % levels
+    across = (level + levels // 2) % levels
+
+    def kept(z):
+        return z // per_plane == plane
+
+    def column(z, x, c, part=0):
+        return (((z % per_plane) * 2 + x) * 2 + c) * (rows // 128) + part * (half // 128)
+
+    product = functools.partial(products, stats, log_derivs, side_rows, samples=samples)
+    shape = (rows, rows * 4 * per_plane)
+
+    keep_own, keep_side, sent = product(
+        kept(near).astype(jnp.int32)[None], one, one_core, joined=True, name="products_one"
+    )
+    got = send(sent, over_plane)
+    from_side = send(keep_side + got[rows:], over_side)
+    z = jnp.where(kept(near), near, far)
+    c = jnp.where(kept(near), core, 1 - core)
+    pieces = [((keep_own, got), [column(z, side, c)]), ((from_side,), [column(z, 1 - side, c)])]
+
+    keep_own, keep_side, sent = product(
+        kept(level).astype(jnp.int32)[None],
+        [log_derivs, core_rows],
+        [*two, *two_core],
+        joined=True,
+        name="products_two",
+    )
+    got = send(sent, over_plane)
+    from_side = send(keep_side + got[rows:], over_side)
+    z = jnp.where(kept(level), level, across)
+    pieces += [
+        ((keep_own, got), [column(z, side, core), column(z, side, 1 - core)]),
+        ((from_side,), [column(z, 1 - side, core), column(z, 1 - side, 1 - core)]),
+    ]
+    gram = place(pieces, shape, None, "place_most")
+
+    z = jnp.where(kept(far), far, near)
+    c = jnp.where(kept(far), core, 1 - core)
+    pieces = []
+    for part in range(2):
+        keep_own, keep_side, send_own, send_side = product(
+            kept(far).astype(jnp.int32)[None],
+            [three[part]],
+            [three_core[part]],
+            joined=False,
+            name="products_three",
+        )
+        got_own = send(send_own, over_plane)
+        got_side = send(send_side, diagonal)
+        from_side = send(keep_side, over_side)
+        pieces += [
+            ((keep_own, got_own), [column(z, side, c, part)]),
+            ((from_side, got_side), [column(z, 1 - side, c, part)]),
+        ]
+    return (place(pieces, shape, gram, "place_last"), update)
+
+
 def solution(mesh):
     placed = (P("smp", "par"), P("smp"))
+    levels, planes = mesh.shape["smp"] // 4, mesh.shape["par"]
     return jax.shard_map(
-        local,
+        ringed if planes == 2 and levels == 2 * planes else gathered,
         mesh=mesh,
         in_specs=placed,
         out_specs=(P("smp", "par"), P(("par", "smp"))),

time: 248 us -> 138 us (0.56)
  waiting for transfers between devices: 144 us -> 70.5 us
  blocking collectives: 65.5 us -> 0 us
  starting transfers between devices: 0.08 us -> 27.6 us
  Pallas kernels: 0 us -> 26.6 us
  matrix products: 19 us -> 0 us
  between operations: 14.7 us -> 0.98 us
  local copies, waits for them, and re-layouts: 1.19 us -> 9.8 us
    all_gather x1 -> x0, waiting for transfers between devices: 124 us -> none  [local(): lax.all_gather(centred, 'smp', axis=0, tiled=True)]
    ppermute x0 -> x29, waiting for transfers between devices: none -> 70.5 us  [send(): return lax.ppermute(value, BOTH, pairs)]
    psum x1 -> x0, blocking collectives: 34.9 us -> none  [local(): column_total = lax.psum(jnp.sum(log_derivs, axis=0), 'smp')]
    unnamed x1 -> x0, blocking collectives: 30.6 us -> none
    ppermute x0 -> x29, starting transfers between devices: none -> 27.6 us  [send(): return lax.ppermute(value, BOTH, pairs)]
    pallas_call x0 -> x7, Pallas kernels: none -> 26.6 us  [the longest x4 22.1 us: products(): pl.pallas_call(functools.partial(products_kernel, 1.0 / samples, (len(fir...]
    reduce_scatter x1 -> x0, waiting for transfers between devices: 19.5 us -> none  [local(): lax.psum_scatter(partial_gram, 'par', scatter_dimension=1, tiled=True)]
    dot_general x2 -> x0, matrix products: 19 us -> none  [the longest x1 18.3 us: row_products(): lax.dot_general(left_rows, right_rows, (((1,), (1,)), ((), ())), precisio...]
  transfers between devices with their start and end apart: 2 -> 29, of which waited for: 2 -> 14; matrix products, arithmetic and copies ran while one was open for 1% -> 2% of each run, Pallas kernels for 0% -> 12%
where the time goes in v1:
time: 138 us
  waiting for transfers between devices  70.5 us (51%)
  starting transfers between devices  27.6 us (20%)
  Pallas kernels  26.6 us (19%)
  local copies, waits for them, and re-layouts  9.8 us (7%)
  other arithmetic  2.58 us (2%)
    ppermute x29, waiting for transfers between devices, send(): return lax.ppermute(value, BOTH, pairs)  70.5 us
    ppermute x29, starting transfers between devices, send(): return lax.ppermute(value, BOTH, pairs)  27.6 us
    pallas_call x4, Pallas kernels, products(): pl.pallas_call(functools.partial(products_kernel, 1.0 / samples, (len(fir...  22.1 us
    unnamed x28, local copies, waits for them, and re-layouts  7.13 us
    pallas_call x2, Pallas kernels, place(): pl.pallas_call(functools.partial(place_kernel, [len(terms) for terms, _ i...  4.26 us
  transfers between devices with their start and end apart: 29, of which 14 were waited for; matrix products, arithmetic and copies ran while one was open for 2% of the time, Pallas kernels for 12%

profile of v1, /device:TPU:0, one launch (start us, length us, event | category | flops | bytes accessed | tf_op | source)
XLA Modules:
  0.0 138.0 jit_solution(16812252708644078414)
XLA Ops:
  0.6 2.4 %fusion.5 = (f32[128,1024]{1,0:T(8,128)}, f32[128,1024]{1,0:T(8,128)}) fusion(f32[256,1024]{1,0:T(8,128)} %refs_0_.1), kind=kLoop, calls=%fused_computation.24 | loop fusion | bytes 2097152 | tf_op jit(solution)/shard_map/slice | solution.py:197
  3.0 3.0 %collective-permute-start.6 = (f32[128,1024]{1,0:T(8,128)}, f32[128,1024]{1,0:T(8,128)}, u32[]{:S(2)}, u32[]{:S(2)}) collective-permute-start(f32[128,1024]{1,0:T(8,128)} %get-tuple-element.37), channel_id=1, source_target_pairs={{0,8},{1,9},{2,26},{3,27},{4,12},{5,13},{6,30},{7,31},{8,16},{9,17... | collective-permute-start | bytes 1572872 | tf_op jit(solution)/shard_map/ppermute | solution.py:195
  6.1 1.6 %collective-permute-start.13 = (f32[128,1024]{1,0:T(8,128)}, f32[128,1024]{1,0:T(8,128)}, u32[]{:S(2)}, u32[]{:S(2)}) collective-permute-start(f32[128,1024]{1,0:T(8,128)} %get-tuple-element.36), channel_id=1, source_target_pairs={{0,8},{1,9},{2,26},{3,27},{4,12},{5,13},{6,30},{7,31},{8,16},{9,17... | collective-permute-start | bytes 1572872 | tf_op jit(solution)/shard_map/ppermute | solution.py:195
  8.2 1.5 %collective-permute-start.5 = (f32[256,1024]{1,0:T(8,128)S(1)}, f32[256,1024]{1,0:T(8,128)S(1)}, u32[]{:S(2)}, u32[]{:S(2)}) collective-permute-start(f32[256,1024]{1,0:T(8,128)S(1)} %copy-done), channel_id=1, source_target_pairs={{0,4},{1,5},{2,6},{3,7},{4,0},{5,1},{6,2},{7,3},{8,12},{9,13},{10,... | collective-permute-start | bytes 3145736 | tf_op jit(solution)/shard_map/ppermute | solution.py:195
  9.9 11.2 %collective-permute-done.6.refs_0_ = f32[128,1024]{1,0:T(8,128)} collective-permute-done((f32[128,1024]{1,0:T(8,128)}, f32[128,1024]{1,0:T(8,128)}, u32[]{:S(2)}, u32[]{:S(2)}) %collective-permute-start.6) | collective-permute-done | bytes 524320 | tf_op jit(solution)/shard_map/ppermute | solution.py:195
  21.1 11.2 %collective-permute-done.13.refs_1_ = f32[128,1024]{1,0:T(8,128)} collective-permute-done((f32[128,1024]{1,0:T(8,128)}, f32[128,1024]{1,0:T(8,128)}, u32[]{:S(2)}, u32[]{:S(2)}) %collective-permute-start.13) | collective-permute-done | bytes 524320 | tf_op jit(solution)/shard_map/ppermute | solution.py:195
  32.4 1.8 %collective-permute-start.1 = (f32[8,1024]{1,0:T(8,128)S(1)}, f32[8,1024]{1,0:T(8,128)S(1)}, u32[]{:S(2)}, u32[]{:S(2)}) collective-permute-start(f32[8,1024]{1,0:T(8,128)S(1)} %maximum_maximum_fusion), channel_id=1, source_target_pairs={{0,4},{1,5},{2,6},{3,7},{4,0},{5,1},{6,2},{7,3},{8,12},{9,13},{10,... | collective-permute-start | bytes 98312 | tf_op jit(solution)/shard_map/ppermute | solution.py:195
  34.2 2.2 %collective-permute-done.1 = f32[8,1024]{1,0:T(8,128)S(1)} collective-permute-done((f32[8,1024]{1,0:T(8,128)S(1)}, f32[8,1024]{1,0:T(8,128)S(1)}, u32[]{:S(2)}, u32[]{:S(2)}) %collective-permute-start.1) | collective-permute-done | bytes 32800 | tf_op jit(solution)/shard_map/ppermute | solution.py:195
  37.3 6.3 %collective-permute-done.7.refs_2_ = f32[128,1024]{1,0:T(8,128)} collective-permute-done((f32[128,1024]{1,0:T(8,128)}, f32[128,1024]{1,0:T(8,128)}, u32[]{:S(2)}, u32[]{:S(2)}) %collective-permute-start.7) | collective-permute-done | bytes 524320 | tf_op jit(solution)/shard_map/ppermute | solution.py:195
  43.6 10.9 %collective-permute-done.14.refs_3_ = f32[128,1024]{1,0:T(8,128)} collective-permute-done((f32[128,1024]{1,0:T(8,128)}, f32[128,1024]{1,0:T(8,128)}, u32[]{:S(2)}, u32[]{:S(2)}) %collective-permute-start.14) | collective-permute-done | bytes 524320 | tf_op jit(solution)/shard_map/ppermute | solution.py:195
  54.8 1.7 %collective-permute-start.3 = (f32[8,1024]{1,0:T(8,128)S(1)}, f32[8,1024]{1,0:T(8,128)S(1)}, u32[]{:S(2)}, u32[]{:S(2)}) collective-permute-start(f32[8,1024]{1,0:T(8,128)S(1)} %maximum_maximum_fusion.1), channel_id=1, source_target_pairs={{0,16},{1,17},{2,18},{3,19},{4,20},{5,21},{6,22},{7,23},{8,24},{9,... | collective-permute-start | bytes 98312 | tf_op jit(solution)/shard_map/ppermute | solution.py:195
  56.5 3.5 %collective-permute-done.3 = f32[8,1024]{1,0:T(8,128)S(1)} collective-permute-done((f32[8,1024]{1,0:T(8,128)S(1)}, f32[8,1024]{1,0:T(8,128)S(1)}, u32[]{:S(2)}, u32[]{:S(2)}) %collective-permute-start.3) | collective-permute-done | bytes 32800 | tf_op jit(solution)/shard_map/ppermute | solution.py:195
  59.9 2.6 %collective-permute-start.4 = (f32[8,1024]{1,0:T(8,128)S(1)}, f32[8,1024]{1,0:T(8,128)S(1)}, u32[]{:S(2)}, u32[]{:S(2)}) collective-permute-start(f32[8,1024]{1,0:T(8,128)S(1)} %maximum_maximum_fusion.1), channel_id=1, source_target_pairs={{0,24},{1,25},{2,26},{3,27},{4,28},{5,29},{6,30},{7,31},{8,0},{9,1... | collective-permute-start | bytes 98312 | tf_op jit(solution)/shard_map/ppermute | solution.py:195
  62.5 1.6 %collective-permute-done.4 = f32[8,1024]{1,0:T(8,128)S(1)} collective-permute-done((f32[8,1024]{1,0:T(8,128)S(1)}, f32[8,1024]{1,0:T(8,128)S(1)}, u32[]{:S(2)}, u32[]{:S(2)}) %collective-permute-start.4) | collective-permute-done | bytes 32800 | tf_op jit(solution)/shard_map/ppermute | solution.py:195
  64.3 8.1 %products_two.1 = (f32[256,512]{1,0:T(8,128)S(1)}, f32[256,512]{1,0:T(8,128)S(1)}, f32[512,512]{1,0:T(8,128)}) custom-call(s32[1]{0:T(128)} %bitcast.13.flag_ref, f32[8,1024]{1,0:T(8,128)S(1)} %maximum_maximum_fusion.2.mean_ref, f32[256,1024]{1,0:T(8,128)S(1)} %copy-done, f32[256,1024]{1,0:T(8,128)S(1)} %collective-permute-done.5.side_ref, ...), custom_call_target="tpu_custom_call" | custom-call | flops 3221225472 | bytes 12582912 | tf_op jit(solution)/shard_map/products_two/pallas_call | solution.py:110
  74.0 1.5 %collective-permute-start.27 = (f32[512,512]{1,0:T(8,128)}, f32[512,512]{1,0:T(8,128)S(1)}, u32[]{:S(2)}, u32[]{:S(2)}) collective-permute-start(f32[512,512]{1,0:T(8,128)} %get-tuple-element.28), channel_id=1, source_target_pairs={{0,1},{1,0},{2,3},{3,2},{4,5},{5,4},{6,7},{7,6},{8,9},{9,8},{10,11... | collective-permute-start | bytes 3145736 | tf_op jit(solution)/shard_map/ppermute | solution.py:195
  76.0 1.7 %collective-permute-start.8 = (f32[128,1024]{1,0:T(8,128)}, f32[128,1024]{1,0:T(8,128)}, u32[]{:S(2)}, u32[]{:S(2)}) collective-permute-start(f32[128,1024]{1,0:T(8,128)} %collective-permute-done.7.refs_2_), channel_id=1, source_target_pairs={{0,8},{1,9},{2,26},{3,27},{4,12},{5,13},{6,30},{7,31},{8,16},{9,17... | collective-permute-start | bytes 1572872 | tf_op jit(solution)/shard_map/ppermute | solution.py:195
  78.4 5.7 %products_one.1 = (f32[256,256]{1,0:T(8,128)S(1)}, f32[256,256]{1,0:T(8,128)S(1)}, f32[512,256]{1,0:T(8,128)S(1)}) custom-call(s32[1]{0:T(128)} %bitcast.12.flag_ref, f32[8,1024]{1,0:T(8,128)S(1)} %maximum_maximum_fusion.2.mean_ref, f32[256,1024]{1,0:T(8,128)S(1)} %copy-done, f32[256,1024]{1,0:T(8,128)S(1)} %collective-permute-done.5.side_ref, ...), custom_call_target="tpu_custom_call" | custom-call | flops 1610612736 | bytes 8388608 | tf_op jit(solution)/shard_map/products_one/pallas_call | solution.py:110
  84.7 8.4 %collective-permute-done.15.refs_0_ = f32[128,1024]{1,0:T(8,128)} collective-permute-done((f32[128,1024]{1,0:T(8,128)}, f32[128,1024]{1,0:T(8,128)}, u32[]{:S(2)}, u32[]{:S(2)}) %collective-permute-start.15) | collective-permute-done | bytes 524320 | tf_op jit(solution)/shard_map/ppermute | solution.py:195
  93.2 10.6 %collective-permute-done.8.refs_0_ = f32[128,1024]{1,0:T(8,128)} collective-permute-done((f32[128,1024]{1,0:T(8,128)}, f32[128,1024]{1,0:T(8,128)}, u32[]{:S(2)}, u32[]{:S(2)}) %collective-permute-start.8) | collective-permute-done | bytes 524320 | tf_op jit(solution)/shard_map/ppermute | solution.py:195
  104.7 1.5 %collective-permute-start.28 = (f32[256,512]{1,0:T(8,128)}, f32[256,512]{1,0:T(8,128)}, u32[]{:S(2)}, u32[]{:S(2)}) collective-permute-start(f32[256,512]{1,0:T(8,128)} %slice_add_fusion), channel_id=1, source_target_pairs={{0,4},{1,5},{2,6},{3,7},{4,0},{5,1},{6,2},{7,3},{8,12},{9,13},{10,... | collective-permute-start | bytes 1572872 | tf_op jit(solution)/shard_map/ppermute | solution.py:195
  106.2 2.8 %collective-permute-done.22.refs_1_ = f32[512,256]{1,0:T(8,128)S(1)} collective-permute-done((f32[512,256]{1,0:T(8,128)S(1)}, f32[512,256]{1,0:T(8,128)S(1)}, u32[]{:S(2)}, u32[]{:S(2)}) %collective-permute-start.22) | collective-permute-done | bytes 524320 | tf_op jit(solution)/shard_map/ppermute | solution.py:195
  110.5 1.5 %collective-permute-start.23 = (f32[256,256]{1,0:T(8,128)}, f32[256,256]{1,0:T(8,128)}, u32[]{:S(2)}, u32[]{:S(2)}) collective-permute-start(f32[256,256]{1,0:T(8,128)} %slice_add_fusion.1), channel_id=1, source_target_pairs={{0,4},{1,5},{2,6},{3,7},{4,0},{5,1},{6,2},{7,3},{8,12},{9,13},{10,... | collective-permute-start | bytes 786440 | tf_op jit(solution)/shard_map/ppermute | solution.py:195
  112.0 4.1 %products_three.3 = (f32[256,128]{1,0:T(8,128)S(1)}, f32[256,128]{1,0:T(8,128)S(1)}, f32[256,128]{1,0:T(8,128)}, f32[256,128]{1,0:T(8,128)S(1)}) custom-call(s32[1]{0:T(128)} %bitcast.4.flag_ref, f32[8,1024]{1,0:T(8,128)S(1)} %maximum_maximum_fusion.2.mean_ref, f32[256,1024]{1,0:T(8,128)S(1)} %copy-done, f32[256,1024]{1,0:T(8,128)S(1)} %collective-permute-done.5.side_ref, ...), custom_call_target="tpu_custom_call" | custom-call | flops 805306368 | bytes 6291456 | tf_op jit(solution)/shard_map/products_three/pallas_call | solution.py:110
  118.1 1.5 %collective-permute-start.17 = (f32[256,128]{1,0:T(8,128)}, f32[256,128]{1,0:T(8,128)}, u32[]{:S(2)}, u32[]{:S(2)}) collective-permute-start(f32[256,128]{1,0:T(8,128)} %get-tuple-element.21), channel_id=1, source_target_pairs={{0,1},{1,0},{2,3},{3,2},{4,5},{5,4},{6,7},{7,6},{8,9},{9,8},{10,11... | collective-permute-start | bytes 393224 | tf_op jit(solution)/shard_map/ppermute | solution.py:195
  120.1 1.5 %collective-permute-start.19 = (f32[256,128]{1,0:T(8,128)}, f32[256,128]{1,0:T(8,128)}, u32[]{:S(2)}, u32[]{:S(2)}) collective-permute-start(f32[256,128]{1,0:T(8,128)} %copy-done.11), channel_id=1, source_target_pairs={{0,5},{1,4},{2,7},{3,6},{4,1},{5,0},{6,3},{7,2},{8,13},{9,12},{10,... | collective-permute-start | bytes 393224 | tf_op jit(solution)/shard_map/ppermute | solution.py:195
  121.6 4.2 %products_three.2 = (f32[256,128]{1,0:T(8,128)S(1)}, f32[256,128]{1,0:T(8,128)}, f32[256,128]{1,0:T(8,128)}, f32[256,128]{1,0:T(8,128)}) custom-call(s32[1]{0:T(128)} %bitcast.4.flag_ref, f32[8,1024]{1,0:T(8,128)S(1)} %maximum_maximum_fusion.2.mean_ref, f32[256,1024]{1,0:T(8,128)S(1)} %copy-done, f32[256,1024]{1,0:T(8,128)S(1)} %collective-permute-done.5.side_ref, ...), custom_call_target="tpu_custom_call" | custom-call | flops 805306368 | bytes 6291456 | tf_op jit(solution)/shard_map/products_three/pallas_call | solution.py:110
  126.5 1.5 %collective-permute-start.10 = (f32[256,128]{1,0:T(8,128)}, f32[256,128]{1,0:T(8,128)S(1)}, u32[]{:S(2)}, u32[]{:S(2)}) collective-permute-start(f32[256,128]{1,0:T(8,128)} %get-tuple-element.17), channel_id=1, source_target_pairs={{0,1},{1,0},{2,3},{3,2},{4,5},{5,4},{6,7},{7,6},{8,9},{9,8},{10,11... | collective-permute-start | bytes 393224 | tf_op jit(solution)/shard_map/ppermute | solution.py:195
  128.5 1.5 %collective-permute-start.12 = (f32[256,128]{1,0:T(8,128)}, f32[256,128]{1,0:T(8,128)S(1)}, u32[]{:S(2)}, u32[]{:S(2)}) collective-permute-start(f32[256,128]{1,0:T(8,128)} %get-tuple-element.19), channel_id=1, source_target_pairs={{0,5},{1,4},{2,7},{3,6},{4,1},{5,0},{6,3},{7,2},{8,13},{9,12},{10,... | collective-permute-start | bytes 393224 | tf_op jit(solution)/shard_map/ppermute | solution.py:195
  131.8 1.0 copy-done.6
  132.9 2.4 %place_most.1.refs_8_ = f32[256,2048]{1,0:T(8,128)} custom-call(s32[6]{0:T(128)S(1)} %stack.47.at_ref, f32[256,256]{1,0:T(8,128)S(1)} %get-tuple-element.24.refs_0_, f32[512,256]{1,0:T(8,128)S(1)} %copy-done.2, f32[256,256]{1,0:T(8,128)} %collective-permute-done.23.refs_2_, f32[256,512]{1,0:T(8,128)S(1)} %copy-done.6, ...), custom_call_target="tpu_custom_call" | custom-call | tf_op jit(solution)/shard_map/place_most/pallas_call | solution.py:150
  136.0 1.9 %place_last.1 = f32[256,2048]{1,0:T(8,128)} custom-call(s32[4]{0:T(128)S(1)} %pad_add_fusion.at_ref, f32[256,128]{1,0:T(8,128)S(1)} %copy-done.10, f32[256,128]{1,0:T(8,128)S(1)} %collective-permute-done.10.refs_1_, f32[256,128]{1,0:T(8,128)S(1)} %collective-permute-done.11.refs_2_, ...), custom_call_target="tpu_custom_call", output_to_operand_aliasing={{}: (9, {})} | custom-call | tf_op jit(solution)/shard_map/place_last/pallas_call | solution.py:150
  (76 shorter events, 14.3 us)
Async XLA Ops:
  0.6 7.1 %copy-start = (f32[256,1024]{1,0:T(8,128)S(1)}, f32[256,1024]{1,0:T(8,128)}, u32[]{:S(2)}) copy-start(f32[256,1024]{1,0:T(8,128)} %refs_0_.1) | copy-start | bytes 3145732
  0.6 7.0 %copy-start.13 = (f32[256]{0:T(256)S(1)}, f32[256]{0:T(256)}, u32[]{:S(2)}) copy-start(f32[256]{0:T(256)} %param.3) | copy-start | bytes 3076
  3.0 18.1 %collective-permute-start.6 = (f32[128,1024]{1,0:T(8,128)}, f32[128,1024]{1,0:T(8,128)}, u32[]{:S(2)}, u32[]{:S(2)}) collective-permute-start(f32[128,1024]{1,0:T(8,128)} %get-tuple-element.37), channel_id=1, source_target_pairs={{0,8},{1,9},{2,26},{3,27},{4,12},{5,13},{6,30},{7,31},{8,16},{9,17... | collective-permute-start | bytes 1572872 | tf_op jit(solution)/shard_map/ppermute | solution.py:195
  6.1 26.3 %collective-permute-start.13 = (f32[128,1024]{1,0:T(8,128)}, f32[128,1024]{1,0:T(8,128)}, u32[]{:S(2)}, u32[]{:S(2)}) collective-permute-start(f32[128,1024]{1,0:T(8,128)} %get-tuple-element.36), channel_id=1, source_target_pairs={{0,8},{1,9},{2,26},{3,27},{4,12},{5,13},{6,30},{7,31},{8,16},{9,17... | collective-permute-start | bytes 1572872 | tf_op jit(solution)/shard_map/ppermute | solution.py:195
  8.0 1.9 %collective-permute-start = (f32[8,1024]{1,0:T(8,128)S(1)}, f32[8,1024]{1,0:T(8,128)S(1)}, u32[]{:S(2)}, u32[]{:S(2)}) collective-permute-start(f32[8,1024]{1,0:T(8,128)S(1)} %block_stats.1), channel_id=1, source_target_pairs={{0,2},{1,3},{2,0},{3,1},{4,6},{5,7},{6,4},{7,5},{8,10},{9,11},{10,... | collective-permute-start | bytes 98312 | tf_op jit(solution)/shard_map/ppermute | solution.py:195
  8.2 56.0 %collective-permute-start.5 = (f32[256,1024]{1,0:T(8,128)S(1)}, f32[256,1024]{1,0:T(8,128)S(1)}, u32[]{:S(2)}, u32[]{:S(2)}) collective-permute-start(f32[256,1024]{1,0:T(8,128)S(1)} %copy-done), channel_id=1, source_target_pairs={{0,4},{1,5},{2,6},{3,7},{4,0},{5,1},{6,2},{7,3},{8,12},{9,13},{10,... | collective-permute-start | bytes 3145736 | tf_op jit(solution)/shard_map/ppermute | solution.py:195
  9.7 54.5 %collective-permute-start.24 = (f32[256,1024]{1,0:T(8,128)S(1)}, f32[256,1024]{1,0:T(8,128)S(1)}, u32[]{:S(2)}, u32[]{:S(2)}) collective-permute-start(f32[256,1024]{1,0:T(8,128)S(1)} %copy-done), channel_id=1, source_target_pairs={{0,2},{1,3},{2,0},{3,1},{4,6},{5,7},{6,4},{7,5},{8,10},{9,11},{10,... | collective-permute-start | bytes 3145736 | tf_op jit(solution)/shard_map/ppermute | solution.py:195
  21.1 22.5 %collective-permute-start.7 = (f32[128,1024]{1,0:T(8,128)}, f32[128,1024]{1,0:T(8,128)}, u32[]{:S(2)}, u32[]{:S(2)}) collective-permute-start(f32[128,1024]{1,0:T(8,128)} %collective-permute-done.6.refs_0_), channel_id=1, source_target_pairs={{0,8},{1,9},{2,26},{3,27},{4,12},{5,13},{6,30},{7,31},{8,16},{9,17... | collective-permute-start | bytes 1572872 | tf_op jit(solution)/shard_map/ppermute | solution.py:195
  32.4 22.2 %collective-permute-start.14 = (f32[128,1024]{1,0:T(8,128)}, f32[128,1024]{1,0:T(8,128)}, u32[]{:S(2)}, u32[]{:S(2)}) collective-permute-start(f32[128,1024]{1,0:T(8,128)} %collective-permute-done.13.refs_1_), channel_id=1, source_target_pairs={{0,8},{1,9},{2,26},{3,27},{4,12},{5,13},{6,30},{7,31},{8,16},{9,17... | collective-permute-start | bytes 1572872 | tf_op jit(solution)/shard_map/ppermute | solution.py:195
  32.4 3.9 %collective-permute-start.1 = (f32[8,1024]{1,0:T(8,128)S(1)}, f32[8,1024]{1,0:T(8,128)S(1)}, u32[]{:S(2)}, u32[]{:S(2)}) collective-permute-start(f32[8,1024]{1,0:T(8,128)S(1)} %maximum_maximum_fusion), channel_id=1, source_target_pairs={{0,4},{1,5},{2,6},{3,7},{4,0},{5,1},{6,2},{7,3},{8,12},{9,13},{10,... | collective-permute-start | bytes 98312 | tf_op jit(solution)/shard_map/ppermute | solution.py:195
  36.5 18.3 %collective-permute-start.2 = (f32[8,1024]{1,0:T(8,128)S(1)}, f32[8,1024]{1,0:T(8,128)S(1)}, u32[]{:S(2)}, u32[]{:S(2)}) collective-permute-start(f32[8,1024]{1,0:T(8,128)S(1)} %maximum_maximum_fusion.1), channel_id=1, source_target_pairs={{0,8},{1,9},{2,10},{3,11},{4,12},{5,13},{6,14},{7,15},{8,16},{9,17... | collective-permute-start | bytes 98312 | tf_op jit(solution)/shard_map/ppermute | solution.py:195
  43.6 20.7 %collective-permute-start.25 = (f32[128,1024]{1,0:T(8,128)}, f32[128,1024]{1,0:T(8,128)}, u32[]{:S(2)}, u32[]{:S(2)}) collective-permute-start(f32[128,1024]{1,0:T(8,128)} %collective-permute-done.7.refs_2_), channel_id=1, source_target_pairs={{0,2},{1,3},{2,0},{3,1},{4,6},{5,7},{6,4},{7,5},{8,10},{9,11},{10,... | collective-permute-start | bytes 1572872 | tf_op jit(solution)/shard_map/ppermute | solution.py:195
  54.5 9.7 %collective-permute-start.26 = (f32[128,1024]{1,0:T(8,128)}, f32[128,1024]{1,0:T(8,128)}, u32[]{:S(2)}, u32[]{:S(2)}) collective-permute-start(f32[128,1024]{1,0:T(8,128)} %collective-permute-done.14.refs_3_), channel_id=1, source_target_pairs={{0,2},{1,3},{2,0},{3,1},{4,6},{5,7},{6,4},{7,5},{8,10},{9,11},{10,... | collective-permute-start | bytes 1572872 | tf_op jit(solution)/shard_map/ppermute | solution.py:195
  54.8 5.2 %collective-permute-start.3 = (f32[8,1024]{1,0:T(8,128)S(1)}, f32[8,1024]{1,0:T(8,128)S(1)}, u32[]{:S(2)}, u32[]{:S(2)}) collective-permute-start(f32[8,1024]{1,0:T(8,128)S(1)} %maximum_maximum_fusion.1), channel_id=1, source_target_pairs={{0,16},{1,17},{2,18},{3,19},{4,20},{5,21},{6,22},{7,23},{8,24},{9,... | collective-permute-start | bytes 98312 | tf_op jit(solution)/shard_map/ppermute | solution.py:195
  59.9 4.2 %collective-permute-start.4 = (f32[8,1024]{1,0:T(8,128)S(1)}, f32[8,1024]{1,0:T(8,128)S(1)}, u32[]{:S(2)}, u32[]{:S(2)}) collective-permute-start(f32[8,1024]{1,0:T(8,128)S(1)} %maximum_maximum_fusion.1), channel_id=1, source_target_pairs={{0,24},{1,25},{2,26},{3,27},{4,28},{5,29},{6,30},{7,31},{8,0},{9,1... | collective-permute-start | bytes 98312 | tf_op jit(solution)/shard_map/ppermute | solution.py:195
  74.0 29.8 %collective-permute-start.27 = (f32[512,512]{1,0:T(8,128)}, f32[512,512]{1,0:T(8,128)S(1)}, u32[]{:S(2)}, u32[]{:S(2)}) collective-permute-start(f32[512,512]{1,0:T(8,128)} %get-tuple-element.28), channel_id=1, source_target_pairs={{0,1},{1,0},{2,3},{3,2},{4,5},{5,4},{6,7},{7,6},{8,9},{9,8},{10,11... | collective-permute-start | bytes 3145736 | tf_op jit(solution)/shard_map/ppermute | solution.py:195
  75.4 2.3 %collective-permute-start.20 = (f32[128,1024]{1,0:T(8,128)}, f32[128,1024]{1,0:T(8,128)}, u32[]{:S(2)}, u32[]{:S(2)}) collective-permute-start(f32[128,1024]{1,0:T(8,128)} %collective-permute-done.6.refs_0_), channel_id=1, source_target_pairs={{0,2},{1,3},{2,0},{3,1},{4,6},{5,7},{6,4},{7,5},{8,10},{9,11},{10,... | collective-permute-start | bytes 1572872 | tf_op jit(solution)/shard_map/ppermute | solution.py:195
  75.4 3.0 %collective-permute-start.21 = (f32[128,1024]{1,0:T(8,128)}, f32[128,1024]{1,0:T(8,128)}, u32[]{:S(2)}, u32[]{:S(2)}) collective-permute-start(f32[128,1024]{1,0:T(8,128)} %collective-permute-done.13.refs_1_), channel_id=1, source_target_pairs={{0,2},{1,3},{2,0},{3,1},{4,6},{5,7},{6,4},{7,5},{8,10},{9,11},{10,... | collective-permute-start | bytes 1572872 | tf_op jit(solution)/shard_map/ppermute | solution.py:195
  76.0 17.2 %collective-permute-start.15 = (f32[128,1024]{1,0:T(8,128)}, f32[128,1024]{1,0:T(8,128)}, u32[]{:S(2)}, u32[]{:S(2)}) collective-permute-start(f32[128,1024]{1,0:T(8,128)} %collective-permute-done.14.refs_3_), channel_id=1, source_target_pairs={{0,8},{1,9},{2,26},{3,27},{4,12},{5,13},{6,30},{7,31},{8,16},{9,17... | collective-permute-start | bytes 1572872 | tf_op jit(solution)/shard_map/ppermute | solution.py:195
  76.0 27.8 %collective-permute-start.8 = (f32[128,1024]{1,0:T(8,128)}, f32[128,1024]{1,0:T(8,128)}, u32[]{:S(2)}, u32[]{:S(2)}) collective-permute-start(f32[128,1024]{1,0:T(8,128)} %collective-permute-done.7.refs_2_), channel_id=1, source_target_pairs={{0,8},{1,9},{2,26},{3,27},{4,12},{5,13},{6,30},{7,31},{8,16},{9,17... | collective-permute-start | bytes 1572872 | tf_op jit(solution)/shard_map/ppermute | solution.py:195
  78.4 25.3 %copy-start.4 = (f32[256,512]{1,0:T(8,128)S(1)}, f32[256,512]{1,0:T(8,128)}, u32[]{:S(2)}) copy-start(f32[256,512]{1,0:T(8,128)} %copy-done.3) | copy-start | bytes 1572868
  84.1 24.9 %collective-permute-start.22 = (f32[512,256]{1,0:T(8,128)S(1)}, f32[512,256]{1,0:T(8,128)S(1)}, u32[]{:S(2)}, u32[]{:S(2)}) collective-permute-start(f32[512,256]{1,0:T(8,128)S(1)} %get-tuple-element.25), channel_id=1, source_target_pairs={{0,1},{1,0},{2,3},{3,2},{4,5},{5,4},{6,7},{7,6},{8,9},{9,8},{10,11... | collective-permute-start | bytes 1572872 | tf_op jit(solution)/shard_map/ppermute | solution.py:195
  93.2 18.9 %collective-permute-start.16 = (f32[128,1024]{1,0:T(8,128)}, f32[128,1024]{1,0:T(8,128)}, u32[]{:S(2)}, u32[]{:S(2)}) collective-permute-start(f32[128,1024]{1,0:T(8,128)} %collective-permute-done.15.refs_0_), channel_id=1, source_target_pairs={{0,2},{1,3},{2,0},{3,1},{4,6},{5,7},{6,4},{7,5},{8,10},{9,11},{10,... | collective-permute-start | bytes 1572872 | tf_op jit(solution)/shard_map/ppermute | solution.py:195
  103.8 16.4 %collective-permute-start.9 = (f32[128,1024]{1,0:T(8,128)}, f32[128,1024]{1,0:T(8,128)}, u32[]{:S(2)}, u32[]{:S(2)}) collective-permute-start(f32[128,1024]{1,0:T(8,128)} %collective-permute-done.8.refs_0_), channel_id=1, source_target_pairs={{0,2},{1,3},{2,0},{3,1},{4,6},{5,7},{6,4},{7,5},{8,10},{9,11},{10,... | collective-permute-start | bytes 1572872 | tf_op jit(solution)/shard_map/ppermute | solution.py:195
  104.7 23.9 %collective-permute-start.28 = (f32[256,512]{1,0:T(8,128)}, f32[256,512]{1,0:T(8,128)}, u32[]{:S(2)}, u32[]{:S(2)}) collective-permute-start(f32[256,512]{1,0:T(8,128)} %slice_add_fusion), channel_id=1, source_target_pairs={{0,4},{1,5},{2,6},{3,7},{4,0},{5,1},{6,2},{7,3},{8,12},{9,13},{10,... | collective-permute-start | bytes 1572872 | tf_op jit(solution)/shard_map/ppermute | solution.py:195
  110.5 16.0 %collective-permute-start.23 = (f32[256,256]{1,0:T(8,128)}, f32[256,256]{1,0:T(8,128)}, u32[]{:S(2)}, u32[]{:S(2)}) collective-permute-start(f32[256,256]{1,0:T(8,128)} %slice_add_fusion.1), channel_id=1, source_target_pairs={{0,4},{1,5},{2,6},{3,7},{4,0},{5,1},{6,2},{7,3},{8,12},{9,13},{10,... | collective-permute-start | bytes 786440 | tf_op jit(solution)/shard_map/ppermute | solution.py:195
  118.1 9.9 %collective-permute-start.17 = (f32[256,128]{1,0:T(8,128)}, f32[256,128]{1,0:T(8,128)}, u32[]{:S(2)}, u32[]{:S(2)}) collective-permute-start(f32[256,128]{1,0:T(8,128)} %get-tuple-element.21), channel_id=1, source_target_pairs={{0,1},{1,0},{2,3},{3,2},{4,5},{5,4},{6,7},{7,6},{8,9},{9,8},{10,11... | collective-permute-start | bytes 393224 | tf_op jit(solution)/shard_map/ppermute | solution.py:195
  119.6 15.7 %collective-permute-start.18 = (f32[256,128]{1,0:T(8,128)}, f32[256,128]{1,0:T(8,128)}, u32[]{:S(2)}, u32[]{:S(2)}) collective-permute-start(f32[256,128]{1,0:T(8,128)} %copy-done.12), channel_id=1, source_target_pairs={{0,4},{1,5},{2,6},{3,7},{4,0},{5,1},{6,2},{7,3},{8,12},{9,13},{10,... | collective-permute-start | bytes 393224 | tf_op jit(solution)/shard_map/ppermute | solution.py:195
  120.1 15.1 %collective-permute-start.19 = (f32[256,128]{1,0:T(8,128)}, f32[256,128]{1,0:T(8,128)}, u32[]{:S(2)}, u32[]{:S(2)}) collective-permute-start(f32[256,128]{1,0:T(8,128)} %copy-done.11), channel_id=1, source_target_pairs={{0,5},{1,4},{2,7},{3,6},{4,1},{5,0},{6,3},{7,2},{8,13},{9,12},{10,... | collective-permute-start | bytes 393224 | tf_op jit(solution)/shard_map/ppermute | solution.py:195
  126.5 8.8 %collective-permute-start.10 = (f32[256,128]{1,0:T(8,128)}, f32[256,128]{1,0:T(8,128)S(1)}, u32[]{:S(2)}, u32[]{:S(2)}) collective-permute-start(f32[256,128]{1,0:T(8,128)} %get-tuple-element.17), channel_id=1, source_target_pairs={{0,1},{1,0},{2,3},{3,2},{4,5},{5,4},{6,7},{7,6},{8,9},{9,8},{10,11... | collective-permute-start | bytes 393224 | tf_op jit(solution)/shard_map/ppermute | solution.py:195
  128.0 7.3 %collective-permute-start.11 = (f32[256,128]{1,0:T(8,128)}, f32[256,128]{1,0:T(8,128)S(1)}, u32[]{:S(2)}, u32[]{:S(2)}) collective-permute-start(f32[256,128]{1,0:T(8,128)} %get-tuple-element.18), channel_id=1, source_target_pairs={{0,4},{1,5},{2,6},{3,7},{4,0},{5,1},{6,2},{7,3},{8,12},{9,13},{10,... | collective-permute-start | bytes 393224 | tf_op jit(solution)/shard_map/ppermute | solution.py:195
  128.5 7.4 %collective-permute-start.12 = (f32[256,128]{1,0:T(8,128)}, f32[256,128]{1,0:T(8,128)S(1)}, u32[]{:S(2)}, u32[]{:S(2)}) collective-permute-start(f32[256,128]{1,0:T(8,128)} %get-tuple-element.19), channel_id=1, source_target_pairs={{0,5},{1,4},{2,7},{3,6},{4,1},{5,0},{6,3},{7,2},{8,13},{9,12},{10,... | collective-permute-start | bytes 393224 | tf_op jit(solution)/shard_map/ppermute | solution.py:195
  (11 other events, 13.3 us)

commit v2 on v0

--- a/solution.py
+++ b/solution.py
@@ -1,7 +1,16 @@
+import functools
+
 import jax
 import jax.numpy as jnp
+import numpy as np
 from jax import lax
+from jax.experimental import pallas as pl
+from jax.experimental.pallas import tpu as pltpu
 from jax.sharding import PartitionSpec as P
+
+BOTH = ("smp", "par")
+VMEM_LIMIT = 24 * 1024 * 1024
+FREE = pl.CostEstimate(flops=0, bytes_accessed=0, transcendentals=0)
 
 
 def row_products(left_rows, right_rows):
@@ -14,7 +23,7 @@
     )
 
 
-def local(log_derivs, coefficients):
+def gathered(log_derivs, coefficients):
     samples = log_derivs.shape[0] * lax.axis_size("smp")
     column_total = lax.psum(jnp.sum(log_derivs, axis=0), "smp")
     centred = (log_derivs - column_total[None, :] / samples) / jnp.sqrt(jnp.float32(samples))
@@ -31,10 +40,283 @@
     return (gram, update)
 
 
+def after(value, *others):
+    return lax.optimization_barrier((value, *others))[0]
+
+
+def stats_kernel(rows_ref, coef_ref, stats_ref):
+    rows = rows_ref[...]
+    mean = jnp.sum(rows, axis=0, keepdims=True) / rows.shape[0]
+    stats_ref[0:1, :] = mean
+    stats_ref[1:2, :] = jnp.dot(
+        coef_ref[...], rows - mean, precision=lax.Precision.HIGHEST, preferred_element_type=jnp.float32
+    )
+    stats_ref[2:3, :] = jnp.broadcast_to(jnp.sum(coef_ref[...], axis=1, keepdims=True), mean.shape)
+    stats_ref[3:, :] = jnp.zeros((stats_ref.shape[0] - 3, mean.shape[1]), jnp.float32)
+
+
+def block_stats(rows, coefficients):
+    return pl.pallas_call(
+        stats_kernel,
+        out_shape=jax.ShapeDtypeStruct((8, rows.shape[1]), jnp.float32),
+        compiler_params=pltpu.CompilerParams(vmem_limit_bytes=VMEM_LIMIT),
+        cost_estimate=FREE,
+        name="block_stats",
+    )(rows, coefficients[None, :])
+
+
+def merge_kernel(count, *refs):
+    parts, out = refs[:count], refs[count]
+    mean = sum(p[0:1, :] for p in parts) / count
+    out[...] = jnp.zeros_like(out)
+    out[0:1, :] = mean
+    out[1:2, :] = sum(p[1:2, :] + p[2:3, :] * (p[0:1, :] - mean) for p in parts)
+    out[2:3, :] = sum(p[2:3, :] for p in parts)
+
+
+def merge(*parts):
+    return kernel_call(functools.partial(merge_kernel, len(parts)), [parts[0].shape], "merge", *parts)[0]
+
+
+def split(values):
+    high = values.astype(jnp.bfloat16)
+    return high, (values - high.astype(jnp.float32)).astype(jnp.bfloat16)
+
+
+def dot_nt(left, right):
+    return lax.dot_general(left, right, (((1,), (1,)), ((), ())), preferred_element_type=jnp.float32)
+
+
+def device_row(planes):
+    return lax.axis_index("smp") * planes + lax.axis_index("par")
+
+
+def product_of(row_ref, mean, high, low, scale):
+    row_high, row_low = split(row_ref[...] - mean)
+    return (dot_nt(row_high, high) + (dot_nt(row_high, low) + dot_nt(row_low, high))) * scale
+
+
+def one_level_kernel(scale, mean_ref, *refs):
+    rows, block, outs = refs[:4], refs[4], refs[5:]
+    mean = mean_ref[0:1, :]
+    high, low = split(block[...] - mean)
+    straight = lax.axis_index("par") == 0
+    for side in range(2):
+        same = product_of(rows[2 * side], mean, high, low, scale)
+        other = product_of(rows[2 * side + 1], mean, high, low, scale)
+        outs[2 * side][...] = jnp.where(straight, same, other)
+        outs[2 * side + 1][...] = jnp.where(straight, other, same)
+
+
+def two_levels_kernel(scale, planes, flag_at, table_ref, mean_ref, *refs):
+    rows, blocks, outs = refs[:4], refs[4:6], refs[6:]
+    mean = mean_ref[0:1, :]
+    first = table_ref[device_row(planes), flag_at] == 1
+    high, low = split(jnp.concatenate([block[...] for block in blocks], axis=0) - mean)
+    height, width = rows[0].shape[0], blocks[0].shape[0]
+    for k, row in enumerate(rows):
+        total = product_of(row, mean, high, low, scale)
+        one, other = total[:, :width], total[:, width:]
+        place = slice(k % 2 * height, (k % 2 + 1) * height)
+        outs[k // 2][place, :] = jnp.where(first, one, other)
+        outs[2 + k // 2][place, :] = jnp.where(first, other, one)
+
+
+def across_kernel(keep_own, got_own, from_side, got_side, own, side):
+    height = own.shape[0]
+    own[...] = keep_own[height:, :] + got_own[height:, :]
+    side[...] = from_side[height:, :] + got_side[height:, :]
+
+
+def kernel_call(kernel, out_shapes, name, *args, smem=0):
+    return pl.pallas_call(
+        kernel,
+        out_shape=[jax.ShapeDtypeStruct(s, jnp.float32) for s in out_shapes],
+        in_specs=[pl.BlockSpec(memory_space=pltpu.SMEM)] * smem
+        + [pl.BlockSpec(memory_space=pltpu.VMEM)] * (len(args) - smem),
+        out_specs=[pl.BlockSpec(memory_space=pltpu.VMEM)] * len(out_shapes),
+        compiler_params=pltpu.CompilerParams(vmem_limit_bytes=VMEM_LIMIT),
+        cost_estimate=FREE,
+        name=name,
+    )(*args)
+
+
+def place_kernel(planes, summands, columns, aliased, table_ref, *refs):
+    blocks = list(refs[: sum(summands)])
+    out = refs[len(blocks) + aliased]
+    *totals, sems = refs[len(blocks) + aliased + 1 :]
+    row = device_row(planes)
+    stores = []
+    for total, terms, places in zip(totals, summands, columns):
+        taken, blocks = blocks[:terms], blocks[terms:]
+        if terms > 1:
+            total[...] = taken[0][0 : total.shape[0], :] + taken[1][0 : total.shape[0], :]
+        else:
+            total = taken[0]
+        width = total.shape[1] // len(places)
+        for part, (where, offset) in enumerate(places):
+            column = pl.multiple_of((table_ref[row, where] + offset) * 128, 128)
+            stores.append(
+                pltpu.make_async_copy(
+                    total.at[:, pl.ds(part * width, width)], out.at[:, pl.ds(column, width)], sems.at[len(stores)]
+                )
+            )
+            stores[-1].start()
+    for store in stores:
+        store.wait()
+
+
+def place(table, planes, pieces, shape, into, name):
+    blocks = [block for terms, _ in pieces for block in terms]
+    columns = [places for _, places in pieces]
+    aliased = 0 if into is None else 1
+    near, far = pl.BlockSpec(memory_space=pltpu.VMEM), pl.BlockSpec(memory_space=pl.ANY)
+    return pl.pallas_call(
+        functools.partial(place_kernel, planes, [len(terms) for terms, _ in pieces], columns, aliased),
+        out_shape=jax.ShapeDtypeStruct(shape, jnp.float32),
+        in_specs=[pl.BlockSpec(memory_space=pltpu.SMEM)] + [near] * len(blocks) + [far] * aliased,
+        out_specs=far,
+        scratch_shapes=[pltpu.VMEM((shape[0], terms[0].shape[1]), jnp.float32) for terms, _ in pieces]
+        + [pltpu.SemaphoreType.DMA((sum(map(len, columns)),))],
+        input_output_aliases={1 + len(blocks): 0} if aliased else {},
+        compiler_params=pltpu.CompilerParams(vmem_limit_bytes=VMEM_LIMIT),
+        cost_estimate=FREE,
+        name=name,
+    )(table, *blocks, *([into] if aliased else []))
+
+
+def column_table(levels, planes, block):
+    per_plane = levels // planes
+    table = np.zeros((levels * 4 * planes, 16), np.int32)
+
+    def column(level, side, core):
+        return ((level % per_plane * 2 + side) * 2 + core) * block
+
+    for z in range(levels):
+        for x in range(2):
+            for c in range(2):
+                for y in range(planes):
+                    row = [int(z // per_plane == y)]
+                    for step in (-1, 1):
+                        for core in range(2):
+                            level = (z + step * (1 - 2 * core)) % levels
+                            if level // per_plane == y:
+                                row += [column(level, x, core), column(level, 1 - x, core)]
+                    level = z if row[0] else (z + levels // 2) % levels
+                    for core in (c, 1 - c):
+                        row += [column(level, x, core), column(level, 1 - x, core)]
+                    table[((z * 2 + x) * 2 + c) * planes + y, : len(row)] = row
+    return table
+
+
+def ringed(log_derivs, coefficients):
+    rows, params = log_derivs.shape
+    samples = rows * lax.axis_size("smp")
+    levels, planes = lax.axis_size("smp") // 4, lax.axis_size("par")
+    per_plane = levels // planes
+    shape = (rows, rows * 4 * per_plane)
+    scale = 1.0 / samples
+
+    def moves(to):
+        pairs = []
+        for z in range(levels):
+            for x in range(2):
+                for c in range(2):
+                    for y in range(planes):
+                        tz, tx, tc, ty = to(z, x, c, y)
+                        target = ((tz % levels) * 2 + tx) * 2 + tc
+                        pairs.append((((z * 2 + x) * 2 + c) * planes + y, target * planes + ty))
+        return pairs
+
+    def holder(z):
+        return z % levels // per_plane
+
+    ring = moves(lambda z, x, c, y: (z + 1 - 2 * c, x, c, y))
+    over_core = moves(lambda z, x, c, y: (z, x, 1 - c, y))
+    over_side = moves(lambda z, x, c, y: (z, 1 - x, c, y))
+    over_both = moves(lambda z, x, c, y: (z, 1 - x, 1 - c, y))
+    over_plane = moves(lambda z, x, c, y: (z, x, c, 1 - y))
+    diagonal = moves(lambda z, x, c, y: (z, 1 - x, c, 1 - y))
+    turns = [moves(lambda z, x, c, y, k=k: (z + k, x, c, y)) for k in range(1, levels)]
+
+    def to_holder(step, side, swap):
+        return moves(lambda z, x, c, y: (z, x ^ side, c ^ y ^ swap, holder(z - step * (1 - 2 * c))))
+
+    def send(value, pairs):
+        return lax.ppermute(value, BOTH, pairs)
+
+    table = jnp.asarray(column_table(levels, planes, rows // 128))
+
+    core_rows = send(log_derivs, over_core)
+    one = send(log_derivs, ring)
+
+    side_rows = send(log_derivs, over_side)
+
+    stats = block_stats(log_derivs, coefficients)
+    stats = merge(stats, *[send(stats, turn) for turn in turns])
+    one, side_rows = lax.optimization_barrier((one, side_rows, stats))[:2]
+    two = send(one, ring)
+    stats = merge(stats, send(stats, over_core), send(stats, over_side), send(stats, over_both))
+    side_core_rows = send(side_rows, over_core)
+    all_rows = (log_derivs, core_rows, side_rows, side_core_rows)
+
+    def one_level(block, step, name):
+        out = kernel_call(functools.partial(one_level_kernel, scale), [(rows, rows)] * 4, name, stats, *all_rows, block)
+        sent = [send(out[2 * side + swap], to_holder(step, side, swap)) for side in range(2) for swap in range(2)]
+        return out, (sent[:2], sent[2:])
+
+    out, near = one_level(one, 1, "products_near")
+    share = params // lax.axis_size("smp")
+
+    two = after(two, *near[0], *near[1])
+    three = send(two, ring)
+    keep_own, keep_side, sent_own, sent_side = kernel_call(
+        functools.partial(two_levels_kernel, scale, planes, 0),
+        [(2 * rows, rows)] * 4,
+        "products_across",
+        table,
+        stats,
+        *all_rows,
+        log_derivs,
+        two,
+        smem=1,
+    )
+    got_own = send(sent_own, over_plane)
+    got_side = send(sent_side, diagonal)
+    from_side = send(keep_side, over_side)
+
+    out, far = one_level(three, -1, "products_far")
+
+    got_own = after(got_own, out[0])
+    own, side = kernel_call(across_kernel, [(rows, rows)] * 2, "sum_across", keep_own, got_own, from_side, got_side)
+    across_own, across_side = send(own, over_core), send(side, over_core)
+    update = lax.dynamic_slice(after(stats, out[0]), (1, lax.axis_index("smp") * share), (1, share))[0]
+    update = update / jnp.sqrt(jnp.float32(samples))
+    gram = place(
+        table,
+        planes,
+        [(near[0], [(1, 0)]), (near[1], [(2, 0)]), ((keep_own, got_own), [(5, 0)]), ((from_side, got_side), [(6, 0)])],
+        shape,
+        None,
+        "place_most",
+    )
+    gram = after(gram, *far[0], *far[1])
+    gram = place(
+        table,
+        planes,
+        [(far[0], [(3, 0)]), (far[1], [(4, 0)]), ((across_own,), [(7, 0)]), ((across_side,), [(8, 0)])],
+        shape,
+        gram,
+        "place_last",
+    )
+    return (gram, update)
+
+
 def solution(mesh):
     placed = (P("smp", "par"), P("smp"))
+    levels, planes = mesh.shape["smp"] // 4, mesh.shape["par"]
     return jax.shard_map(
-        local,
+        ringed if planes == 2 and levels == 2 * planes else gathered,
         mesh=mesh,
         in_specs=placed,
         out_specs=(P("smp", "par"), P(("par", "smp"))),

time: 248 us -> 113 us (0.46)
  waiting for transfers between devices: 144 us -> 54 us
  blocking collectives: 65.5 us -> 0 us
  starting transfers between devices: 0.08 us -> 36.8 us
  Pallas kernels: 0 us -> 19.3 us
  matrix products: 19 us -> 0 us
  between operations: 14.7 us -> 0.77 us
  other arithmetic: 3.66 us -> 0.59 us
    all_gather x1 -> x0, waiting for transfers between devices: 124 us -> none  [local(): lax.all_gather(centred, 'smp', axis=0, tiled=True)]
    ppermute x0 -> x25, waiting for transfers between devices: none -> 54 us  [send(): return lax.ppermute(value, BOTH, pairs)]
    ppermute x0 -> x25, starting transfers between devices: none -> 36.8 us  [send(): return lax.ppermute(value, BOTH, pairs)]
    psum x1 -> x0, blocking collectives: 34.9 us -> none  [local(): column_total = lax.psum(jnp.sum(log_derivs, axis=0), 'smp')]
    unnamed x1 -> x0, blocking collectives: 30.6 us -> none
    reduce_scatter x1 -> x0, waiting for transfers between devices: 19.5 us -> none  [local(): lax.psum_scatter(partial_gram, 'par', scatter_dimension=1, tiled=True)]
    pallas_call x0 -> x9, Pallas kernels: none -> 19.3 us  [the longest x6 13.3 us: kernel_call(): pl.pallas_call(kernel, out_shape=[jax.ShapeDtypeStruct(s, jnp.float32) fo...]
    dot_general x2 -> x0, matrix products: 19 us -> none  [the longest x1 18.3 us: row_products(): lax.dot_general(left_rows, right_rows, (((1,), (1,)), ((), ())), precisio...]
  transfers between devices with their start and end apart: 2 -> 25, of which waited for: 2 -> 10; matrix products, arithmetic and copies ran while one was open for 1% -> 1% of each run, Pallas kernels for 0% -> 15%
where the time goes in v2:
time: 113 us; the launch traced here: 112 us
  waiting for transfers between devices  54 us (48%)
  starting transfers between devices  36.8 us (33%)
  Pallas kernels  19.3 us (17%)
    ppermute x25, waiting for transfers between devices, send(): return lax.ppermute(value, BOTH, pairs)  54 us
    ppermute x25, starting transfers between devices, send(): return lax.ppermute(value, BOTH, pairs)  36.8 us
    pallas_call x6, Pallas kernels, kernel_call(): pl.pallas_call(kernel, out_shape=[jax.ShapeDtypeStruct(s, jnp.float32) fo...  13.3 us
    pallas_call x2, Pallas kernels, place(): pl.pallas_call(functools.partial(place_kernel, planes, [len(terms) for te...  4.13 us
  transfers between devices with their start and end apart: 25, of which 10 were waited for; matrix products, arithmetic and copies ran while one was open for 1% of the time, Pallas kernels for 15%

profile of v2, /device:TPU:0, one launch (start us, length us, event | category | flops | bytes accessed | tf_op | source)
XLA Modules:
  0.0 112.1 jit_solution(7076771898912759708)
XLA Ops:
  0.6 3.0 %collective-permute-start.8 = (f32[256,1024]{1,0:T(8,128)}, f32[256,1024]{1,0:T(8,128)S(1)}, u32[]{:S(2)}, u32[]{:S(2)}) collective-permute-start(f32[256,1024]{1,0:T(8,128)} %refs_4_.1), channel_id=1, source_target_pairs={{0,4},{1,5},{2,6},{3,7},{4,0},{5,1},{6,2},{7,3},{8,12},{9,13},{10,... | collective-permute-start | bytes 3145736 | tf_op jit(solution)/shard_map/ppermute | solution.py:246
  3.6 1.6 %collective-permute-start.7 = (f32[256,1024]{1,0:T(8,128)}, f32[256,1024]{1,0:T(8,128)S(1)}, u32[]{:S(2)}, u32[]{:S(2)}) collective-permute-start(f32[256,1024]{1,0:T(8,128)} %refs_4_.1), channel_id=1, source_target_pairs={{0,8},{1,9},{2,26},{3,27},{4,12},{5,13},{6,30},{7,31},{8,16},{9,17... | collective-permute-start | bytes 3145736 | tf_op jit(solution)/shard_map/ppermute | solution.py:246
  5.9 1.9 %block_stats.1.refs_0_ = f32[8,1024]{1,0:T(8,128)S(1)} custom-call(f32[256,1024]{1,0:T(8,128)} %refs_4_.1, f32[1,256]{1,0:T(1,128)S(1)} %bitcast.3), custom_call_target="tpu_custom_call" | custom-call | tf_op jit(solution)/shard_map/block_stats/pallas_call | solution.py:59
  7.8 2.3 %collective-permute-start.2 = (f32[8,1024]{1,0:T(8,128)S(1)}, f32[8,1024]{1,0:T(8,128)S(1)}, u32[]{:S(2)}, u32[]{:S(2)}) collective-permute-start(f32[8,1024]{1,0:T(8,128)S(1)} %block_stats.1.refs_0_), channel_id=1, source_target_pairs={{0,24},{1,25},{2,26},{3,27},{4,28},{5,29},{6,30},{7,31},{8,0},{9,1... | collective-permute-start | bytes 98312 | tf_op jit(solution)/shard_map/ppermute | solution.py:246
  10.0 0.8 collective-permute-start.1
  10.8 1.6 %collective-permute-start = (f32[8,1024]{1,0:T(8,128)S(1)}, f32[8,1024]{1,0:T(8,128)S(1)}, u32[]{:S(2)}, u32[]{:S(2)}) collective-permute-start(f32[8,1024]{1,0:T(8,128)S(1)} %block_stats.1.refs_0_), channel_id=1, source_target_pairs={{0,8},{1,9},{2,10},{3,11},{4,12},{5,13},{6,14},{7,15},{8,16},{9,17... | collective-permute-start | bytes 98312 | tf_op jit(solution)/shard_map/ppermute | solution.py:246
  12.4 16.7 %collective-permute-done.2.refs_3_ = f32[8,1024]{1,0:T(8,128)S(1)} collective-permute-done((f32[8,1024]{1,0:T(8,128)S(1)}, f32[8,1024]{1,0:T(8,128)S(1)}, u32[]{:S(2)}, u32[]{:S(2)}) %collective-permute-start.2) | collective-permute-done | bytes 32800 | tf_op jit(solution)/shard_map/ppermute | solution.py:246
  29.1 1.2 %collective-permute-start.6 = (f32[256,1024]{1,0:T(8,128)}, f32[256,1024]{1,0:T(8,128)S(1)}, u32[]{:S(2)}, u32[]{:S(2)}) collective-permute-start(f32[256,1024]{1,0:T(8,128)} %refs_4_.1), channel_id=1, source_target_pairs={{0,2},{1,3},{2,0},{3,1},{4,6},{5,7},{6,4},{7,5},{8,10},{9,11},{10,... | collective-permute-start | bytes 3145736 | tf_op jit(solution)/shard_map/ppermute | solution.py:246
  30.4 2.2 %collective-permute-done.refs_1_ = f32[8,1024]{1,0:T(8,128)S(1)} collective-permute-done((f32[8,1024]{1,0:T(8,128)S(1)}, f32[8,1024]{1,0:T(8,128)S(1)}, u32[]{:S(2)}, u32[]{:S(2)}) %collective-permute-start) | collective-permute-done | bytes 32800 | tf_op jit(solution)/shard_map/ppermute | solution.py:246
  32.7 0.8 collective-permute-start.10
  33.5 2.8 %collective-permute-start.5 = (f32[8,1024]{1,0:T(8,128)S(1)}, f32[8,1024]{1,0:T(8,128)S(1)}, u32[]{:S(2)}, u32[]{:S(2)}) collective-permute-start(f32[8,1024]{1,0:T(8,128)S(1)} %merge.2.refs_0_), channel_id=1, source_target_pairs={{0,6},{1,7},{2,4},{3,5},{4,2},{5,3},{6,0},{7,1},{8,14},{9,15},{10,... | collective-permute-start | bytes 98312 | tf_op jit(solution)/shard_map/ppermute | solution.py:246
  36.3 1.5 %collective-permute-start.4 = (f32[8,1024]{1,0:T(8,128)S(1)}, f32[8,1024]{1,0:T(8,128)S(1)}, u32[]{:S(2)}, u32[]{:S(2)}) collective-permute-start(f32[8,1024]{1,0:T(8,128)S(1)} %merge.2.refs_0_), channel_id=1, source_target_pairs={{0,4},{1,5},{2,6},{3,7},{4,0},{5,1},{6,2},{7,3},{8,12},{9,13},{10,... | collective-permute-start | bytes 98312 | tf_op jit(solution)/shard_map/ppermute | solution.py:246
  37.9 1.9 %collective-permute-start.3 = (f32[8,1024]{1,0:T(8,128)S(1)}, f32[8,1024]{1,0:T(8,128)S(1)}, u32[]{:S(2)}, u32[]{:S(2)}) collective-permute-start(f32[8,1024]{1,0:T(8,128)S(1)} %merge.2.refs_0_), channel_id=1, source_target_pairs={{0,2},{1,3},{2,0},{3,1},{4,6},{5,7},{6,4},{7,5},{8,10},{9,11},{10,... | collective-permute-start | bytes 98312 | tf_op jit(solution)/shard_map/ppermute | solution.py:246
  40.7 3.1 %products_near.1 = (f32[256,256]{1,0:T(8,128)S(1)}, f32[256,256]{1,0:T(8,128)S(1)}, f32[256,256]{1,0:T(8,128)S(1)}, f32[256,256]{1,0:T(8,128)S(1)}) custom-call(f32[8,1024]{1,0:T(8,128)S(1)} %merge.3.mean_ref, f32[256,1024]{1,0:T(8,128)} %refs_4_.1, f32[256,1024]{1,0:T(8,128)S(1)} %collective-permute-done.6.refs_1_, ...), custom_call_target="tpu_custom_call" | custom-call | tf_op jit(solution)/shard_map/products_near/pallas_call | solution.py:132
  43.9 3.4 %collective-permute-start.11 = (f32[256,256]{1,0:T(8,128)S(1)}, f32[256,256]{1,0:T(8,128)S(1)}, u32[]{:S(2)}, u32[]{:S(2)}) collective-permute-start(f32[256,256]{1,0:T(8,128)S(1)} %get-tuple-element.24), channel_id=1, source_target_pairs={{0,1},{1,3},{2,2},{3,0},{4,5},{5,7},{6,6},{7,4},{8,8},{9,10},{10,1... | collective-permute-start | bytes 786440 | tf_op jit(solution)/shard_map/ppermute | solution.py:246
  47.3 2.1 %collective-permute-start.12 = (f32[256,256]{1,0:T(8,128)S(1)}, f32[256,256]{1,0:T(8,128)S(1)}, u32[]{:S(2)}, u32[]{:S(2)}) collective-permute-start(f32[256,256]{1,0:T(8,128)S(1)} %get-tuple-element.25), channel_id=1, source_target_pairs={{0,3},{1,1},{2,0},{3,2},{4,7},{5,5},{6,4},{7,6},{8,10},{9,8},{10,9... | collective-permute-start | bytes 786440 | tf_op jit(solution)/shard_map/ppermute | solution.py:246
  49.5 2.6 %collective-permute-start.14 = (f32[256,256]{1,0:T(8,128)S(1)}, f32[256,256]{1,0:T(8,128)S(1)}, u32[]{:S(2)}, u32[]{:S(2)}) collective-permute-start(f32[256,256]{1,0:T(8,128)S(1)} %get-tuple-element.27), channel_id=1, source_target_pairs={{0,7},{1,5},{2,4},{3,6},{4,3},{5,1},{6,0},{7,2},{8,14},{9,12},{10,... | collective-permute-start | bytes 786440 | tf_op jit(solution)/shard_map/ppermute | solution.py:246
  52.1 8.3 %collective-permute-done.10.refs_5_ = f32[256,1024]{1,0:T(8,128)S(1)} collective-permute-done((f32[256,1024]{1,0:T(8,128)S(1)}, f32[256,1024]{1,0:T(8,128)S(1)}, u32[]{:S(2)}, u32[]{:S(2)}) %collective-permute-start.10) | collective-permute-done | bytes 1048608 | tf_op jit(solution)/shard_map/ppermute | solution.py:246
  60.4 2.9 %collective-permute-done.14.refs_3_ = f32[256,256]{1,0:T(8,128)S(1)} collective-permute-done((f32[256,256]{1,0:T(8,128)S(1)}, f32[256,256]{1,0:T(8,128)S(1)}, u32[]{:S(2)}, u32[]{:S(2)}) %collective-permute-start.14) | collective-permute-done | bytes 262176 | tf_op jit(solution)/shard_map/ppermute | solution.py:246
  63.3 5.3 %products_across.1 = (f32[512,256]{1,0:T(8,128)S(1)}, f32[512,256]{1,0:T(8,128)S(1)}, f32[512,256]{1,0:T(8,128)S(1)}, f32[512,256]{1,0:T(8,128)S(1)}) custom-call(s32[32,16]{1,0:T(8,128)S(1)} %copy-done, f32[8,1024]{1,0:T(8,128)S(1)} %merge.3.mean_ref, f32[256,1024]{1,0:T(8,128)} %refs_4_.1, f32[256,1024]{1,0:T(8,128)S(1)} %collective-permute-done.6.refs_1_, ...), custom_call_target="tpu_custom_call" | custom-call | tf_op jit(solution)/shard_map/products_across/pallas_call | solution.py:132
  68.8 1.1 collective-permute-start.21
  69.9 2.3 %collective-permute-start.22 = (f32[512,256]{1,0:T(8,128)S(1)}, f32[512,256]{1,0:T(8,128)S(1)}, u32[]{:S(2)}, u32[]{:S(2)}) collective-permute-start(f32[512,256]{1,0:T(8,128)S(1)} %get-tuple-element.37), channel_id=1, source_target_pairs={{0,5},{1,4},{2,7},{3,6},{4,1},{5,0},{6,3},{7,2},{8,13},{9,12},{10,... | collective-permute-start | bytes 1572872 | tf_op jit(solution)/shard_map/ppermute | solution.py:246
  72.2 15.7 %collective-permute-done.15.refs_4_ = f32[256,1024]{1,0:T(8,128)S(1)} collective-permute-done((f32[256,1024]{1,0:T(8,128)S(1)}, f32[256,1024]{1,0:T(8,128)S(1)}, u32[]{:S(2)}, u32[]{:S(2)}) %collective-permute-start.15) | collective-permute-done | bytes 1048608 | tf_op jit(solution)/shard_map/ppermute | solution.py:246
  87.9 4.0 %products_far.1 = (f32[256,256]{1,0:T(8,128)}, f32[256,256]{1,0:T(8,128)S(1)}, f32[256,256]{1,0:T(8,128)}, f32[256,256]{1,0:T(8,128)}) custom-call(f32[8,1024]{1,0:T(8,128)S(1)} %merge.3.mean_ref, f32[256,1024]{1,0:T(8,128)} %refs_4_.1, f32[256,1024]{1,0:T(8,128)S(1)} %collective-permute-done.6.refs_1_, f32[256,1024]{1,0:T(8,128)S(1)} %collective-permute-done.8.refs_2_, ...), custom_call_target="tpu_custom_call" | custom-call | tf_op jit(solution)/shard_map/products_far/pallas_call | solution.py:132
  91.8 2.8 %collective-permute-start.17 = (f32[256,256]{1,0:T(8,128)S(1)}, f32[256,256]{1,0:T(8,128)S(1)}, u32[]{:S(2)}, u32[]{:S(2)}) collective-permute-start(f32[256,256]{1,0:T(8,128)S(1)} %get-tuple-element.30), channel_id=1, source_target_pairs={{0,2},{1,0},{2,1},{3,3},{4,6},{5,4},{6,5},{7,7},{8,11},{9,9},{10,8... | collective-permute-start | bytes 786440 | tf_op jit(solution)/shard_map/ppermute | solution.py:246
  94.6 1.1 collective-permute-start.18
  95.7 3.6 %collective-permute-start.16 = (f32[256,256]{1,0:T(8,128)}, f32[256,256]{1,0:T(8,128)}, u32[]{:S(2)}, u32[]{:S(2)}) collective-permute-start(f32[256,256]{1,0:T(8,128)} %get-tuple-element.29), channel_id=1, source_target_pairs={{0,0},{1,2},{2,3},{3,1},{4,4},{5,6},{6,7},{7,5},{8,9},{9,11},{10,1... | collective-permute-start | bytes 786440 | tf_op jit(solution)/shard_map/ppermute | solution.py:246
  99.3 0.9 sum_across.1
  100.2 1.1 %collective-permute-done.17.refs_1_ = f32[256,256]{1,0:T(8,128)S(1)} collective-permute-done((f32[256,256]{1,0:T(8,128)S(1)}, f32[256,256]{1,0:T(8,128)S(1)}, u32[]{:S(2)}, u32[]{:S(2)}) %collective-permute-start.17) | collective-permute-done | bytes 262176 | tf_op jit(solution)/shard_map/ppermute | solution.py:246
  101.3 1.8 %place_most.1.refs_6_ = f32[256,2048]{1,0:T(8,128)} custom-call(s32[32,16]{1,0:T(8,128)S(1)} %copy-done, f32[256,256]{1,0:T(8,128)S(1)} %collective-permute-done.11.refs_0_, f32[256,256]{1,0:T(8,128)S(1)} %collective-permute-done.12.refs_1_, f32[256,256]{1,0:T(8,128)S(1)} %collective-permute-done.13.refs_2_, f32[256,256]{1,0:T(8,128)S(1)} %collective-permute-done.14.refs_3_, ...), custom_call_target="tpu_custom_call" | custom-call | tf_op jit(solution)/shard_map/place_most/pallas_call | solution.py:174
  103.7 6.1 %collective-permute-done.19.refs_3_ = f32[256,256]{1,0:T(8,128)} collective-permute-done((f32[256,256]{1,0:T(8,128)}, f32[256,256]{1,0:T(8,128)}, u32[]{:S(2)}, u32[]{:S(2)}) %collective-permute-start.19) | collective-permute-done | bytes 262176 | tf_op jit(solution)/shard_map/ppermute | solution.py:246
  109.8 2.3 %place_last.1 = f32[256,2048]{1,0:T(8,128)} custom-call(s32[32,16]{1,0:T(8,128)S(1)} %copy-done, f32[256,256]{1,0:T(8,128)} %collective-permute-done.16.refs_0_, f32[256,256]{1,0:T(8,128)S(1)} %collective-permute-done.17.refs_1_, f32[256,256]{1,0:T(8,128)} %collective-permute-done.18.refs_2_, ...), custom_call_target="tpu_custom_call", output_to_operand_aliasing={{}: (7, {})} | custom-call | tf_op jit(solution)/shard_map/place_last/pallas_call | solution.py:174
  (32 shorter events, 2.6 us)
Async XLA Ops:
  0.6 32.0 %collective-permute-start.8 = (f32[256,1024]{1,0:T(8,128)}, f32[256,1024]{1,0:T(8,128)S(1)}, u32[]{:S(2)}, u32[]{:S(2)}) collective-permute-start(f32[256,1024]{1,0:T(8,128)} %refs_4_.1), channel_id=1, source_target_pairs={{0,4},{1,5},{2,6},{3,7},{4,0},{5,1},{6,2},{7,3},{8,12},{9,13},{10,... | collective-permute-start | bytes 3145736 | tf_op jit(solution)/shard_map/ppermute | solution.py:246
  3.6 29.0 %collective-permute-start.7 = (f32[256,1024]{1,0:T(8,128)}, f32[256,1024]{1,0:T(8,128)S(1)}, u32[]{:S(2)}, u32[]{:S(2)}) collective-permute-start(f32[256,1024]{1,0:T(8,128)} %refs_4_.1), channel_id=1, source_target_pairs={{0,8},{1,9},{2,26},{3,27},{4,12},{5,13},{6,30},{7,31},{8,16},{9,17... | collective-permute-start | bytes 3145736 | tf_op jit(solution)/shard_map/ppermute | solution.py:246
  5.2 0.7 copy-start.1
  7.8 21.3 %collective-permute-start.2 = (f32[8,1024]{1,0:T(8,128)S(1)}, f32[8,1024]{1,0:T(8,128)S(1)}, u32[]{:S(2)}, u32[]{:S(2)}) collective-permute-start(f32[8,1024]{1,0:T(8,128)S(1)} %block_stats.1.refs_0_), channel_id=1, source_target_pairs={{0,24},{1,25},{2,26},{3,27},{4,28},{5,29},{6,30},{7,31},{8,0},{9,1... | collective-permute-start | bytes 98312 | tf_op jit(solution)/shard_map/ppermute | solution.py:246
  10.0 20.3 %collective-permute-start.1 = (f32[8,1024]{1,0:T(8,128)S(1)}, f32[8,1024]{1,0:T(8,128)S(1)}, u32[]{:S(2)}, u32[]{:S(2)}) collective-permute-start(f32[8,1024]{1,0:T(8,128)S(1)} %block_stats.1.refs_0_), channel_id=1, source_target_pairs={{0,16},{1,17},{2,18},{3,19},{4,20},{5,21},{6,22},{7,23},{8,24},{9,... | collective-permute-start | bytes 98312 | tf_op jit(solution)/shard_map/ppermute | solution.py:246
  10.8 21.8 %collective-permute-start = (f32[8,1024]{1,0:T(8,128)S(1)}, f32[8,1024]{1,0:T(8,128)S(1)}, u32[]{:S(2)}, u32[]{:S(2)}) collective-permute-start(f32[8,1024]{1,0:T(8,128)S(1)} %block_stats.1.refs_0_), channel_id=1, source_target_pairs={{0,8},{1,9},{2,10},{3,11},{4,12},{5,13},{6,14},{7,15},{8,16},{9,17... | collective-permute-start | bytes 98312 | tf_op jit(solution)/shard_map/ppermute | solution.py:246
  29.1 11.6 %collective-permute-start.6 = (f32[256,1024]{1,0:T(8,128)}, f32[256,1024]{1,0:T(8,128)S(1)}, u32[]{:S(2)}, u32[]{:S(2)}) collective-permute-start(f32[256,1024]{1,0:T(8,128)} %refs_4_.1), channel_id=1, source_target_pairs={{0,2},{1,3},{2,0},{3,1},{4,6},{5,7},{6,4},{7,5},{8,10},{9,11},{10,... | collective-permute-start | bytes 3145736 | tf_op jit(solution)/shard_map/ppermute | solution.py:246
  32.6 8.1 %collective-permute-start.9 = (f32[256,1024]{1,0:T(8,128)S(1)}, f32[256,1024]{1,0:T(8,128)S(1)}, u32[]{:S(2)}, u32[]{:S(2)}) collective-permute-start(f32[256,1024]{1,0:T(8,128)S(1)} %collective-permute-done.8.refs_2_), channel_id=1, source_target_pairs={{0,2},{1,3},{2,0},{3,1},{4,6},{5,7},{6,4},{7,5},{8,10},{9,11},{10,... | collective-permute-start | bytes 3145736 | tf_op jit(solution)/shard_map/ppermute | solution.py:246
  32.7 27.7 %collective-permute-start.10 = (f32[256,1024]{1,0:T(8,128)S(1)}, f32[256,1024]{1,0:T(8,128)S(1)}, u32[]{:S(2)}, u32[]{:S(2)}) collective-permute-start(f32[256,1024]{1,0:T(8,128)S(1)} %collective-permute-done.7.refs_4_), channel_id=1, source_target_pairs={{0,8},{1,9},{2,26},{3,27},{4,12},{5,13},{6,30},{7,31},{8,16},{9,17... | collective-permute-start | bytes 3145736 | tf_op jit(solution)/shard_map/ppermute | solution.py:246
  33.5 4.4 %collective-permute-start.5 = (f32[8,1024]{1,0:T(8,128)S(1)}, f32[8,1024]{1,0:T(8,128)S(1)}, u32[]{:S(2)}, u32[]{:S(2)}) collective-permute-start(f32[8,1024]{1,0:T(8,128)S(1)} %merge.2.refs_0_), channel_id=1, source_target_pairs={{0,6},{1,7},{2,4},{3,5},{4,2},{5,3},{6,0},{7,1},{8,14},{9,15},{10,... | collective-permute-start | bytes 98312 | tf_op jit(solution)/shard_map/ppermute | solution.py:246
  36.3 3.9 %collective-permute-start.4 = (f32[8,1024]{1,0:T(8,128)S(1)}, f32[8,1024]{1,0:T(8,128)S(1)}, u32[]{:S(2)}, u32[]{:S(2)}) collective-permute-start(f32[8,1024]{1,0:T(8,128)S(1)} %merge.2.refs_0_), channel_id=1, source_target_pairs={{0,4},{1,5},{2,6},{3,7},{4,0},{5,1},{6,2},{7,3},{8,12},{9,13},{10,... | collective-permute-start | bytes 98312 | tf_op jit(solution)/shard_map/ppermute | solution.py:246
  37.9 2.8 %collective-permute-start.3 = (f32[8,1024]{1,0:T(8,128)S(1)}, f32[8,1024]{1,0:T(8,128)S(1)}, u32[]{:S(2)}, u32[]{:S(2)}) collective-permute-start(f32[8,1024]{1,0:T(8,128)S(1)} %merge.2.refs_0_), channel_id=1, source_target_pairs={{0,2},{1,3},{2,0},{3,1},{4,6},{5,7},{6,4},{7,5},{8,10},{9,11},{10,... | collective-permute-start | bytes 98312 | tf_op jit(solution)/shard_map/ppermute | solution.py:246
  40.7 22.7 %copy-start = (s32[32,16]{1,0:T(8,128)S(1)}, s32[32,16]{1,0:T(8,128)}, u32[]{:S(2)}) copy-start(s32[32,16]{1,0:T(8,128)} %constant.19.clone.table_ref) | copy-start | bytes 6148
  43.9 16.5 %collective-permute-start.11 = (f32[256,256]{1,0:T(8,128)S(1)}, f32[256,256]{1,0:T(8,128)S(1)}, u32[]{:S(2)}, u32[]{:S(2)}) collective-permute-start(f32[256,256]{1,0:T(8,128)S(1)} %get-tuple-element.24), channel_id=1, source_target_pairs={{0,1},{1,3},{2,2},{3,0},{4,5},{5,7},{6,6},{7,4},{8,8},{9,10},{10,1... | collective-permute-start | bytes 786440 | tf_op jit(solution)/shard_map/ppermute | solution.py:246
  47.3 13.1 %collective-permute-start.12 = (f32[256,256]{1,0:T(8,128)S(1)}, f32[256,256]{1,0:T(8,128)S(1)}, u32[]{:S(2)}, u32[]{:S(2)}) collective-permute-start(f32[256,256]{1,0:T(8,128)S(1)} %get-tuple-element.25), channel_id=1, source_target_pairs={{0,3},{1,1},{2,0},{3,2},{4,7},{5,5},{6,4},{7,6},{8,10},{9,8},{10,9... | collective-permute-start | bytes 786440 | tf_op jit(solution)/shard_map/ppermute | solution.py:246
  49.4 11.0 %collective-permute-start.13 = (f32[256,256]{1,0:T(8,128)S(1)}, f32[256,256]{1,0:T(8,128)S(1)}, u32[]{:S(2)}, u32[]{:S(2)}) collective-permute-start(f32[256,256]{1,0:T(8,128)S(1)} %get-tuple-element.26), channel_id=1, source_target_pairs={{0,5},{1,7},{2,6},{3,4},{4,1},{5,3},{6,2},{7,0},{8,12},{9,14},{10,... | collective-permute-start | bytes 786440 | tf_op jit(solution)/shard_map/ppermute | solution.py:246
  49.5 13.8 %collective-permute-start.14 = (f32[256,256]{1,0:T(8,128)S(1)}, f32[256,256]{1,0:T(8,128)S(1)}, u32[]{:S(2)}, u32[]{:S(2)}) collective-permute-start(f32[256,256]{1,0:T(8,128)S(1)} %get-tuple-element.27), channel_id=1, source_target_pairs={{0,7},{1,5},{2,4},{3,6},{4,3},{5,1},{6,0},{7,2},{8,14},{9,12},{10,... | collective-permute-start | bytes 786440 | tf_op jit(solution)/shard_map/ppermute | solution.py:246
  63.3 24.6 %collective-permute-start.15 = (f32[256,1024]{1,0:T(8,128)S(1)}, f32[256,1024]{1,0:T(8,128)S(1)}, u32[]{:S(2)}, u32[]{:S(2)}) collective-permute-start(f32[256,1024]{1,0:T(8,128)S(1)} %collective-permute-done.10.refs_5_), channel_id=1, source_target_pairs={{0,8},{1,9},{2,26},{3,27},{4,12},{5,13},{6,30},{7,31},{8,16},{9,17... | collective-permute-start | bytes 3145736 | tf_op jit(solution)/shard_map/ppermute | solution.py:246
  68.6 27.1 %collective-permute-start.20 = (f32[512,256]{1,0:T(8,128)S(1)}, f32[512,256]{1,0:T(8,128)S(1)}, u32[]{:S(2)}, u32[]{:S(2)}) collective-permute-start(f32[512,256]{1,0:T(8,128)S(1)} %get-tuple-element.34), channel_id=1, source_target_pairs={{0,1},{1,0},{2,3},{3,2},{4,5},{5,4},{6,7},{7,6},{8,9},{9,8},{10,11... | collective-permute-start | bytes 1572872 | tf_op jit(solution)/shard_map/ppermute | solution.py:246
  68.8 30.5 %collective-permute-start.21 = (f32[512,256]{1,0:T(8,128)S(1)}, f32[512,256]{1,0:T(8,128)S(1)}, u32[]{:S(2)}, u32[]{:S(2)}) collective-permute-start(f32[512,256]{1,0:T(8,128)S(1)} %get-tuple-element.36), channel_id=1, source_target_pairs={{0,4},{1,5},{2,6},{3,7},{4,0},{5,1},{6,2},{7,3},{8,12},{9,13},{10,... | collective-permute-start | bytes 1572872 | tf_op jit(solution)/shard_map/ppermute | solution.py:246
  69.9 29.4 %collective-permute-start.22 = (f32[512,256]{1,0:T(8,128)S(1)}, f32[512,256]{1,0:T(8,128)S(1)}, u32[]{:S(2)}, u32[]{:S(2)}) collective-permute-start(f32[512,256]{1,0:T(8,128)S(1)} %get-tuple-element.37), channel_id=1, source_target_pairs={{0,5},{1,4},{2,7},{3,6},{4,1},{5,0},{6,3},{7,2},{8,13},{9,12},{10,... | collective-permute-start | bytes 1572872 | tf_op jit(solution)/shard_map/ppermute | solution.py:246
  91.8 9.5 %collective-permute-start.17 = (f32[256,256]{1,0:T(8,128)S(1)}, f32[256,256]{1,0:T(8,128)S(1)}, u32[]{:S(2)}, u32[]{:S(2)}) collective-permute-start(f32[256,256]{1,0:T(8,128)S(1)} %get-tuple-element.30), channel_id=1, source_target_pairs={{0,2},{1,0},{2,1},{3,3},{4,6},{5,4},{6,5},{7,7},{8,11},{9,9},{10,8... | collective-permute-start | bytes 786440 | tf_op jit(solution)/shard_map/ppermute | solution.py:246
  94.6 9.1 %collective-permute-start.18 = (f32[256,256]{1,0:T(8,128)}, f32[256,256]{1,0:T(8,128)}, u32[]{:S(2)}, u32[]{:S(2)}) collective-permute-start(f32[256,256]{1,0:T(8,128)} %get-tuple-element.31), channel_id=1, source_target_pairs={{0,4},{1,6},{2,7},{3,5},{4,0},{5,2},{6,3},{7,1},{8,13},{9,15},{10,... | collective-permute-start | bytes 786440 | tf_op jit(solution)/shard_map/ppermute | solution.py:246
  95.7 14.1 %collective-permute-start.16 = (f32[256,256]{1,0:T(8,128)}, f32[256,256]{1,0:T(8,128)}, u32[]{:S(2)}, u32[]{:S(2)}) collective-permute-start(f32[256,256]{1,0:T(8,128)} %get-tuple-element.29), channel_id=1, source_target_pairs={{0,0},{1,2},{2,3},{3,1},{4,4},{5,6},{6,7},{7,5},{8,9},{9,11},{10,1... | collective-permute-start | bytes 786440 | tf_op jit(solution)/shard_map/ppermute | solution.py:246
  99.3 10.5 %collective-permute-start.19 = (f32[256,256]{1,0:T(8,128)}, f32[256,256]{1,0:T(8,128)}, u32[]{:S(2)}, u32[]{:S(2)}) collective-permute-start(f32[256,256]{1,0:T(8,128)} %get-tuple-element.32), channel_id=1, source_target_pairs={{0,6},{1,4},{2,5},{3,7},{4,2},{5,0},{6,1},{7,3},{8,15},{9,13},{10,... | collective-permute-start | bytes 786440 | tf_op jit(solution)/shard_map/ppermute | solution.py:246
  100.2 9.6 %collective-permute-start.23 = (f32[256,256]{1,0:T(8,128)}, f32[256,256]{1,0:T(8,128)}, u32[]{:S(2)}, u32[]{:S(2)}) collective-permute-start(f32[256,256]{1,0:T(8,128)} %get-tuple-element.38), channel_id=1, source_target_pairs={{0,2},{1,3},{2,0},{3,1},{4,6},{5,7},{6,4},{7,5},{8,10},{9,11},{10,... | collective-permute-start | bytes 786440 | tf_op jit(solution)/shard_map/ppermute | solution.py:246
  101.3 8.5 %collective-permute-start.24 = (f32[256,256]{1,0:T(8,128)}, f32[256,256]{1,0:T(8,128)}, u32[]{:S(2)}, u32[]{:S(2)}) collective-permute-start(f32[256,256]{1,0:T(8,128)} %get-tuple-element.39), channel_id=1, source_target_pairs={{0,2},{1,3},{2,0},{3,1},{4,6},{5,7},{6,4},{7,5},{8,10},{9,11},{10,... | collective-permute-start | bytes 786440 | tf_op jit(solution)/shard_map/ppermute | solution.py:246

commit v3 on v2

--- a/solution.py
+++ b/solution.py
@@ -9,7 +9,7 @@
 from jax.sharding import PartitionSpec as P
 
 BOTH = ("smp", "par")
-VMEM_LIMIT = 24 * 1024 * 1024
+VMEM_LIMIT = 16 * 1024 * 1024
 FREE = pl.CostEstimate(flops=0, bytes_accessed=0, transcendentals=0)
 
 
@@ -44,25 +44,23 @@
     return lax.optimization_barrier((value, *others))[0]
 
 
-def stats_kernel(rows_ref, coef_ref, stats_ref):
-    rows = rows_ref[...]
-    mean = jnp.sum(rows, axis=0, keepdims=True) / rows.shape[0]
+def stats_kernel(rows_ref, other_ref, coef_ref, other_coef_ref, stats_ref):
+    blocks = (rows_ref, other_ref)
+    mean = sum(jnp.sum(ref[...], axis=0, keepdims=True) for ref in blocks) / sum(ref.shape[0] for ref in blocks)
+    stats_ref[...] = jnp.zeros_like(stats_ref)
     stats_ref[0:1, :] = mean
-    stats_ref[1:2, :] = jnp.dot(
-        coef_ref[...], rows - mean, precision=lax.Precision.HIGHEST, preferred_element_type=jnp.float32
-    )
-    stats_ref[2:3, :] = jnp.broadcast_to(jnp.sum(coef_ref[...], axis=1, keepdims=True), mean.shape)
-    stats_ref[3:, :] = jnp.zeros((stats_ref.shape[0] - 3, mean.shape[1]), jnp.float32)
-
-
-def block_stats(rows, coefficients):
-    return pl.pallas_call(
-        stats_kernel,
-        out_shape=jax.ShapeDtypeStruct((8, rows.shape[1]), jnp.float32),
-        compiler_params=pltpu.CompilerParams(vmem_limit_bytes=VMEM_LIMIT),
-        cost_estimate=FREE,
-        name="block_stats",
-    )(rows, coefficients[None, :])
+    stats_ref[1:2, :] = sum(
+        jnp.dot(coef[...], ref[...] - mean, precision=lax.Precision.HIGHEST, preferred_element_type=jnp.float32)
+        for coef, ref in zip((coef_ref, other_coef_ref), blocks)
+    )
+    total = sum(jnp.sum(coef[...], axis=1, keepdims=True) for coef in (coef_ref, other_coef_ref))
+    stats_ref[2:3, :] = jnp.broadcast_to(total, mean.shape)
+
+
+def block_stats(rows, other, coefficients, other_coefficients):
+    return kernel_call(
+        stats_kernel, [(8, rows.shape[1])], "block_stats", rows, other, coefficients, other_coefficients
+    )[0]
 
 
 def merge_kernel(count, *refs):
@@ -108,18 +106,27 @@
         outs[2 * side + 1][...] = jnp.where(straight, other, same)
 
 
-def two_levels_kernel(scale, planes, flag_at, table_ref, mean_ref, *refs):
-    rows, blocks, outs = refs[:4], refs[4:6], refs[6:]
+def own_level_kernel(scale, mean_ref, *refs):
+    rows, block, outs = refs[:4], refs[4], refs[5:]
+    mean = mean_ref[0:1, :]
+    high, low = split(block[...] - mean)
+    height = rows[0].shape[0]
+    for k, row in enumerate(rows):
+        outs[k // 2][k % 2 * height : (k % 2 + 1) * height, :] = product_of(row, mean, high, low, scale)
+
+
+def across_level_kernel(scale, planes, flag_at, table_ref, mean_ref, *refs):
+    rows, block, level, outs = refs[:4], refs[4], refs[5:7], refs[7:]
     mean = mean_ref[0:1, :]
     first = table_ref[device_row(planes), flag_at] == 1
-    high, low = split(jnp.concatenate([block[...] for block in blocks], axis=0) - mean)
-    height, width = rows[0].shape[0], blocks[0].shape[0]
+    high, low = split(block[...] - mean)
+    height = rows[0].shape[0]
     for k, row in enumerate(rows):
         total = product_of(row, mean, high, low, scale)
-        one, other = total[:, :width], total[:, width:]
         place = slice(k % 2 * height, (k % 2 + 1) * height)
-        outs[k // 2][place, :] = jnp.where(first, one, other)
-        outs[2 + k // 2][place, :] = jnp.where(first, other, one)
+        here = level[k // 2][place, :]
+        outs[k // 2][place, :] = jnp.where(first, here, total)
+        outs[2 + k // 2][place, :] = jnp.where(first, total, here)
 
 
 def across_kernel(keep_own, got_own, from_side, got_side, own, side):
@@ -234,7 +241,6 @@
     ring = moves(lambda z, x, c, y: (z + 1 - 2 * c, x, c, y))
     over_core = moves(lambda z, x, c, y: (z, x, 1 - c, y))
     over_side = moves(lambda z, x, c, y: (z, 1 - x, c, y))
-    over_both = moves(lambda z, x, c, y: (z, 1 - x, 1 - c, y))
     over_plane = moves(lambda z, x, c, y: (z, x, c, 1 - y))
     diagonal = moves(lambda z, x, c, y: (z, 1 - x, c, 1 - y))
     turns = [moves(lambda z, x, c, y, k=k: (z + k, x, c, y)) for k in range(1, levels)]
@@ -252,11 +258,12 @@
 
     side_rows = send(log_derivs, over_side)
 
-    stats = block_stats(log_derivs, coefficients)
+    coefficients = coefficients[None, :]
+    stats = block_stats(log_derivs, core_rows, coefficients, send(coefficients, over_core))
     stats = merge(stats, *[send(stats, turn) for turn in turns])
     one, side_rows = lax.optimization_barrier((one, side_rows, stats))[:2]
     two = send(one, ring)
-    stats = merge(stats, send(stats, over_core), send(stats, over_side), send(stats, over_both))
+    stats = merge(stats, send(stats, over_side))
     side_core_rows = send(side_rows, over_core)
     all_rows = (log_derivs, core_rows, side_rows, side_core_rows)
 
@@ -268,17 +275,25 @@
     out, near = one_level(one, 1, "products_near")
     share = params // lax.axis_size("smp")
 
-    two = after(two, *near[0], *near[1])
+    own_level = kernel_call(
+        functools.partial(own_level_kernel, scale),
+        [(2 * rows, rows)] * 2,
+        "products_level",
+        stats,
+        *all_rows,
+        after(log_derivs, out[0]),
+    )
+    two = after(two, *near[0], *near[1], *own_level)
     three = send(two, ring)
     keep_own, keep_side, sent_own, sent_side = kernel_call(
-        functools.partial(two_levels_kernel, scale, planes, 0),
+        functools.partial(across_level_kernel, scale, planes, 0),
         [(2 * rows, rows)] * 4,
         "products_across",
         table,
         stats,
         *all_rows,
-        log_derivs,
         two,
+        *own_level,
         smem=1,
     )
     got_own = send(sent_own, over_plane)

time: 113 us -> 110 us (0.973)
  Pallas kernels: 19.3 us -> 15.4 us
  local copies, waits for them, and re-layouts: 0.69 us -> 1.91 us
    pallas_call x6 -> x8, Pallas kernels: 13.3 us -> 11.3 us  [kernel_call(): pl.pallas_call(kernel, out_shape=[jax.ShapeDtypeStruct(s, jnp.float32) fo...]
    pallas_call x1 -> x0, Pallas kernels: 1.89 us -> none  [block_stats(): pl.pallas_call(stats_kernel, out_shape=jax.ShapeDtypeStruct((8, rows.shap...]
    unnamed x4 -> x8, local copies, waits for them, and re-layouts: 0.69 us -> 1.91 us
    ppermute x25 -> x24, waiting for transfers between devices: 54 us -> 55 us  [send(): return lax.ppermute(value, BOTH, pairs)]
    ppermute x25 -> x24, starting transfers between devices: 36.8 us -> 35.9 us  [send(): return lax.ppermute(value, BOTH, pairs)]
  transfers between devices with their start and end apart: 25 -> 24, of which waited for: 10 -> 7; matrix products, arithmetic and copies ran while one was open for 1% -> 1% of each run, Pallas kernels for 15% -> 12%
where the time goes in v3:
time: 110 us
  waiting for transfers between devices  55 us (50%)
  starting transfers between devices  35.9 us (33%)
  Pallas kernels  15.4 us (14%)
  local copies, waits for them, and re-layouts  1.91 us (2%)
    ppermute x24, waiting for transfers between devices, send(): return lax.ppermute(value, BOTH, pairs)  55 us
    ppermute x24, starting transfers between devices, send(): return lax.ppermute(value, BOTH, pairs)  35.9 us
    pallas_call x8, Pallas kernels, kernel_call(): pl.pallas_call(kernel, out_shape=[jax.ShapeDtypeStruct(s, jnp.float32) fo...  11.3 us
    pallas_call x2, Pallas kernels, place(): pl.pallas_call(functools.partial(place_kernel, planes, [len(terms) for te...  4.12 us
  transfers between devices with their start and end apart: 24, of which 7 were waited for; matrix products, arithmetic and copies ran while one was open for 1% of the time, Pallas kernels for 12%

profile of v3, /device:TPU:0, one launch (start us, length us, event | category | flops | bytes accessed | tf_op | source)
XLA Modules:
  0.0 109.6 jit_solution(16579250892754827940)
XLA Ops:
  1.1 2.6 %collective-permute-start.6 = (f32[256,1024]{1,0:T(8,128)}, f32[256,1024]{1,0:T(8,128)S(1)}, u32[]{:S(2)}, u32[]{:S(2)}) collective-permute-start(f32[256,1024]{1,0:T(8,128)} %refs_0_.7), channel_id=1, source_target_pairs={{0,8},{1,9},{2,26},{3,27},{4,12},{5,13},{6,30},{7,31},{8,16},{9,17... | collective-permute-start | bytes 3145736 | tf_op jit(solution)/shard_map/ppermute | solution.py:252
  3.8 1.5 %collective-permute-start.7 = (f32[256,1024]{1,0:T(8,128)}, f32[256,1024]{1,0:T(8,128)S(1)}, u32[]{:S(2)}, u32[]{:S(2)}) collective-permute-start(f32[256,1024]{1,0:T(8,128)} %refs_0_.7), channel_id=1, source_target_pairs={{0,4},{1,5},{2,6},{3,7},{4,0},{5,1},{6,2},{7,3},{8,12},{9,13},{10,... | collective-permute-start | bytes 3145736 | tf_op jit(solution)/shard_map/ppermute | solution.py:252
  5.3 1.9 %collective-permute-start.1 = (f32[1,256]{1,0:T(1,128)}, f32[1,256]{1,0:T(1,128)S(1)}, u32[]{:S(2)}, u32[]{:S(2)}) collective-permute-start(f32[1,256]{1,0:T(1,128)} %bitcast.3), channel_id=1, source_target_pairs={{0,2},{1,3},{2,0},{3,1},{4,6},{5,7},{6,4},{7,5},{8,10},{9,11},{10,... | collective-permute-start | bytes 3080 | tf_op jit(solution)/shard_map/ppermute | solution.py:252
  7.2 1.0 collective-permute-done.1.other_coef_ref
  8.2 1.2 %copy-done = f32[256,1024]{1,0:T(8,128)S(1)} copy-done((f32[256,1024]{1,0:T(8,128)S(1)}, f32[256,1024]{1,0:T(8,128)}, u32[]{:S(2)}) %copy-start) | copy-done | bytes 1048600
  9.4 0.7 copy-done.3
  10.1 1.2 %block_stats.1.refs_0_ = f32[8,1024]{1,0:T(8,128)S(1)} custom-call(f32[256,1024]{1,0:T(8,128)S(1)} %copy-done, f32[256,1024]{1,0:T(8,128)S(1)} %collective-permute-done.other_ref.refs_1_, f32[1,256]{1,0:T(1,128)S(1)} %bitcast.4, f32[1,256]{1,0:T(1,128)S(1)} %collective-permute-done.1.other_coef_ref), custom_call_target="tpu_custom_call" | custom-call | tf_op jit(solution)/shard_map/block_stats/pallas_call | solution.py:139
  11.3 1.3 %collective-permute-start.3 = (f32[8,1024]{1,0:T(8,128)S(1)}, f32[8,1024]{1,0:T(8,128)S(1)}, u32[]{:S(2)}, u32[]{:S(2)}) collective-permute-start(f32[8,1024]{1,0:T(8,128)S(1)} %block_stats.1.refs_0_), channel_id=1, source_target_pairs={{0,16},{1,17},{2,18},{3,19},{4,20},{5,21},{6,22},{7,23},{8,24},{9,... | collective-permute-start | bytes 98312 | tf_op jit(solution)/shard_map/ppermute | solution.py:252
  12.6 2.7 %collective-permute-start.4 = (f32[8,1024]{1,0:T(8,128)S(1)}, f32[8,1024]{1,0:T(8,128)S(1)}, u32[]{:S(2)}, u32[]{:S(2)}) collective-permute-start(f32[8,1024]{1,0:T(8,128)S(1)} %block_stats.1.refs_0_), channel_id=1, source_target_pairs={{0,24},{1,25},{2,26},{3,27},{4,28},{5,29},{6,30},{7,31},{8,0},{9,1... | collective-permute-start | bytes 98312 | tf_op jit(solution)/shard_map/ppermute | solution.py:252
  15.3 15.6 %collective-permute-done.2.refs_1_ = f32[8,1024]{1,0:T(8,128)S(1)} collective-permute-done((f32[8,1024]{1,0:T(8,128)S(1)}, f32[8,1024]{1,0:T(8,128)S(1)}, u32[]{:S(2)}, u32[]{:S(2)}) %collective-permute-start.2) | collective-permute-done | bytes 32800 | tf_op jit(solution)/shard_map/ppermute | solution.py:252
  31.0 1.3 %collective-permute-start.9 = (f32[256,1024]{1,0:T(8,128)S(1)}, f32[256,1024]{1,0:T(8,128)S(1)}, u32[]{:S(2)}, u32[]{:S(2)}) collective-permute-start(f32[256,1024]{1,0:T(8,128)S(1)} %collective-permute-done.6.refs_4_), channel_id=1, source_target_pairs={{0,8},{1,9},{2,26},{3,27},{4,12},{5,13},{6,30},{7,31},{8,16},{9,17... | collective-permute-start | bytes 3145736 | tf_op jit(solution)/shard_map/ppermute | solution.py:252
  32.3 1.7 %collective-permute-start.5 = (f32[8,1024]{1,0:T(8,128)S(1)}, f32[8,1024]{1,0:T(8,128)S(1)}, u32[]{:S(2)}, u32[]{:S(2)}) collective-permute-start(f32[8,1024]{1,0:T(8,128)S(1)} %merge.2.refs_0_), channel_id=1, source_target_pairs={{0,4},{1,5},{2,6},{3,7},{4,0},{5,1},{6,2},{7,3},{8,12},{9,13},{10,... | collective-permute-start | bytes 98312 | tf_op jit(solution)/shard_map/ppermute | solution.py:252
  34.0 2.2 %collective-permute-done.5.refs_1_ = f32[8,1024]{1,0:T(8,128)S(1)} collective-permute-done((f32[8,1024]{1,0:T(8,128)S(1)}, f32[8,1024]{1,0:T(8,128)S(1)}, u32[]{:S(2)}, u32[]{:S(2)}) %collective-permute-start.5) | collective-permute-done | bytes 32800 | tf_op jit(solution)/shard_map/ppermute | solution.py:252
  36.2 1.9 %products_near.1 = (f32[256,256]{1,0:T(8,128)S(1)}, f32[256,256]{1,0:T(8,128)S(1)}, f32[256,256]{1,0:T(8,128)S(1)}, f32[256,256]{1,0:T(8,128)S(1)}) custom-call(f32[8,1024]{1,0:T(8,128)S(1)} %merge.3.mean_ref, f32[256,1024]{1,0:T(8,128)S(1)} %copy-done.1, f32[256,1024]{1,0:T(8,128)S(1)} %collective-permute-done.other_ref.refs_1_, ...), custom_call_target="tpu_custom_call" | custom-call | tf_op jit(solution)/shard_map/products_near/pallas_call | solution.py:139
  38.1 3.6 %collective-permute-start.10 = (f32[256,256]{1,0:T(8,128)S(1)}, f32[256,256]{1,0:T(8,128)S(1)}, u32[]{:S(2)}, u32[]{:S(2)}) collective-permute-start(f32[256,256]{1,0:T(8,128)S(1)} %get-tuple-element.27), channel_id=1, source_target_pairs={{0,1},{1,3},{2,2},{3,0},{4,5},{5,7},{6,6},{7,4},{8,8},{9,10},{10,1... | collective-permute-start | bytes 786440 | tf_op jit(solution)/shard_map/ppermute | solution.py:252
  41.8 3.3 %collective-permute-start.11 = (f32[256,256]{1,0:T(8,128)S(1)}, f32[256,256]{1,0:T(8,128)S(1)}, u32[]{:S(2)}, u32[]{:S(2)}) collective-permute-start(f32[256,256]{1,0:T(8,128)S(1)} %get-tuple-element.28), channel_id=1, source_target_pairs={{0,3},{1,1},{2,0},{3,2},{4,7},{5,5},{6,4},{7,6},{8,10},{9,8},{10,9... | collective-permute-start | bytes 786440 | tf_op jit(solution)/shard_map/ppermute | solution.py:252
  45.2 2.6 %collective-permute-start.13 = (f32[256,256]{1,0:T(8,128)S(1)}, f32[256,256]{1,0:T(8,128)S(1)}, u32[]{:S(2)}, u32[]{:S(2)}) collective-permute-start(f32[256,256]{1,0:T(8,128)S(1)} %get-tuple-element.30), channel_id=1, source_target_pairs={{0,7},{1,5},{2,4},{3,6},{4,3},{5,1},{6,0},{7,2},{8,14},{9,12},{10,... | collective-permute-start | bytes 786440 | tf_op jit(solution)/shard_map/ppermute | solution.py:252
  47.8 1.9 %products_level.1 = (f32[512,256]{1,0:T(8,128)S(1)}, f32[512,256]{1,0:T(8,128)S(1)}) custom-call(f32[8,1024]{1,0:T(8,128)S(1)} %merge.3.mean_ref, f32[256,1024]{1,0:T(8,128)S(1)} %copy-done.1, f32[256,1024]{1,0:T(8,128)S(1)} %collective-permute-done.other_ref.refs_1_, f32[256,1024]{1,0:T(8,128)S(1)} %collective-permute-done.7.refs_2_, ...), custom_call_target="tpu_custom_call" | custom-call | tf_op jit(solution)/shard_map/products_level/pallas_call | solution.py:139
  49.7 9.0 %collective-permute-done.9.refs_4_ = f32[256,1024]{1,0:T(8,128)S(1)} collective-permute-done((f32[256,1024]{1,0:T(8,128)S(1)}, f32[256,1024]{1,0:T(8,128)S(1)}, u32[]{:S(2)}, u32[]{:S(2)}) %collective-permute-start.9) | collective-permute-done | bytes 1048608 | tf_op jit(solution)/shard_map/ppermute | solution.py:252
  59.2 2.7 %products_across.1 = (f32[512,256]{1,0:T(8,128)S(1)}, f32[512,256]{1,0:T(8,128)S(1)}, f32[512,256]{1,0:T(8,128)S(1)}, f32[512,256]{1,0:T(8,128)S(1)}) custom-call(s32[32,16]{1,0:T(8,128)S(1)} %copy-done.2, f32[8,1024]{1,0:T(8,128)S(1)} %merge.3.mean_ref, f32[256,1024]{1,0:T(8,128)S(1)} %copy-done.1, f32[256,1024]{1,0:T(8,128)S(1)} %collective-permute-done.other_ref.refs_1_, ...), custom_call_target="tpu_custom_call" | custom-call | tf_op jit(solution)/shard_map/products_across/pallas_call | solution.py:139
  61.9 1.2 %collective-permute-start.19 = (f32[512,256]{1,0:T(8,128)S(1)}, f32[512,256]{1,0:T(8,128)S(1)}, u32[]{:S(2)}, u32[]{:S(2)}) collective-permute-start(f32[512,256]{1,0:T(8,128)S(1)} %get-tuple-element.40), channel_id=1, source_target_pairs={{0,1},{1,0},{2,3},{3,2},{4,5},{5,4},{6,7},{7,6},{8,9},{9,8},{10,11... | collective-permute-start | bytes 1572872 | tf_op jit(solution)/shard_map/ppermute | solution.py:252
  63.1 1.5 %collective-permute-start.20 = (f32[512,256]{1,0:T(8,128)S(1)}, f32[512,256]{1,0:T(8,128)S(1)}, u32[]{:S(2)}, u32[]{:S(2)}) collective-permute-start(f32[512,256]{1,0:T(8,128)S(1)} %get-tuple-element.42), channel_id=1, source_target_pairs={{0,4},{1,5},{2,6},{3,7},{4,0},{5,1},{6,2},{7,3},{8,12},{9,13},{10,... | collective-permute-start | bytes 1572872 | tf_op jit(solution)/shard_map/ppermute | solution.py:252
  64.6 0.9 collective-permute-start.21
  65.5 18.5 %collective-permute-done.14.refs_4_ = f32[256,1024]{1,0:T(8,128)S(1)} collective-permute-done((f32[256,1024]{1,0:T(8,128)S(1)}, f32[256,1024]{1,0:T(8,128)S(1)}, u32[]{:S(2)}, u32[]{:S(2)}) %collective-permute-start.14) | collective-permute-done | bytes 1048608 | tf_op jit(solution)/shard_map/ppermute | solution.py:252
  84.0 2.7 %products_far.1 = (f32[256,256]{1,0:T(8,128)S(1)}, f32[256,256]{1,0:T(8,128)}, f32[256,256]{1,0:T(8,128)}, f32[256,256]{1,0:T(8,128)}) custom-call(f32[8,1024]{1,0:T(8,128)S(1)} %merge.3.mean_ref, f32[256,1024]{1,0:T(8,128)S(1)} %copy-done.1, f32[256,1024]{1,0:T(8,128)S(1)} %collective-permute-done.other_ref.refs_1_, ...), custom_call_target="tpu_custom_call" | custom-call | tf_op jit(solution)/shard_map/products_far/pallas_call | solution.py:139
  87.4 3.5 %collective-permute-start.16 = (f32[256,256]{1,0:T(8,128)}, f32[256,256]{1,0:T(8,128)}, u32[]{:S(2)}, u32[]{:S(2)}) collective-permute-start(f32[256,256]{1,0:T(8,128)} %get-tuple-element.36), channel_id=1, source_target_pairs={{0,2},{1,0},{2,1},{3,3},{4,6},{5,4},{6,5},{7,7},{8,11},{9,9},{10,8... | collective-permute-start | bytes 786440 | tf_op jit(solution)/shard_map/ppermute | solution.py:252
  90.9 1.6 %collective-permute-start.17 = (f32[256,256]{1,0:T(8,128)}, f32[256,256]{1,0:T(8,128)}, u32[]{:S(2)}, u32[]{:S(2)}) collective-permute-start(f32[256,256]{1,0:T(8,128)} %get-tuple-element.37), channel_id=1, source_target_pairs={{0,4},{1,6},{2,7},{3,5},{4,0},{5,2},{6,3},{7,1},{8,13},{9,15},{10,... | collective-permute-start | bytes 786440 | tf_op jit(solution)/shard_map/ppermute | solution.py:252
  92.5 2.3 %collective-permute-start.18 = (f32[256,256]{1,0:T(8,128)}, f32[256,256]{1,0:T(8,128)}, u32[]{:S(2)}, u32[]{:S(2)}) collective-permute-start(f32[256,256]{1,0:T(8,128)} %get-tuple-element.38), channel_id=1, source_target_pairs={{0,6},{1,4},{2,5},{3,7},{4,2},{5,0},{6,1},{7,3},{8,15},{9,13},{10,... | collective-permute-start | bytes 786440 | tf_op jit(solution)/shard_map/ppermute | solution.py:252
  94.8 0.9 sum_across.1
  96.3 1.8 %place_most.1.refs_6_ = f32[256,2048]{1,0:T(8,128)} custom-call(s32[32,16]{1,0:T(8,128)S(1)} %copy-done.2, f32[256,256]{1,0:T(8,128)S(1)} %collective-permute-done.10.refs_0_, f32[256,256]{1,0:T(8,128)S(1)} %collective-permute-done.11.refs_1_, f32[256,256]{1,0:T(8,128)S(1)} %collective-permute-done.12.refs_2_, ...), custom_call_target="tpu_custom_call" | custom-call | tf_op jit(solution)/shard_map/place_most/pallas_call | solution.py:181
  98.9 8.4 %collective-permute-done.18.refs_3_ = f32[256,256]{1,0:T(8,128)} collective-permute-done((f32[256,256]{1,0:T(8,128)}, f32[256,256]{1,0:T(8,128)}, u32[]{:S(2)}, u32[]{:S(2)}) %collective-permute-start.18) | collective-permute-done | bytes 262176 | tf_op jit(solution)/shard_map/ppermute | solution.py:252
  107.3 2.3 %place_last.1 = f32[256,2048]{1,0:T(8,128)} custom-call(s32[32,16]{1,0:T(8,128)S(1)} %copy-done.2, f32[256,256]{1,0:T(8,128)S(1)} %collective-permute-done.15.refs_0_, f32[256,256]{1,0:T(8,128)} %collective-permute-done.16.refs_1_, f32[256,256]{1,0:T(8,128)} %collective-permute-done.17.refs_2_, ...), custom_call_target="tpu_custom_call", output_to_operand_aliasing={{}: (7, {})} | custom-call | tf_op jit(solution)/shard_map/place_last/pallas_call | solution.py:181
  (35 shorter events, 3.3 us)
Async XLA Ops:
  0.6 7.6 %collective-permute-start = (f32[256,1024]{1,0:T(8,128)}, f32[256,1024]{1,0:T(8,128)S(1)}, u32[]{:S(2)}, u32[]{:S(2)}) collective-permute-start(f32[256,1024]{1,0:T(8,128)} %refs_0_.7), channel_id=1, source_target_pairs={{0,2},{1,3},{2,0},{3,1},{4,6},{5,7},{6,4},{7,5},{8,10},{9,11},{10,... | collective-permute-start | bytes 3145736 | tf_op jit(solution)/shard_map/ppermute | solution.py:252
  1.1 29.7 %collective-permute-start.6 = (f32[256,1024]{1,0:T(8,128)}, f32[256,1024]{1,0:T(8,128)S(1)}, u32[]{:S(2)}, u32[]{:S(2)}) collective-permute-start(f32[256,1024]{1,0:T(8,128)} %refs_0_.7), channel_id=1, source_target_pairs={{0,8},{1,9},{2,26},{3,27},{4,12},{5,13},{6,30},{7,31},{8,16},{9,17... | collective-permute-start | bytes 3145736 | tf_op jit(solution)/shard_map/ppermute | solution.py:252
  3.8 27.1 %collective-permute-start.7 = (f32[256,1024]{1,0:T(8,128)}, f32[256,1024]{1,0:T(8,128)S(1)}, u32[]{:S(2)}, u32[]{:S(2)}) collective-permute-start(f32[256,1024]{1,0:T(8,128)} %refs_0_.7), channel_id=1, source_target_pairs={{0,4},{1,5},{2,6},{3,7},{4,0},{5,1},{6,2},{7,3},{8,12},{9,13},{10,... | collective-permute-start | bytes 3145736 | tf_op jit(solution)/shard_map/ppermute | solution.py:252
  5.3 2.9 %collective-permute-start.1 = (f32[1,256]{1,0:T(1,128)}, f32[1,256]{1,0:T(1,128)S(1)}, u32[]{:S(2)}, u32[]{:S(2)}) collective-permute-start(f32[1,256]{1,0:T(1,128)} %bitcast.3), channel_id=1, source_target_pairs={{0,2},{1,3},{2,0},{3,1},{4,6},{5,7},{6,4},{7,5},{8,10},{9,11},{10,... | collective-permute-start | bytes 3080 | tf_op jit(solution)/shard_map/ppermute | solution.py:252
  8.2 1.2 %copy-start = (f32[256,1024]{1,0:T(8,128)S(1)}, f32[256,1024]{1,0:T(8,128)}, u32[]{:S(2)}) copy-start(f32[256,1024]{1,0:T(8,128)} %refs_0_.7) | copy-start | bytes 3145732
  9.4 0.7 copy-start.3
  10.1 26.1 %copy-start.1 = (f32[256,1024]{1,0:T(8,128)S(1)}, f32[256,1024]{1,0:T(8,128)}, u32[]{:S(2)}) copy-start(f32[256,1024]{1,0:T(8,128)} %refs_0_.7) | copy-start | bytes 3145732
  11.3 19.5 %collective-permute-start.2 = (f32[8,1024]{1,0:T(8,128)S(1)}, f32[8,1024]{1,0:T(8,128)S(1)}, u32[]{:S(2)}, u32[]{:S(2)}) collective-permute-start(f32[8,1024]{1,0:T(8,128)S(1)} %block_stats.1.refs_0_), channel_id=1, source_target_pairs={{0,8},{1,9},{2,10},{3,11},{4,12},{5,13},{6,14},{7,15},{8,16},{9,17... | collective-permute-start | bytes 98312 | tf_op jit(solution)/shard_map/ppermute | solution.py:252
  11.3 19.5 %collective-permute-start.3 = (f32[8,1024]{1,0:T(8,128)S(1)}, f32[8,1024]{1,0:T(8,128)S(1)}, u32[]{:S(2)}, u32[]{:S(2)}) collective-permute-start(f32[8,1024]{1,0:T(8,128)S(1)} %block_stats.1.refs_0_), channel_id=1, source_target_pairs={{0,16},{1,17},{2,18},{3,19},{4,20},{5,21},{6,22},{7,23},{8,24},{9,... | collective-permute-start | bytes 98312 | tf_op jit(solution)/shard_map/ppermute | solution.py:252
  12.6 18.3 %collective-permute-start.4 = (f32[8,1024]{1,0:T(8,128)S(1)}, f32[8,1024]{1,0:T(8,128)S(1)}, u32[]{:S(2)}, u32[]{:S(2)}) collective-permute-start(f32[8,1024]{1,0:T(8,128)S(1)} %block_stats.1.refs_0_), channel_id=1, source_target_pairs={{0,24},{1,25},{2,26},{3,27},{4,28},{5,29},{6,30},{7,31},{8,0},{9,1... | collective-permute-start | bytes 98312 | tf_op jit(solution)/shard_map/ppermute | solution.py:252
  30.9 5.3 %collective-permute-start.8 = (f32[256,1024]{1,0:T(8,128)S(1)}, f32[256,1024]{1,0:T(8,128)S(1)}, u32[]{:S(2)}, u32[]{:S(2)}) collective-permute-start(f32[256,1024]{1,0:T(8,128)S(1)} %collective-permute-done.7.refs_2_), channel_id=1, source_target_pairs={{0,2},{1,3},{2,0},{3,1},{4,6},{5,7},{6,4},{7,5},{8,10},{9,11},{10,... | collective-permute-start | bytes 3145736 | tf_op jit(solution)/shard_map/ppermute | solution.py:252
  31.0 27.7 %collective-permute-start.9 = (f32[256,1024]{1,0:T(8,128)S(1)}, f32[256,1024]{1,0:T(8,128)S(1)}, u32[]{:S(2)}, u32[]{:S(2)}) collective-permute-start(f32[256,1024]{1,0:T(8,128)S(1)} %collective-permute-done.6.refs_4_), channel_id=1, source_target_pairs={{0,8},{1,9},{2,26},{3,27},{4,12},{5,13},{6,30},{7,31},{8,16},{9,17... | collective-permute-start | bytes 3145736 | tf_op jit(solution)/shard_map/ppermute | solution.py:252
  32.3 3.9 %collective-permute-start.5 = (f32[8,1024]{1,0:T(8,128)S(1)}, f32[8,1024]{1,0:T(8,128)S(1)}, u32[]{:S(2)}, u32[]{:S(2)}) collective-permute-start(f32[8,1024]{1,0:T(8,128)S(1)} %merge.2.refs_0_), channel_id=1, source_target_pairs={{0,4},{1,5},{2,6},{3,7},{4,0},{5,1},{6,2},{7,3},{8,12},{9,13},{10,... | collective-permute-start | bytes 98312 | tf_op jit(solution)/shard_map/ppermute | solution.py:252
  38.1 20.6 %collective-permute-start.10 = (f32[256,256]{1,0:T(8,128)S(1)}, f32[256,256]{1,0:T(8,128)S(1)}, u32[]{:S(2)}, u32[]{:S(2)}) collective-permute-start(f32[256,256]{1,0:T(8,128)S(1)} %get-tuple-element.27), channel_id=1, source_target_pairs={{0,1},{1,3},{2,2},{3,0},{4,5},{5,7},{6,6},{7,4},{8,8},{9,10},{10,1... | collective-permute-start | bytes 786440 | tf_op jit(solution)/shard_map/ppermute | solution.py:252
  41.8 16.9 %collective-permute-start.11 = (f32[256,256]{1,0:T(8,128)S(1)}, f32[256,256]{1,0:T(8,128)S(1)}, u32[]{:S(2)}, u32[]{:S(2)}) collective-permute-start(f32[256,256]{1,0:T(8,128)S(1)} %get-tuple-element.28), channel_id=1, source_target_pairs={{0,3},{1,1},{2,0},{3,2},{4,7},{5,5},{6,4},{7,6},{8,10},{9,8},{10,9... | collective-permute-start | bytes 786440 | tf_op jit(solution)/shard_map/ppermute | solution.py:252
  45.1 13.6 %collective-permute-start.12 = (f32[256,256]{1,0:T(8,128)S(1)}, f32[256,256]{1,0:T(8,128)S(1)}, u32[]{:S(2)}, u32[]{:S(2)}) collective-permute-start(f32[256,256]{1,0:T(8,128)S(1)} %get-tuple-element.29), channel_id=1, source_target_pairs={{0,5},{1,7},{2,6},{3,4},{4,1},{5,3},{6,2},{7,0},{8,12},{9,14},{10,... | collective-permute-start | bytes 786440 | tf_op jit(solution)/shard_map/ppermute | solution.py:252
  45.2 14.0 %copy-start.2 = (s32[32,16]{1,0:T(8,128)S(1)}, s32[32,16]{1,0:T(8,128)}, u32[]{:S(2)}) copy-start(s32[32,16]{1,0:T(8,128)} %constant.19.clone.table_ref) | copy-start | bytes 6148
  45.2 13.5 %collective-permute-start.13 = (f32[256,256]{1,0:T(8,128)S(1)}, f32[256,256]{1,0:T(8,128)S(1)}, u32[]{:S(2)}, u32[]{:S(2)}) collective-permute-start(f32[256,256]{1,0:T(8,128)S(1)} %get-tuple-element.30), channel_id=1, source_target_pairs={{0,7},{1,5},{2,4},{3,6},{4,3},{5,1},{6,0},{7,2},{8,14},{9,12},{10,... | collective-permute-start | bytes 786440 | tf_op jit(solution)/shard_map/ppermute | solution.py:252
  58.7 25.3 %collective-permute-start.14 = (f32[256,1024]{1,0:T(8,128)S(1)}, f32[256,1024]{1,0:T(8,128)S(1)}, u32[]{:S(2)}, u32[]{:S(2)}) collective-permute-start(f32[256,1024]{1,0:T(8,128)S(1)} %collective-permute-done.9.refs_4_), channel_id=1, source_target_pairs={{0,8},{1,9},{2,26},{3,27},{4,12},{5,13},{6,30},{7,31},{8,16},{9,17... | collective-permute-start | bytes 3145736 | tf_op jit(solution)/shard_map/ppermute | solution.py:252
  61.9 25.5 %collective-permute-start.19 = (f32[512,256]{1,0:T(8,128)S(1)}, f32[512,256]{1,0:T(8,128)S(1)}, u32[]{:S(2)}, u32[]{:S(2)}) collective-permute-start(f32[512,256]{1,0:T(8,128)S(1)} %get-tuple-element.40), channel_id=1, source_target_pairs={{0,1},{1,0},{2,3},{3,2},{4,5},{5,4},{6,7},{7,6},{8,9},{9,8},{10,11... | collective-permute-start | bytes 1572872 | tf_op jit(solution)/shard_map/ppermute | solution.py:252
  63.1 29.4 %collective-permute-start.20 = (f32[512,256]{1,0:T(8,128)S(1)}, f32[512,256]{1,0:T(8,128)S(1)}, u32[]{:S(2)}, u32[]{:S(2)}) collective-permute-start(f32[512,256]{1,0:T(8,128)S(1)} %get-tuple-element.42), channel_id=1, source_target_pairs={{0,4},{1,5},{2,6},{3,7},{4,0},{5,1},{6,2},{7,3},{8,12},{9,13},{10,... | collective-permute-start | bytes 1572872 | tf_op jit(solution)/shard_map/ppermute | solution.py:252
  64.6 30.2 %collective-permute-start.21 = (f32[512,256]{1,0:T(8,128)S(1)}, f32[512,256]{1,0:T(8,128)S(1)}, u32[]{:S(2)}, u32[]{:S(2)}) collective-permute-start(f32[512,256]{1,0:T(8,128)S(1)} %get-tuple-element.43), channel_id=1, source_target_pairs={{0,5},{1,4},{2,7},{3,6},{4,1},{5,0},{6,3},{7,2},{8,13},{9,12},{10,... | collective-permute-start | bytes 1572872 | tf_op jit(solution)/shard_map/ppermute | solution.py:252
  86.7 9.5 %collective-permute-start.15 = (f32[256,256]{1,0:T(8,128)S(1)}, f32[256,256]{1,0:T(8,128)S(1)}, u32[]{:S(2)}, u32[]{:S(2)}) collective-permute-start(f32[256,256]{1,0:T(8,128)S(1)} %get-tuple-element.35), channel_id=1, source_target_pairs={{0,0},{1,2},{2,3},{3,1},{4,4},{5,6},{6,7},{7,5},{8,9},{9,11},{10,1... | collective-permute-start | bytes 786440 | tf_op jit(solution)/shard_map/ppermute | solution.py:252
  87.4 11.3 %collective-permute-start.16 = (f32[256,256]{1,0:T(8,128)}, f32[256,256]{1,0:T(8,128)}, u32[]{:S(2)}, u32[]{:S(2)}) collective-permute-start(f32[256,256]{1,0:T(8,128)} %get-tuple-element.36), channel_id=1, source_target_pairs={{0,2},{1,0},{2,1},{3,3},{4,6},{5,4},{6,5},{7,7},{8,11},{9,9},{10,8... | collective-permute-start | bytes 786440 | tf_op jit(solution)/shard_map/ppermute | solution.py:252
  90.9 8.0 %collective-permute-start.17 = (f32[256,256]{1,0:T(8,128)}, f32[256,256]{1,0:T(8,128)}, u32[]{:S(2)}, u32[]{:S(2)}) collective-permute-start(f32[256,256]{1,0:T(8,128)} %get-tuple-element.37), channel_id=1, source_target_pairs={{0,4},{1,6},{2,7},{3,5},{4,0},{5,2},{6,3},{7,1},{8,13},{9,15},{10,... | collective-permute-start | bytes 786440 | tf_op jit(solution)/shard_map/ppermute | solution.py:252
  92.5 14.8 %collective-permute-start.18 = (f32[256,256]{1,0:T(8,128)}, f32[256,256]{1,0:T(8,128)}, u32[]{:S(2)}, u32[]{:S(2)}) collective-permute-start(f32[256,256]{1,0:T(8,128)} %get-tuple-element.38), channel_id=1, source_target_pairs={{0,6},{1,4},{2,5},{3,7},{4,2},{5,0},{6,1},{7,3},{8,15},{9,13},{10,... | collective-permute-start | bytes 786440 | tf_op jit(solution)/shard_map/ppermute | solution.py:252
  95.7 11.6 %collective-permute-start.22 = (f32[256,256]{1,0:T(8,128)}, f32[256,256]{1,0:T(8,128)}, u32[]{:S(2)}, u32[]{:S(2)}) collective-permute-start(f32[256,256]{1,0:T(8,128)} %get-tuple-element.44), channel_id=1, source_target_pairs={{0,2},{1,3},{2,0},{3,1},{4,6},{5,7},{6,4},{7,5},{8,10},{9,11},{10,... | collective-permute-start | bytes 786440 | tf_op jit(solution)/shard_map/ppermute | solution.py:252
  96.2 11.1 %collective-permute-start.23 = (f32[256,256]{1,0:T(8,128)}, f32[256,256]{1,0:T(8,128)}, u32[]{:S(2)}, u32[]{:S(2)}) collective-permute-start(f32[256,256]{1,0:T(8,128)} %get-tuple-element.45), channel_id=1, source_target_pairs={{0,2},{1,3},{2,0},{3,1},{4,6},{5,7},{6,4},{7,5},{8,10},{9,11},{10,... | collective-permute-start | bytes 786440 | tf_op jit(solution)/shard_map/ppermute | solution.py:252

commit v4 on v3

--- a/solution.py
+++ b/solution.py
@@ -99,11 +99,11 @@
     mean = mean_ref[0:1, :]
     high, low = split(block[...] - mean)
     straight = lax.axis_index("par") == 0
-    for side in range(2):
+    for k, side in enumerate((1, 0)):
         same = product_of(rows[2 * side], mean, high, low, scale)
         other = product_of(rows[2 * side + 1], mean, high, low, scale)
-        outs[2 * side][...] = jnp.where(straight, same, other)
-        outs[2 * side + 1][...] = jnp.where(straight, other, same)
+        outs[2 * k][...] = jnp.where(straight, same, other)
+        outs[2 * k + 1][...] = jnp.where(straight, other, same)
 
 
 def own_level_kernel(scale, mean_ref, *refs):
@@ -269,8 +269,8 @@
 
     def one_level(block, step, name):
         out = kernel_call(functools.partial(one_level_kernel, scale), [(rows, rows)] * 4, name, stats, *all_rows, block)
-        sent = [send(out[2 * side + swap], to_holder(step, side, swap)) for side in range(2) for swap in range(2)]
-        return out, (sent[:2], sent[2:])
+        sent = [[send(out[2 * k + swap], to_holder(step, 1 - k, swap)) for swap in range(2)] for k in range(2)]
+        return out, sent[::-1]
 
     out, near = one_level(one, 1, "products_near")
     share = params // lax.axis_size("smp")
@@ -283,7 +283,7 @@
         *all_rows,
         after(log_derivs, out[0]),
     )
-    two = after(two, *near[0], *near[1], *own_level)
+    two = after(two, *near[1], *near[0], *own_level)
     three = send(two, ring)
     keep_own, keep_side, sent_own, sent_side = kernel_call(
         functools.partial(across_level_kernel, scale, planes, 0),
@@ -315,11 +315,11 @@
         None,
         "place_most",
     )
-    gram = after(gram, *far[0], *far[1])
+    gram = after(gram, *far[1], *far[0])
     gram = place(
         table,
         planes,
-        [(far[0], [(3, 0)]), (far[1], [(4, 0)]), ((across_own,), [(7, 0)]), ((across_side,), [(8, 0)])],
+        [(far[1], [(4, 0)]), (far[0], [(3, 0)]), ((across_own,), [(7, 0)]), ((across_side,), [(8, 0)])],
         shape,
         gram,
         "place_last",

time: 110 us -> 106 us (0.964)
  waiting for transfers between devices: 55 us -> 52 us
    ppermute x24, waiting for transfers between devices: 55 us -> 52 us  [send(): return lax.ppermute(value, BOTH, pairs)]
  transfers between devices with their start and end apart: 24 -> 24, of which waited for: 7 -> 8; matrix products, arithmetic and copies ran while one was open for 1% -> 1% of each run, Pallas kernels for 12% -> 12%
where the time goes in v4:
time: 106 us
  waiting for transfers between devices  52 us (49%)
  starting transfers between devices  35.2 us (33%)
  Pallas kernels  15.4 us (15%)
  local copies, waits for them, and re-layouts  1.91 us (2%)
    ppermute x24, waiting for transfers between devices, send(): return lax.ppermute(value, BOTH, pairs)  52 us
    ppermute x24, starting transfers between devices, send(): return lax.ppermute(value, BOTH, pairs)  35.2 us
    pallas_call x8, Pallas kernels, kernel_call(): pl.pallas_call(kernel, out_shape=[jax.ShapeDtypeStruct(s, jnp.float32) fo...  11.3 us
    pallas_call x2, Pallas kernels, place(): pl.pallas_call(functools.partial(place_kernel, planes, [len(terms) for te...  4.12 us
  transfers between devices with their start and end apart: 24, of which 8 were waited for; matrix products, arithmetic and copies ran while one was open for 1% of the time, Pallas kernels for 12%

profile of v4, /device:TPU:0, one launch (start us, length us, event | category | flops | bytes accessed | tf_op | source)
XLA Modules:
  0.0 106.0 jit_solution(14087429977606259789)
XLA Ops:
  1.1 2.6 %collective-permute-start.6 = (f32[256,1024]{1,0:T(8,128)}, f32[256,1024]{1,0:T(8,128)S(1)}, u32[]{:S(2)}, u32[]{:S(2)}) collective-permute-start(f32[256,1024]{1,0:T(8,128)} %refs_0_.7), channel_id=1, source_target_pairs={{0,8},{1,9},{2,26},{3,27},{4,12},{5,13},{6,30},{7,31},{8,16},{9,17... | collective-permute-start | bytes 3145736 | tf_op jit(solution)/shard_map/ppermute | solution.py:252
  3.8 1.5 %collective-permute-start.7 = (f32[256,1024]{1,0:T(8,128)}, f32[256,1024]{1,0:T(8,128)S(1)}, u32[]{:S(2)}, u32[]{:S(2)}) collective-permute-start(f32[256,1024]{1,0:T(8,128)} %refs_0_.7), channel_id=1, source_target_pairs={{0,4},{1,5},{2,6},{3,7},{4,0},{5,1},{6,2},{7,3},{8,12},{9,13},{10,... | collective-permute-start | bytes 3145736 | tf_op jit(solution)/shard_map/ppermute | solution.py:252
  5.3 1.9 %collective-permute-start.1 = (f32[1,256]{1,0:T(1,128)}, f32[1,256]{1,0:T(1,128)S(1)}, u32[]{:S(2)}, u32[]{:S(2)}) collective-permute-start(f32[1,256]{1,0:T(1,128)} %bitcast.3), channel_id=1, source_target_pairs={{0,2},{1,3},{2,0},{3,1},{4,6},{5,7},{6,4},{7,5},{8,10},{9,11},{10,... | collective-permute-start | bytes 3080 | tf_op jit(solution)/shard_map/ppermute | solution.py:252
  7.2 1.0 collective-permute-done.1.other_coef_ref
  8.2 1.2 %copy-done = f32[256,1024]{1,0:T(8,128)S(1)} copy-done((f32[256,1024]{1,0:T(8,128)S(1)}, f32[256,1024]{1,0:T(8,128)}, u32[]{:S(2)}) %copy-start) | copy-done | bytes 1048600
  10.1 1.2 %block_stats.1.refs_0_ = f32[8,1024]{1,0:T(8,128)S(1)} custom-call(f32[256,1024]{1,0:T(8,128)S(1)} %copy-done, f32[256,1024]{1,0:T(8,128)S(1)} %collective-permute-done.other_ref.refs_1_, f32[1,256]{1,0:T(1,128)S(1)} %bitcast.4, f32[1,256]{1,0:T(1,128)S(1)} %collective-permute-done.1.other_coef_ref), custom_call_target="tpu_custom_call" | custom-call | tf_op jit(solution)/shard_map/block_stats/pallas_call | solution.py:139
  11.3 1.3 %collective-permute-start.3 = (f32[8,1024]{1,0:T(8,128)S(1)}, f32[8,1024]{1,0:T(8,128)S(1)}, u32[]{:S(2)}, u32[]{:S(2)}) collective-permute-start(f32[8,1024]{1,0:T(8,128)S(1)} %block_stats.1.refs_0_), channel_id=1, source_target_pairs={{0,16},{1,17},{2,18},{3,19},{4,20},{5,21},{6,22},{7,23},{8,24},{9,... | collective-permute-start | bytes 98312 | tf_op jit(solution)/shard_map/ppermute | solution.py:252
  12.6 2.7 %collective-permute-start.4 = (f32[8,1024]{1,0:T(8,128)S(1)}, f32[8,1024]{1,0:T(8,128)S(1)}, u32[]{:S(2)}, u32[]{:S(2)}) collective-permute-start(f32[8,1024]{1,0:T(8,128)S(1)} %block_stats.1.refs_0_), channel_id=1, source_target_pairs={{0,24},{1,25},{2,26},{3,27},{4,28},{5,29},{6,30},{7,31},{8,0},{9,1... | collective-permute-start | bytes 98312 | tf_op jit(solution)/shard_map/ppermute | solution.py:252
  15.3 15.6 %collective-permute-done.2.refs_1_ = f32[8,1024]{1,0:T(8,128)S(1)} collective-permute-done((f32[8,1024]{1,0:T(8,128)S(1)}, f32[8,1024]{1,0:T(8,128)S(1)}, u32[]{:S(2)}, u32[]{:S(2)}) %collective-permute-start.2) | collective-permute-done | bytes 32800 | tf_op jit(solution)/shard_map/ppermute | solution.py:252
  31.0 1.3 %collective-permute-start.9 = (f32[256,1024]{1,0:T(8,128)S(1)}, f32[256,1024]{1,0:T(8,128)S(1)}, u32[]{:S(2)}, u32[]{:S(2)}) collective-permute-start(f32[256,1024]{1,0:T(8,128)S(1)} %collective-permute-done.6.refs_4_), channel_id=1, source_target_pairs={{0,8},{1,9},{2,26},{3,27},{4,12},{5,13},{6,30},{7,31},{8,16},{9,17... | collective-permute-start | bytes 3145736 | tf_op jit(solution)/shard_map/ppermute | solution.py:252
  32.3 1.7 %collective-permute-start.5 = (f32[8,1024]{1,0:T(8,128)S(1)}, f32[8,1024]{1,0:T(8,128)S(1)}, u32[]{:S(2)}, u32[]{:S(2)}) collective-permute-start(f32[8,1024]{1,0:T(8,128)S(1)} %merge.2.refs_0_), channel_id=1, source_target_pairs={{0,4},{1,5},{2,6},{3,7},{4,0},{5,1},{6,2},{7,3},{8,12},{9,13},{10,... | collective-permute-start | bytes 98312 | tf_op jit(solution)/shard_map/ppermute | solution.py:252
  34.0 2.2 %collective-permute-done.5.refs_1_ = f32[8,1024]{1,0:T(8,128)S(1)} collective-permute-done((f32[8,1024]{1,0:T(8,128)S(1)}, f32[8,1024]{1,0:T(8,128)S(1)}, u32[]{:S(2)}, u32[]{:S(2)}) %collective-permute-start.5) | collective-permute-done | bytes 32800 | tf_op jit(solution)/shard_map/ppermute | solution.py:252
  36.2 1.9 %products_near.1 = (f32[256,256]{1,0:T(8,128)S(1)}, f32[256,256]{1,0:T(8,128)S(1)}, f32[256,256]{1,0:T(8,128)S(1)}, f32[256,256]{1,0:T(8,128)S(1)}) custom-call(f32[8,1024]{1,0:T(8,128)S(1)} %merge.3.mean_ref, f32[256,1024]{1,0:T(8,128)S(1)} %copy-done.1, f32[256,1024]{1,0:T(8,128)S(1)} %collective-permute-done.other_ref.refs_1_, ...), custom_call_target="tpu_custom_call" | custom-call | tf_op jit(solution)/shard_map/products_near/pallas_call | solution.py:139
  38.1 2.7 %collective-permute-start.10 = (f32[256,256]{1,0:T(8,128)S(1)}, f32[256,256]{1,0:T(8,128)S(1)}, u32[]{:S(2)}, u32[]{:S(2)}) collective-permute-start(f32[256,256]{1,0:T(8,128)S(1)} %get-tuple-element.27), channel_id=1, source_target_pairs={{0,5},{1,7},{2,6},{3,4},{4,1},{5,3},{6,2},{7,0},{8,12},{9,14},{10,... | collective-permute-start | bytes 786440 | tf_op jit(solution)/shard_map/ppermute | solution.py:252
  40.8 1.4 %collective-permute-start.11 = (f32[256,256]{1,0:T(8,128)S(1)}, f32[256,256]{1,0:T(8,128)S(1)}, u32[]{:S(2)}, u32[]{:S(2)}) collective-permute-start(f32[256,256]{1,0:T(8,128)S(1)} %get-tuple-element.28), channel_id=1, source_target_pairs={{0,7},{1,5},{2,4},{3,6},{4,3},{5,1},{6,0},{7,2},{8,14},{9,12},{10,... | collective-permute-start | bytes 786440 | tf_op jit(solution)/shard_map/ppermute | solution.py:252
  42.3 2.9 %collective-permute-start.12 = (f32[256,256]{1,0:T(8,128)S(1)}, f32[256,256]{1,0:T(8,128)S(1)}, u32[]{:S(2)}, u32[]{:S(2)}) collective-permute-start(f32[256,256]{1,0:T(8,128)S(1)} %get-tuple-element.29), channel_id=1, source_target_pairs={{0,1},{1,3},{2,2},{3,0},{4,5},{5,7},{6,6},{7,4},{8,8},{9,10},{10,1... | collective-permute-start | bytes 786440 | tf_op jit(solution)/shard_map/ppermute | solution.py:252
  45.2 2.6 %collective-permute-start.13 = (f32[256,256]{1,0:T(8,128)S(1)}, f32[256,256]{1,0:T(8,128)S(1)}, u32[]{:S(2)}, u32[]{:S(2)}) collective-permute-start(f32[256,256]{1,0:T(8,128)S(1)} %get-tuple-element.30), channel_id=1, source_target_pairs={{0,3},{1,1},{2,0},{3,2},{4,7},{5,5},{6,4},{7,6},{8,10},{9,8},{10,9... | collective-permute-start | bytes 786440 | tf_op jit(solution)/shard_map/ppermute | solution.py:252
  47.9 1.9 %products_level.1 = (f32[512,256]{1,0:T(8,128)S(1)}, f32[512,256]{1,0:T(8,128)S(1)}) custom-call(f32[8,1024]{1,0:T(8,128)S(1)} %merge.3.mean_ref, f32[256,1024]{1,0:T(8,128)S(1)} %copy-done.1, f32[256,1024]{1,0:T(8,128)S(1)} %collective-permute-done.other_ref.refs_1_, f32[256,1024]{1,0:T(8,128)S(1)} %collective-permute-done.7.refs_2_, ...), custom_call_target="tpu_custom_call" | custom-call | tf_op jit(solution)/shard_map/products_level/pallas_call | solution.py:139
  49.8 8.9 %collective-permute-done.9.refs_4_ = f32[256,1024]{1,0:T(8,128)S(1)} collective-permute-done((f32[256,1024]{1,0:T(8,128)S(1)}, f32[256,1024]{1,0:T(8,128)S(1)}, u32[]{:S(2)}, u32[]{:S(2)}) %collective-permute-start.9) | collective-permute-done | bytes 1048608 | tf_op jit(solution)/shard_map/ppermute | solution.py:252
  58.8 2.7 %products_across.1 = (f32[512,256]{1,0:T(8,128)S(1)}, f32[512,256]{1,0:T(8,128)S(1)}, f32[512,256]{1,0:T(8,128)S(1)}, f32[512,256]{1,0:T(8,128)S(1)}) custom-call(s32[32,16]{1,0:T(8,128)S(1)} %copy-done.2, f32[8,1024]{1,0:T(8,128)S(1)} %merge.3.mean_ref, f32[256,1024]{1,0:T(8,128)S(1)} %copy-done.1, f32[256,1024]{1,0:T(8,128)S(1)} %collective-permute-done.other_ref.refs_1_, ...), custom_call_target="tpu_custom_call" | custom-call | tf_op jit(solution)/shard_map/products_across/pallas_call | solution.py:139
  61.5 1.6 %collective-permute-start.19 = (f32[512,256]{1,0:T(8,128)S(1)}, f32[512,256]{1,0:T(8,128)S(1)}, u32[]{:S(2)}, u32[]{:S(2)}) collective-permute-start(f32[512,256]{1,0:T(8,128)S(1)} %get-tuple-element.40), channel_id=1, source_target_pairs={{0,1},{1,0},{2,3},{3,2},{4,5},{5,4},{6,7},{7,6},{8,9},{9,8},{10,11... | collective-permute-start | bytes 1572872 | tf_op jit(solution)/shard_map/ppermute | solution.py:252
  63.1 1.5 %collective-permute-start.20 = (f32[512,256]{1,0:T(8,128)S(1)}, f32[512,256]{1,0:T(8,128)S(1)}, u32[]{:S(2)}, u32[]{:S(2)}) collective-permute-start(f32[512,256]{1,0:T(8,128)S(1)} %get-tuple-element.42), channel_id=1, source_target_pairs={{0,4},{1,5},{2,6},{3,7},{4,0},{5,1},{6,2},{7,3},{8,12},{9,13},{10,... | collective-permute-start | bytes 1572872 | tf_op jit(solution)/shard_map/ppermute | solution.py:252
  65.1 18.6 %collective-permute-done.14.refs_4_ = f32[256,1024]{1,0:T(8,128)S(1)} collective-permute-done((f32[256,1024]{1,0:T(8,128)S(1)}, f32[256,1024]{1,0:T(8,128)S(1)}, u32[]{:S(2)}, u32[]{:S(2)}) %collective-permute-start.14) | collective-permute-done | bytes 1048608 | tf_op jit(solution)/shard_map/ppermute | solution.py:252
  83.7 2.7 %products_far.1 = (f32[256,256]{1,0:T(8,128)S(1)}, f32[256,256]{1,0:T(8,128)}, f32[256,256]{1,0:T(8,128)}, f32[256,256]{1,0:T(8,128)}) custom-call(f32[8,1024]{1,0:T(8,128)S(1)} %merge.3.mean_ref, f32[256,1024]{1,0:T(8,128)S(1)} %copy-done.1, f32[256,1024]{1,0:T(8,128)S(1)} %collective-permute-done.other_ref.refs_1_, ...), custom_call_target="tpu_custom_call" | custom-call | tf_op jit(solution)/shard_map/products_far/pallas_call | solution.py:139
  86.4 1.5 %collective-permute-start.15 = (f32[256,256]{1,0:T(8,128)S(1)}, f32[256,256]{1,0:T(8,128)S(1)}, u32[]{:S(2)}, u32[]{:S(2)}) collective-permute-start(f32[256,256]{1,0:T(8,128)S(1)} %get-tuple-element.35), channel_id=1, source_target_pairs={{0,4},{1,6},{2,7},{3,5},{4,0},{5,2},{6,3},{7,1},{8,13},{9,15},{10,... | collective-permute-start | bytes 786440 | tf_op jit(solution)/shard_map/ppermute | solution.py:252
  87.9 3.6 %collective-permute-start.17 = (f32[256,256]{1,0:T(8,128)}, f32[256,256]{1,0:T(8,128)}, u32[]{:S(2)}, u32[]{:S(2)}) collective-permute-start(f32[256,256]{1,0:T(8,128)} %get-tuple-element.37), channel_id=1, source_target_pairs={{0,0},{1,2},{2,3},{3,1},{4,4},{5,6},{6,7},{7,5},{8,9},{9,11},{10,1... | collective-permute-start | bytes 786440 | tf_op jit(solution)/shard_map/ppermute | solution.py:252
  91.5 1.9 %collective-permute-start.18 = (f32[256,256]{1,0:T(8,128)}, f32[256,256]{1,0:T(8,128)}, u32[]{:S(2)}, u32[]{:S(2)}) collective-permute-start(f32[256,256]{1,0:T(8,128)} %get-tuple-element.38), channel_id=1, source_target_pairs={{0,2},{1,0},{2,1},{3,3},{4,6},{5,4},{6,5},{7,7},{8,11},{9,9},{10,8... | collective-permute-start | bytes 786440 | tf_op jit(solution)/shard_map/ppermute | solution.py:252
  94.3 1.1 %collective-permute-start.22 = (f32[256,256]{1,0:T(8,128)}, f32[256,256]{1,0:T(8,128)}, u32[]{:S(2)}, u32[]{:S(2)}) collective-permute-start(f32[256,256]{1,0:T(8,128)} %get-tuple-element.44), channel_id=1, source_target_pairs={{0,2},{1,3},{2,0},{3,1},{4,6},{5,7},{6,4},{7,5},{8,10},{9,11},{10,... | collective-permute-start | bytes 786440 | tf_op jit(solution)/shard_map/ppermute | solution.py:252
  95.8 1.8 %place_most.1.refs_6_ = f32[256,2048]{1,0:T(8,128)} custom-call(s32[32,16]{1,0:T(8,128)S(1)} %copy-done.2, f32[256,256]{1,0:T(8,128)S(1)} %collective-permute-done.12.refs_0_, f32[256,256]{1,0:T(8,128)S(1)} %collective-permute-done.13.refs_1_, f32[256,256]{1,0:T(8,128)S(1)} %collective-permute-done.10.refs_2_, ...), custom_call_target="tpu_custom_call" | custom-call | tf_op jit(solution)/shard_map/place_most/pallas_call | solution.py:181
  98.3 3.5 %collective-permute-done.16.refs_1_ = f32[256,256]{1,0:T(8,128)} collective-permute-done((f32[256,256]{1,0:T(8,128)}, f32[256,256]{1,0:T(8,128)}, u32[]{:S(2)}, u32[]{:S(2)}) %collective-permute-start.16) | collective-permute-done | bytes 262176 | tf_op jit(solution)/shard_map/ppermute | solution.py:252
  101.8 1.9 %collective-permute-done.18.refs_3_ = f32[256,256]{1,0:T(8,128)} collective-permute-done((f32[256,256]{1,0:T(8,128)}, f32[256,256]{1,0:T(8,128)}, u32[]{:S(2)}, u32[]{:S(2)}) %collective-permute-start.18) | collective-permute-done | bytes 262176 | tf_op jit(solution)/shard_map/ppermute | solution.py:252
  103.7 2.3 %place_last.1 = f32[256,2048]{1,0:T(8,128)} custom-call(s32[32,16]{1,0:T(8,128)S(1)} %copy-done.2, f32[256,256]{1,0:T(8,128)S(1)} %collective-permute-done.15.refs_0_, f32[256,256]{1,0:T(8,128)} %collective-permute-done.16.refs_1_, f32[256,256]{1,0:T(8,128)} %collective-permute-done.17.refs_2_, ...), custom_call_target="tpu_custom_call", output_to_operand_aliasing={{}: (7, {})} | custom-call | tf_op jit(solution)/shard_map/place_last/pallas_call | solution.py:181
  (35 shorter events, 3.7 us)
Async XLA Ops:
  0.6 7.6 %collective-permute-start = (f32[256,1024]{1,0:T(8,128)}, f32[256,1024]{1,0:T(8,128)S(1)}, u32[]{:S(2)}, u32[]{:S(2)}) collective-permute-start(f32[256,1024]{1,0:T(8,128)} %refs_0_.7), channel_id=1, source_target_pairs={{0,2},{1,3},{2,0},{3,1},{4,6},{5,7},{6,4},{7,5},{8,10},{9,11},{10,... | collective-permute-start | bytes 3145736 | tf_op jit(solution)/shard_map/ppermute | solution.py:252
  1.1 29.7 %collective-permute-start.6 = (f32[256,1024]{1,0:T(8,128)}, f32[256,1024]{1,0:T(8,128)S(1)}, u32[]{:S(2)}, u32[]{:S(2)}) collective-permute-start(f32[256,1024]{1,0:T(8,128)} %refs_0_.7), channel_id=1, source_target_pairs={{0,8},{1,9},{2,26},{3,27},{4,12},{5,13},{6,30},{7,31},{8,16},{9,17... | collective-permute-start | bytes 3145736 | tf_op jit(solution)/shard_map/ppermute | solution.py:252
  3.8 27.1 %collective-permute-start.7 = (f32[256,1024]{1,0:T(8,128)}, f32[256,1024]{1,0:T(8,128)S(1)}, u32[]{:S(2)}, u32[]{:S(2)}) collective-permute-start(f32[256,1024]{1,0:T(8,128)} %refs_0_.7), channel_id=1, source_target_pairs={{0,4},{1,5},{2,6},{3,7},{4,0},{5,1},{6,2},{7,3},{8,12},{9,13},{10,... | collective-permute-start | bytes 3145736 | tf_op jit(solution)/shard_map/ppermute | solution.py:252
  5.3 2.9 %collective-permute-start.1 = (f32[1,256]{1,0:T(1,128)}, f32[1,256]{1,0:T(1,128)S(1)}, u32[]{:S(2)}, u32[]{:S(2)}) collective-permute-start(f32[1,256]{1,0:T(1,128)} %bitcast.3), channel_id=1, source_target_pairs={{0,2},{1,3},{2,0},{3,1},{4,6},{5,7},{6,4},{7,5},{8,10},{9,11},{10,... | collective-permute-start | bytes 3080 | tf_op jit(solution)/shard_map/ppermute | solution.py:252
  8.2 1.2 %copy-start = (f32[256,1024]{1,0:T(8,128)S(1)}, f32[256,1024]{1,0:T(8,128)}, u32[]{:S(2)}) copy-start(f32[256,1024]{1,0:T(8,128)} %refs_0_.7) | copy-start | bytes 3145732
  9.4 0.7 copy-start.3
  10.1 26.1 %copy-start.1 = (f32[256,1024]{1,0:T(8,128)S(1)}, f32[256,1024]{1,0:T(8,128)}, u32[]{:S(2)}) copy-start(f32[256,1024]{1,0:T(8,128)} %refs_0_.7) | copy-start | bytes 3145732
  11.3 19.5 %collective-permute-start.2 = (f32[8,1024]{1,0:T(8,128)S(1)}, f32[8,1024]{1,0:T(8,128)S(1)}, u32[]{:S(2)}, u32[]{:S(2)}) collective-permute-start(f32[8,1024]{1,0:T(8,128)S(1)} %block_stats.1.refs_0_), channel_id=1, source_target_pairs={{0,8},{1,9},{2,10},{3,11},{4,12},{5,13},{6,14},{7,15},{8,16},{9,17... | collective-permute-start | bytes 98312 | tf_op jit(solution)/shard_map/ppermute | solution.py:252
  11.3 19.5 %collective-permute-start.3 = (f32[8,1024]{1,0:T(8,128)S(1)}, f32[8,1024]{1,0:T(8,128)S(1)}, u32[]{:S(2)}, u32[]{:S(2)}) collective-permute-start(f32[8,1024]{1,0:T(8,128)S(1)} %block_stats.1.refs_0_), channel_id=1, source_target_pairs={{0,16},{1,17},{2,18},{3,19},{4,20},{5,21},{6,22},{7,23},{8,24},{9,... | collective-permute-start | bytes 98312 | tf_op jit(solution)/shard_map/ppermute | solution.py:252
  12.6 18.3 %collective-permute-start.4 = (f32[8,1024]{1,0:T(8,128)S(1)}, f32[8,1024]{1,0:T(8,128)S(1)}, u32[]{:S(2)}, u32[]{:S(2)}) collective-permute-start(f32[8,1024]{1,0:T(8,128)S(1)} %block_stats.1.refs_0_), channel_id=1, source_target_pairs={{0,24},{1,25},{2,26},{3,27},{4,28},{5,29},{6,30},{7,31},{8,0},{9,1... | collective-permute-start | bytes 98312 | tf_op jit(solution)/shard_map/ppermute | solution.py:252
  30.9 5.3 %collective-permute-start.8 = (f32[256,1024]{1,0:T(8,128)S(1)}, f32[256,1024]{1,0:T(8,128)S(1)}, u32[]{:S(2)}, u32[]{:S(2)}) collective-permute-start(f32[256,1024]{1,0:T(8,128)S(1)} %collective-permute-done.7.refs_2_), channel_id=1, source_target_pairs={{0,2},{1,3},{2,0},{3,1},{4,6},{5,7},{6,4},{7,5},{8,10},{9,11},{10,... | collective-permute-start | bytes 3145736 | tf_op jit(solution)/shard_map/ppermute | solution.py:252
  31.0 27.7 %collective-permute-start.9 = (f32[256,1024]{1,0:T(8,128)S(1)}, f32[256,1024]{1,0:T(8,128)S(1)}, u32[]{:S(2)}, u32[]{:S(2)}) collective-permute-start(f32[256,1024]{1,0:T(8,128)S(1)} %collective-permute-done.6.refs_4_), channel_id=1, source_target_pairs={{0,8},{1,9},{2,26},{3,27},{4,12},{5,13},{6,30},{7,31},{8,16},{9,17... | collective-permute-start | bytes 3145736 | tf_op jit(solution)/shard_map/ppermute | solution.py:252
  32.3 3.9 %collective-permute-start.5 = (f32[8,1024]{1,0:T(8,128)S(1)}, f32[8,1024]{1,0:T(8,128)S(1)}, u32[]{:S(2)}, u32[]{:S(2)}) collective-permute-start(f32[8,1024]{1,0:T(8,128)S(1)} %merge.2.refs_0_), channel_id=1, source_target_pairs={{0,4},{1,5},{2,6},{3,7},{4,0},{5,1},{6,2},{7,3},{8,12},{9,13},{10,... | collective-permute-start | bytes 98312 | tf_op jit(solution)/shard_map/ppermute | solution.py:252
  38.1 20.6 %collective-permute-start.10 = (f32[256,256]{1,0:T(8,128)S(1)}, f32[256,256]{1,0:T(8,128)S(1)}, u32[]{:S(2)}, u32[]{:S(2)}) collective-permute-start(f32[256,256]{1,0:T(8,128)S(1)} %get-tuple-element.27), channel_id=1, source_target_pairs={{0,5},{1,7},{2,6},{3,4},{4,1},{5,3},{6,2},{7,0},{8,12},{9,14},{10,... | collective-permute-start | bytes 786440 | tf_op jit(solution)/shard_map/ppermute | solution.py:252
  40.8 17.9 %collective-permute-start.11 = (f32[256,256]{1,0:T(8,128)S(1)}, f32[256,256]{1,0:T(8,128)S(1)}, u32[]{:S(2)}, u32[]{:S(2)}) collective-permute-start(f32[256,256]{1,0:T(8,128)S(1)} %get-tuple-element.28), channel_id=1, source_target_pairs={{0,7},{1,5},{2,4},{3,6},{4,3},{5,1},{6,0},{7,2},{8,14},{9,12},{10,... | collective-permute-start | bytes 786440 | tf_op jit(solution)/shard_map/ppermute | solution.py:252
  42.3 16.4 %collective-permute-start.12 = (f32[256,256]{1,0:T(8,128)S(1)}, f32[256,256]{1,0:T(8,128)S(1)}, u32[]{:S(2)}, u32[]{:S(2)}) collective-permute-start(f32[256,256]{1,0:T(8,128)S(1)} %get-tuple-element.29), channel_id=1, source_target_pairs={{0,1},{1,3},{2,2},{3,0},{4,5},{5,7},{6,6},{7,4},{8,8},{9,10},{10,1... | collective-permute-start | bytes 786440 | tf_op jit(solution)/shard_map/ppermute | solution.py:252
  45.2 13.6 %copy-start.2 = (s32[32,16]{1,0:T(8,128)S(1)}, s32[32,16]{1,0:T(8,128)}, u32[]{:S(2)}) copy-start(s32[32,16]{1,0:T(8,128)} %constant.19.clone.table_ref) | copy-start | bytes 6148
  45.2 13.5 %collective-permute-start.13 = (f32[256,256]{1,0:T(8,128)S(1)}, f32[256,256]{1,0:T(8,128)S(1)}, u32[]{:S(2)}, u32[]{:S(2)}) collective-permute-start(f32[256,256]{1,0:T(8,128)S(1)} %get-tuple-element.30), channel_id=1, source_target_pairs={{0,3},{1,1},{2,0},{3,2},{4,7},{5,5},{6,4},{7,6},{8,10},{9,8},{10,9... | collective-permute-start | bytes 786440 | tf_op jit(solution)/shard_map/ppermute | solution.py:252
  58.7 25.0 %collective-permute-start.14 = (f32[256,1024]{1,0:T(8,128)S(1)}, f32[256,1024]{1,0:T(8,128)S(1)}, u32[]{:S(2)}, u32[]{:S(2)}) collective-permute-start(f32[256,1024]{1,0:T(8,128)S(1)} %collective-permute-done.9.refs_4_), channel_id=1, source_target_pairs={{0,8},{1,9},{2,26},{3,27},{4,12},{5,13},{6,30},{7,31},{8,16},{9,17... | collective-permute-start | bytes 3145736 | tf_op jit(solution)/shard_map/ppermute | solution.py:252
  61.5 26.4 %collective-permute-start.19 = (f32[512,256]{1,0:T(8,128)S(1)}, f32[512,256]{1,0:T(8,128)S(1)}, u32[]{:S(2)}, u32[]{:S(2)}) collective-permute-start(f32[512,256]{1,0:T(8,128)S(1)} %get-tuple-element.40), channel_id=1, source_target_pairs={{0,1},{1,0},{2,3},{3,2},{4,5},{5,4},{6,7},{7,6},{8,9},{9,8},{10,11... | collective-permute-start | bytes 1572872 | tf_op jit(solution)/shard_map/ppermute | solution.py:252
  63.1 28.4 %collective-permute-start.20 = (f32[512,256]{1,0:T(8,128)S(1)}, f32[512,256]{1,0:T(8,128)S(1)}, u32[]{:S(2)}, u32[]{:S(2)}) collective-permute-start(f32[512,256]{1,0:T(8,128)S(1)} %get-tuple-element.42), channel_id=1, source_target_pairs={{0,4},{1,5},{2,6},{3,7},{4,0},{5,1},{6,2},{7,3},{8,12},{9,13},{10,... | collective-permute-start | bytes 1572872 | tf_op jit(solution)/shard_map/ppermute | solution.py:252
  64.6 28.8 %collective-permute-start.21 = (f32[512,256]{1,0:T(8,128)S(1)}, f32[512,256]{1,0:T(8,128)S(1)}, u32[]{:S(2)}, u32[]{:S(2)}) collective-permute-start(f32[512,256]{1,0:T(8,128)S(1)} %get-tuple-element.43), channel_id=1, source_target_pairs={{0,5},{1,4},{2,7},{3,6},{4,1},{5,0},{6,3},{7,2},{8,13},{9,12},{10,... | collective-permute-start | bytes 1572872 | tf_op jit(solution)/shard_map/ppermute | solution.py:252
  86.4 9.2 %collective-permute-start.15 = (f32[256,256]{1,0:T(8,128)S(1)}, f32[256,256]{1,0:T(8,128)S(1)}, u32[]{:S(2)}, u32[]{:S(2)}) collective-permute-start(f32[256,256]{1,0:T(8,128)S(1)} %get-tuple-element.35), channel_id=1, source_target_pairs={{0,4},{1,6},{2,7},{3,5},{4,0},{5,2},{6,3},{7,1},{8,13},{9,15},{10,... | collective-permute-start | bytes 786440 | tf_op jit(solution)/shard_map/ppermute | solution.py:252
  87.9 13.9 %collective-permute-start.16 = (f32[256,256]{1,0:T(8,128)}, f32[256,256]{1,0:T(8,128)}, u32[]{:S(2)}, u32[]{:S(2)}) collective-permute-start(f32[256,256]{1,0:T(8,128)} %get-tuple-element.36), channel_id=1, source_target_pairs={{0,6},{1,4},{2,5},{3,7},{4,2},{5,0},{6,1},{7,3},{8,15},{9,13},{10,... | collective-permute-start | bytes 786440 | tf_op jit(solution)/shard_map/ppermute | solution.py:252
  87.9 13.9 %collective-permute-start.17 = (f32[256,256]{1,0:T(8,128)}, f32[256,256]{1,0:T(8,128)}, u32[]{:S(2)}, u32[]{:S(2)}) collective-permute-start(f32[256,256]{1,0:T(8,128)} %get-tuple-element.37), channel_id=1, source_target_pairs={{0,0},{1,2},{2,3},{3,1},{4,4},{5,6},{6,7},{7,5},{8,9},{9,11},{10,1... | collective-permute-start | bytes 786440 | tf_op jit(solution)/shard_map/ppermute | solution.py:252
  91.5 12.1 %collective-permute-start.18 = (f32[256,256]{1,0:T(8,128)}, f32[256,256]{1,0:T(8,128)}, u32[]{:S(2)}, u32[]{:S(2)}) collective-permute-start(f32[256,256]{1,0:T(8,128)} %get-tuple-element.38), channel_id=1, source_target_pairs={{0,2},{1,0},{2,1},{3,3},{4,6},{5,4},{6,5},{7,7},{8,11},{9,9},{10,8... | collective-permute-start | bytes 786440 | tf_op jit(solution)/shard_map/ppermute | solution.py:252
  94.3 9.4 %collective-permute-start.22 = (f32[256,256]{1,0:T(8,128)}, f32[256,256]{1,0:T(8,128)}, u32[]{:S(2)}, u32[]{:S(2)}) collective-permute-start(f32[256,256]{1,0:T(8,128)} %get-tuple-element.44), channel_id=1, source_target_pairs={{0,2},{1,3},{2,0},{3,1},{4,6},{5,7},{6,4},{7,5},{8,10},{9,11},{10,... | collective-permute-start | bytes 786440 | tf_op jit(solution)/shard_map/ppermute | solution.py:252
  95.7 8.0 %collective-permute-start.23 = (f32[256,256]{1,0:T(8,128)}, f32[256,256]{1,0:T(8,128)}, u32[]{:S(2)}, u32[]{:S(2)}) collective-permute-start(f32[256,256]{1,0:T(8,128)} %get-tuple-element.45), channel_id=1, source_target_pairs={{0,2},{1,3},{2,0},{3,1},{4,6},{5,7},{6,4},{7,5},{8,10},{9,11},{10,... | collective-permute-start | bytes 786440 | tf_op jit(solution)/shard_map/ppermute | solution.py:252

commit v5 on v4

--- a/solution.py
+++ b/solution.py
@@ -10,6 +10,7 @@
 
 BOTH = ("smp", "par")
 VMEM_LIMIT = 16 * 1024 * 1024
+LONG = pl.CostEstimate(flops=4_000_000_000, bytes_accessed=0, transcendentals=0)
 FREE = pl.CostEstimate(flops=0, bytes_accessed=0, transcendentals=0)
 
 
@@ -135,7 +136,7 @@
     side[...] = from_side[height:, :] + got_side[height:, :]
 
 
-def kernel_call(kernel, out_shapes, name, *args, smem=0):
+def kernel_call(kernel, out_shapes, name, *args, smem=0, cost=FREE):
     return pl.pallas_call(
         kernel,
         out_shape=[jax.ShapeDtypeStruct(s, jnp.float32) for s in out_shapes],
@@ -143,7 +144,7 @@
         + [pl.BlockSpec(memory_space=pltpu.VMEM)] * (len(args) - smem),
         out_specs=[pl.BlockSpec(memory_space=pltpu.VMEM)] * len(out_shapes),
         compiler_params=pltpu.CompilerParams(vmem_limit_bytes=VMEM_LIMIT),
-        cost_estimate=FREE,
+        cost_estimate=cost,
         name=name,
     )(*args)
 
@@ -239,6 +240,7 @@
         return z % levels // per_plane
 
     ring = moves(lambda z, x, c, y: (z + 1 - 2 * c, x, c, y))
+    back = moves(lambda z, x, c, y: (z - 1 + 2 * c, x, c, y))
     over_core = moves(lambda z, x, c, y: (z, x, 1 - c, y))
     over_side = moves(lambda z, x, c, y: (z, 1 - x, c, y))
     over_plane = moves(lambda z, x, c, y: (z, x, c, 1 - y))
@@ -283,8 +285,8 @@
         *all_rows,
         after(log_derivs, out[0]),
     )
+    three = send(after(log_derivs, *near[1], *near[0], *own_level), back)
     two = after(two, *near[1], *near[0], *own_level)
-    three = send(two, ring)
     keep_own, keep_side, sent_own, sent_side = kernel_call(
         functools.partial(across_level_kernel, scale, planes, 0),
         [(2 * rows, rows)] * 4,
@@ -295,6 +297,7 @@
         two,
         *own_level,
         smem=1,
+        cost=LONG,
     )
     got_own = send(sent_own, over_plane)
     got_side = send(sent_side, diagonal)

time: 106 us -> 105 us (level)
  waiting for transfers between devices: 52 us -> 50.3 us
    ppermute x24, waiting for transfers between devices: 52 us -> 50.3 us  [send(): return lax.ppermute(value, BOTH, pairs)]
  transfers between devices with their start and end apart: 24 -> 24, of which waited for: 8 -> 10; matrix products, arithmetic and copies ran while one was open for 1% -> 1% of each run, Pallas kernels for 12% -> 13%
where the time goes in v5:
time: 105 us; the launch traced here: 104 us
  waiting for transfers between devices  50.3 us (48%)
  starting transfers between devices  35.3 us (34%)
  Pallas kernels  15.4 us (15%)
  local copies, waits for them, and re-layouts  1.91 us (2%)
    ppermute x24, waiting for transfers between devices, send(): return lax.ppermute(value, BOTH, pairs)  50.3 us
    ppermute x24, starting transfers between devices, send(): return lax.ppermute(value, BOTH, pairs)  35.3 us
    pallas_call x8, Pallas kernels, kernel_call(): pl.pallas_call(kernel, out_shape=[jax.ShapeDtypeStruct(s, jnp.float32) fo...  11.3 us
    pallas_call x2, Pallas kernels, place(): pl.pallas_call(functools.partial(place_kernel, planes, [len(terms) for te...  4.12 us
  transfers between devices with their start and end apart: 24, of which 10 were waited for; matrix products, arithmetic and copies ran while one was open for 1% of the time, Pallas kernels for 13%

profile of v5, /device:TPU:0, one launch (start us, length us, event | category | flops | bytes accessed | tf_op | source)
XLA Modules:
  0.0 104.3 jit_solution(13889649672337572732)
XLA Ops:
  1.1 2.6 %collective-permute-start.6 = (f32[256,1024]{1,0:T(8,128)}, f32[256,1024]{1,0:T(8,128)S(1)}, u32[]{:S(2)}, u32[]{:S(2)}) collective-permute-start(f32[256,1024]{1,0:T(8,128)} %refs_0_.7), channel_id=1, source_target_pairs={{0,8},{1,9},{2,26},{3,27},{4,12},{5,13},{6,30},{7,31},{8,16},{9,17... | collective-permute-start | bytes 3145736 | tf_op jit(solution)/shard_map/ppermute | solution.py:254
  3.8 1.5 %collective-permute-start.7 = (f32[256,1024]{1,0:T(8,128)}, f32[256,1024]{1,0:T(8,128)S(1)}, u32[]{:S(2)}, u32[]{:S(2)}) collective-permute-start(f32[256,1024]{1,0:T(8,128)} %refs_0_.7), channel_id=1, source_target_pairs={{0,4},{1,5},{2,6},{3,7},{4,0},{5,1},{6,2},{7,3},{8,12},{9,13},{10,... | collective-permute-start | bytes 3145736 | tf_op jit(solution)/shard_map/ppermute | solution.py:254
  5.3 1.9 %collective-permute-start.1 = (f32[1,256]{1,0:T(1,128)}, f32[1,256]{1,0:T(1,128)S(1)}, u32[]{:S(2)}, u32[]{:S(2)}) collective-permute-start(f32[1,256]{1,0:T(1,128)} %bitcast.3), channel_id=1, source_target_pairs={{0,2},{1,3},{2,0},{3,1},{4,6},{5,7},{6,4},{7,5},{8,10},{9,11},{10,... | collective-permute-start | bytes 3080 | tf_op jit(solution)/shard_map/ppermute | solution.py:254
  8.2 1.2 %copy-done = f32[256,1024]{1,0:T(8,128)S(1)} copy-done((f32[256,1024]{1,0:T(8,128)S(1)}, f32[256,1024]{1,0:T(8,128)}, u32[]{:S(2)}) %copy-start) | copy-done | bytes 1048600
  10.1 1.2 %block_stats.1.refs_0_ = f32[8,1024]{1,0:T(8,128)S(1)} custom-call(f32[256,1024]{1,0:T(8,128)S(1)} %copy-done, f32[256,1024]{1,0:T(8,128)S(1)} %collective-permute-done.other_ref.refs_1_, f32[1,256]{1,0:T(1,128)S(1)} %bitcast.4, f32[1,256]{1,0:T(1,128)S(1)} %collective-permute-done.1.other_coef_ref), custom_call_target="tpu_custom_call" | custom-call | tf_op jit(solution)/shard_map/block_stats/pallas_call | solution.py:140
  11.3 1.3 %collective-permute-start.3 = (f32[8,1024]{1,0:T(8,128)S(1)}, f32[8,1024]{1,0:T(8,128)S(1)}, u32[]{:S(2)}, u32[]{:S(2)}) collective-permute-start(f32[8,1024]{1,0:T(8,128)S(1)} %block_stats.1.refs_0_), channel_id=1, source_target_pairs={{0,16},{1,17},{2,18},{3,19},{4,20},{5,21},{6,22},{7,23},{8,24},{9,... | collective-permute-start | bytes 98312 | tf_op jit(solution)/shard_map/ppermute | solution.py:254
  12.6 2.7 %collective-permute-start.4 = (f32[8,1024]{1,0:T(8,128)S(1)}, f32[8,1024]{1,0:T(8,128)S(1)}, u32[]{:S(2)}, u32[]{:S(2)}) collective-permute-start(f32[8,1024]{1,0:T(8,128)S(1)} %block_stats.1.refs_0_), channel_id=1, source_target_pairs={{0,24},{1,25},{2,26},{3,27},{4,28},{5,29},{6,30},{7,31},{8,0},{9,1... | collective-permute-start | bytes 98312 | tf_op jit(solution)/shard_map/ppermute | solution.py:254
  15.3 15.6 %collective-permute-done.2.refs_1_ = f32[8,1024]{1,0:T(8,128)S(1)} collective-permute-done((f32[8,1024]{1,0:T(8,128)S(1)}, f32[8,1024]{1,0:T(8,128)S(1)}, u32[]{:S(2)}, u32[]{:S(2)}) %collective-permute-start.2) | collective-permute-done | bytes 32800 | tf_op jit(solution)/shard_map/ppermute | solution.py:254
  31.0 1.3 %collective-permute-start.18 = (f32[256,1024]{1,0:T(8,128)S(1)}, f32[256,1024]{1,0:T(8,128)S(1)}, u32[]{:S(2)}, u32[]{:S(2)}) collective-permute-start(f32[256,1024]{1,0:T(8,128)S(1)} %collective-permute-done.6.refs_4_), channel_id=1, source_target_pairs={{0,8},{1,9},{2,26},{3,27},{4,12},{5,13},{6,30},{7,31},{8,16},{9,17... | collective-permute-start | bytes 3145736 | tf_op jit(solution)/shard_map/ppermute | solution.py:254
  32.3 1.7 %collective-permute-start.5 = (f32[8,1024]{1,0:T(8,128)S(1)}, f32[8,1024]{1,0:T(8,128)S(1)}, u32[]{:S(2)}, u32[]{:S(2)}) collective-permute-start(f32[8,1024]{1,0:T(8,128)S(1)} %merge.2.refs_0_), channel_id=1, source_target_pairs={{0,4},{1,5},{2,6},{3,7},{4,0},{5,1},{6,2},{7,3},{8,12},{9,13},{10,... | collective-permute-start | bytes 98312 | tf_op jit(solution)/shard_map/ppermute | solution.py:254
  34.0 2.2 %collective-permute-done.5.refs_1_ = f32[8,1024]{1,0:T(8,128)S(1)} collective-permute-done((f32[8,1024]{1,0:T(8,128)S(1)}, f32[8,1024]{1,0:T(8,128)S(1)}, u32[]{:S(2)}, u32[]{:S(2)}) %collective-permute-start.5) | collective-permute-done | bytes 32800 | tf_op jit(solution)/shard_map/ppermute | solution.py:254
  36.2 1.9 %products_near.1 = (f32[256,256]{1,0:T(8,128)S(1)}, f32[256,256]{1,0:T(8,128)S(1)}, f32[256,256]{1,0:T(8,128)S(1)}, f32[256,256]{1,0:T(8,128)S(1)}) custom-call(f32[8,1024]{1,0:T(8,128)S(1)} %merge.3.mean_ref, f32[256,1024]{1,0:T(8,128)S(1)} %copy-done.1, f32[256,1024]{1,0:T(8,128)S(1)} %collective-permute-done.other_ref.refs_1_, ...), custom_call_target="tpu_custom_call" | custom-call | tf_op jit(solution)/shard_map/products_near/pallas_call | solution.py:140
  38.1 4.1 %collective-permute-start.10 = (f32[256,256]{1,0:T(8,128)S(1)}, f32[256,256]{1,0:T(8,128)S(1)}, u32[]{:S(2)}, u32[]{:S(2)}) collective-permute-start(f32[256,256]{1,0:T(8,128)S(1)} %get-tuple-element.29), channel_id=1, source_target_pairs={{0,7},{1,5},{2,4},{3,6},{4,3},{5,1},{6,0},{7,2},{8,14},{9,12},{10,... | collective-permute-start | bytes 786440 | tf_op jit(solution)/shard_map/ppermute | solution.py:254
  42.2 1.9 %collective-permute-start.11 = (f32[256,256]{1,0:T(8,128)S(1)}, f32[256,256]{1,0:T(8,128)S(1)}, u32[]{:S(2)}, u32[]{:S(2)}) collective-permute-start(f32[256,256]{1,0:T(8,128)S(1)} %get-tuple-element.30), channel_id=1, source_target_pairs={{0,1},{1,3},{2,2},{3,0},{4,5},{5,7},{6,6},{7,4},{8,8},{9,10},{10,1... | collective-permute-start | bytes 786440 | tf_op jit(solution)/shard_map/ppermute | solution.py:254
  44.1 3.6 %collective-permute-start.12 = (f32[256,256]{1,0:T(8,128)S(1)}, f32[256,256]{1,0:T(8,128)S(1)}, u32[]{:S(2)}, u32[]{:S(2)}) collective-permute-start(f32[256,256]{1,0:T(8,128)S(1)} %get-tuple-element.31), channel_id=1, source_target_pairs={{0,3},{1,1},{2,0},{3,2},{4,7},{5,5},{6,4},{7,6},{8,10},{9,8},{10,9... | collective-permute-start | bytes 786440 | tf_op jit(solution)/shard_map/ppermute | solution.py:254
  47.9 1.9 %products_level.1 = (f32[512,256]{1,0:T(8,128)S(1)}, f32[512,256]{1,0:T(8,128)S(1)}) custom-call(f32[8,1024]{1,0:T(8,128)S(1)} %merge.3.mean_ref, f32[256,1024]{1,0:T(8,128)S(1)} %copy-done.1, f32[256,1024]{1,0:T(8,128)S(1)} %collective-permute-done.other_ref.refs_1_, f32[256,1024]{1,0:T(8,128)S(1)} %collective-permute-done.7.refs_2_, ...), custom_call_target="tpu_custom_call" | custom-call | tf_op jit(solution)/shard_map/products_level/pallas_call | solution.py:140
  49.8 1.2 %collective-permute-done.11.refs_0_ = f32[256,256]{1,0:T(8,128)S(1)} collective-permute-done((f32[256,256]{1,0:T(8,128)S(1)}, f32[256,256]{1,0:T(8,128)S(1)}, u32[]{:S(2)}, u32[]{:S(2)}) %collective-permute-start.11) | collective-permute-done | bytes 262176 | tf_op jit(solution)/shard_map/ppermute | solution.py:254
  51.0 4.5 %collective-permute-done.12.refs_1_ = f32[256,256]{1,0:T(8,128)S(1)} collective-permute-done((f32[256,256]{1,0:T(8,128)S(1)}, f32[256,256]{1,0:T(8,128)S(1)}, u32[]{:S(2)}, u32[]{:S(2)}) %collective-permute-start.12) | collective-permute-done | bytes 262176 | tf_op jit(solution)/shard_map/ppermute | solution.py:254
  55.5 1.0 collective-permute-done.9.refs_2_
  56.5 2.3 %collective-permute-done.18.refs_4_ = f32[256,1024]{1,0:T(8,128)S(1)} collective-permute-done((f32[256,1024]{1,0:T(8,128)S(1)}, f32[256,1024]{1,0:T(8,128)S(1)}, u32[]{:S(2)}, u32[]{:S(2)}) %collective-permute-start.18) | collective-permute-done | bytes 1048608 | tf_op jit(solution)/shard_map/ppermute | solution.py:254
  58.8 2.7 %products_across.1 = (f32[512,256]{1,0:T(8,128)S(1)}, f32[512,256]{1,0:T(8,128)S(1)}, f32[512,256]{1,0:T(8,128)S(1)}, f32[512,256]{1,0:T(8,128)S(1)}) custom-call(s32[32,16]{1,0:T(8,128)S(1)} %copy-done.2, f32[8,1024]{1,0:T(8,128)S(1)} %merge.3.mean_ref, f32[256,1024]{1,0:T(8,128)S(1)} %copy-done.1, f32[256,1024]{1,0:T(8,128)S(1)} %collective-permute-done.other_ref.refs_1_, ...), custom_call_target="tpu_custom_call" | custom-call | flops 4000000000 | tf_op jit(solution)/shard_map/products_across/pallas_call | solution.py:140
  61.5 1.5 %collective-permute-start.19 = (f32[512,256]{1,0:T(8,128)S(1)}, f32[512,256]{1,0:T(8,128)S(1)}, u32[]{:S(2)}, u32[]{:S(2)}) collective-permute-start(f32[512,256]{1,0:T(8,128)S(1)} %get-tuple-element.42), channel_id=1, source_target_pairs={{0,1},{1,0},{2,3},{3,2},{4,5},{5,4},{6,7},{7,6},{8,9},{9,8},{10,11... | collective-permute-start | bytes 1572872 | tf_op jit(solution)/shard_map/ppermute | solution.py:254
  63.0 1.5 %collective-permute-start.20 = (f32[512,256]{1,0:T(8,128)S(1)}, f32[512,256]{1,0:T(8,128)S(1)}, u32[]{:S(2)}, u32[]{:S(2)}) collective-permute-start(f32[512,256]{1,0:T(8,128)S(1)} %get-tuple-element.44), channel_id=1, source_target_pairs={{0,4},{1,5},{2,6},{3,7},{4,0},{5,1},{6,2},{7,3},{8,12},{9,13},{10,... | collective-permute-start | bytes 1572872 | tf_op jit(solution)/shard_map/ppermute | solution.py:254
  65.1 17.5 %collective-permute-done.13.refs_4_ = f32[256,1024]{1,0:T(8,128)S(1)} collective-permute-done((f32[256,1024]{1,0:T(8,128)S(1)}, f32[256,1024]{1,0:T(8,128)S(1)}, u32[]{:S(2)}, u32[]{:S(2)}) %collective-permute-start.13) | collective-permute-done | bytes 1048608 | tf_op jit(solution)/shard_map/ppermute | solution.py:254
  82.6 2.7 %products_far.1 = (f32[256,256]{1,0:T(8,128)S(1)}, f32[256,256]{1,0:T(8,128)}, f32[256,256]{1,0:T(8,128)}, f32[256,256]{1,0:T(8,128)}) custom-call(f32[8,1024]{1,0:T(8,128)S(1)} %merge.3.mean_ref, f32[256,1024]{1,0:T(8,128)S(1)} %copy-done.1, f32[256,1024]{1,0:T(8,128)S(1)} %collective-permute-done.other_ref.refs_1_, ...), custom_call_target="tpu_custom_call" | custom-call | tf_op jit(solution)/shard_map/products_far/pallas_call | solution.py:140
  85.3 2.5 %collective-permute-start.15 = (f32[256,256]{1,0:T(8,128)}, f32[256,256]{1,0:T(8,128)}, u32[]{:S(2)}, u32[]{:S(2)}) collective-permute-start(f32[256,256]{1,0:T(8,128)} %get-tuple-element.37), channel_id=1, source_target_pairs={{0,6},{1,4},{2,5},{3,7},{4,2},{5,0},{6,1},{7,3},{8,15},{9,13},{10,... | collective-permute-start | bytes 786440 | tf_op jit(solution)/shard_map/ppermute | solution.py:254
  87.8 3.6 %collective-permute-start.16 = (f32[256,256]{1,0:T(8,128)}, f32[256,256]{1,0:T(8,128)}, u32[]{:S(2)}, u32[]{:S(2)}) collective-permute-start(f32[256,256]{1,0:T(8,128)} %get-tuple-element.38), channel_id=1, source_target_pairs={{0,0},{1,2},{2,3},{3,1},{4,4},{5,6},{6,7},{7,5},{8,9},{9,11},{10,1... | collective-permute-start | bytes 786440 | tf_op jit(solution)/shard_map/ppermute | solution.py:254
  91.4 1.9 %collective-permute-start.17 = (f32[256,256]{1,0:T(8,128)}, f32[256,256]{1,0:T(8,128)}, u32[]{:S(2)}, u32[]{:S(2)}) collective-permute-start(f32[256,256]{1,0:T(8,128)} %get-tuple-element.39), channel_id=1, source_target_pairs={{0,2},{1,0},{2,1},{3,3},{4,6},{5,4},{6,5},{7,7},{8,11},{9,9},{10,8... | collective-permute-start | bytes 786440 | tf_op jit(solution)/shard_map/ppermute | solution.py:254
  94.7 1.8 %place_most.1.refs_6_ = f32[256,2048]{1,0:T(8,128)} custom-call(s32[32,16]{1,0:T(8,128)S(1)} %copy-done.2, f32[256,256]{1,0:T(8,128)S(1)} %collective-permute-done.11.refs_0_, f32[256,256]{1,0:T(8,128)S(1)} %collective-permute-done.12.refs_1_, f32[256,256]{1,0:T(8,128)S(1)} %collective-permute-done.9.refs_2_, ...), custom_call_target="tpu_custom_call" | custom-call | tf_op jit(solution)/shard_map/place_most/pallas_call | solution.py:182
  97.1 2.6 %collective-permute-done.15.refs_1_ = f32[256,256]{1,0:T(8,128)} collective-permute-done((f32[256,256]{1,0:T(8,128)}, f32[256,256]{1,0:T(8,128)}, u32[]{:S(2)}, u32[]{:S(2)}) %collective-permute-start.15) | collective-permute-done | bytes 262176 | tf_op jit(solution)/shard_map/ppermute | solution.py:254
  99.8 2.2 %collective-permute-done.17.refs_3_ = f32[256,256]{1,0:T(8,128)} collective-permute-done((f32[256,256]{1,0:T(8,128)}, f32[256,256]{1,0:T(8,128)}, u32[]{:S(2)}, u32[]{:S(2)}) %collective-permute-start.17) | collective-permute-done | bytes 262176 | tf_op jit(solution)/shard_map/ppermute | solution.py:254
  102.0 2.3 %place_last.1 = f32[256,2048]{1,0:T(8,128)} custom-call(s32[32,16]{1,0:T(8,128)S(1)} %copy-done.2, f32[256,256]{1,0:T(8,128)S(1)} %collective-permute-done.14.refs_0_, f32[256,256]{1,0:T(8,128)} %collective-permute-done.15.refs_1_, f32[256,256]{1,0:T(8,128)} %collective-permute-done.16.refs_2_, ...), custom_call_target="tpu_custom_call", output_to_operand_aliasing={{}: (7, {})} | custom-call | tf_op jit(solution)/shard_map/place_last/pallas_call | solution.py:182
  (35 shorter events, 5.0 us)
Async XLA Ops:
  0.6 7.6 %collective-permute-start = (f32[256,1024]{1,0:T(8,128)}, f32[256,1024]{1,0:T(8,128)S(1)}, u32[]{:S(2)}, u32[]{:S(2)}) collective-permute-start(f32[256,1024]{1,0:T(8,128)} %refs_0_.7), channel_id=1, source_target_pairs={{0,2},{1,3},{2,0},{3,1},{4,6},{5,7},{6,4},{7,5},{8,10},{9,11},{10,... | collective-permute-start | bytes 3145736 | tf_op jit(solution)/shard_map/ppermute | solution.py:254
  1.1 29.7 %collective-permute-start.6 = (f32[256,1024]{1,0:T(8,128)}, f32[256,1024]{1,0:T(8,128)S(1)}, u32[]{:S(2)}, u32[]{:S(2)}) collective-permute-start(f32[256,1024]{1,0:T(8,128)} %refs_0_.7), channel_id=1, source_target_pairs={{0,8},{1,9},{2,26},{3,27},{4,12},{5,13},{6,30},{7,31},{8,16},{9,17... | collective-permute-start | bytes 3145736 | tf_op jit(solution)/shard_map/ppermute | solution.py:254
  3.8 27.1 %collective-permute-start.7 = (f32[256,1024]{1,0:T(8,128)}, f32[256,1024]{1,0:T(8,128)S(1)}, u32[]{:S(2)}, u32[]{:S(2)}) collective-permute-start(f32[256,1024]{1,0:T(8,128)} %refs_0_.7), channel_id=1, source_target_pairs={{0,4},{1,5},{2,6},{3,7},{4,0},{5,1},{6,2},{7,3},{8,12},{9,13},{10,... | collective-permute-start | bytes 3145736 | tf_op jit(solution)/shard_map/ppermute | solution.py:254
  5.3 2.9 %collective-permute-start.1 = (f32[1,256]{1,0:T(1,128)}, f32[1,256]{1,0:T(1,128)S(1)}, u32[]{:S(2)}, u32[]{:S(2)}) collective-permute-start(f32[1,256]{1,0:T(1,128)} %bitcast.3), channel_id=1, source_target_pairs={{0,2},{1,3},{2,0},{3,1},{4,6},{5,7},{6,4},{7,5},{8,10},{9,11},{10,... | collective-permute-start | bytes 3080 | tf_op jit(solution)/shard_map/ppermute | solution.py:254
  8.2 1.2 %copy-start = (f32[256,1024]{1,0:T(8,128)S(1)}, f32[256,1024]{1,0:T(8,128)}, u32[]{:S(2)}) copy-start(f32[256,1024]{1,0:T(8,128)} %refs_0_.7) | copy-start | bytes 3145732
  9.4 0.7 copy-start.3
  10.1 26.1 %copy-start.1 = (f32[256,1024]{1,0:T(8,128)S(1)}, f32[256,1024]{1,0:T(8,128)}, u32[]{:S(2)}) copy-start(f32[256,1024]{1,0:T(8,128)} %refs_0_.7) | copy-start | bytes 3145732
  11.3 19.5 %collective-permute-start.2 = (f32[8,1024]{1,0:T(8,128)S(1)}, f32[8,1024]{1,0:T(8,128)S(1)}, u32[]{:S(2)}, u32[]{:S(2)}) collective-permute-start(f32[8,1024]{1,0:T(8,128)S(1)} %block_stats.1.refs_0_), channel_id=1, source_target_pairs={{0,8},{1,9},{2,10},{3,11},{4,12},{5,13},{6,14},{7,15},{8,16},{9,17... | collective-permute-start | bytes 98312 | tf_op jit(solution)/shard_map/ppermute | solution.py:254
  11.3 19.5 %collective-permute-start.3 = (f32[8,1024]{1,0:T(8,128)S(1)}, f32[8,1024]{1,0:T(8,128)S(1)}, u32[]{:S(2)}, u32[]{:S(2)}) collective-permute-start(f32[8,1024]{1,0:T(8,128)S(1)} %block_stats.1.refs_0_), channel_id=1, source_target_pairs={{0,16},{1,17},{2,18},{3,19},{4,20},{5,21},{6,22},{7,23},{8,24},{9,... | collective-permute-start | bytes 98312 | tf_op jit(solution)/shard_map/ppermute | solution.py:254
  12.6 18.3 %collective-permute-start.4 = (f32[8,1024]{1,0:T(8,128)S(1)}, f32[8,1024]{1,0:T(8,128)S(1)}, u32[]{:S(2)}, u32[]{:S(2)}) collective-permute-start(f32[8,1024]{1,0:T(8,128)S(1)} %block_stats.1.refs_0_), channel_id=1, source_target_pairs={{0,24},{1,25},{2,26},{3,27},{4,28},{5,29},{6,30},{7,31},{8,0},{9,1... | collective-permute-start | bytes 98312 | tf_op jit(solution)/shard_map/ppermute | solution.py:254
  30.9 5.3 %collective-permute-start.8 = (f32[256,1024]{1,0:T(8,128)S(1)}, f32[256,1024]{1,0:T(8,128)S(1)}, u32[]{:S(2)}, u32[]{:S(2)}) collective-permute-start(f32[256,1024]{1,0:T(8,128)S(1)} %collective-permute-done.7.refs_2_), channel_id=1, source_target_pairs={{0,2},{1,3},{2,0},{3,1},{4,6},{5,7},{6,4},{7,5},{8,10},{9,11},{10,... | collective-permute-start | bytes 3145736 | tf_op jit(solution)/shard_map/ppermute | solution.py:254
  31.0 27.8 %collective-permute-start.18 = (f32[256,1024]{1,0:T(8,128)S(1)}, f32[256,1024]{1,0:T(8,128)S(1)}, u32[]{:S(2)}, u32[]{:S(2)}) collective-permute-start(f32[256,1024]{1,0:T(8,128)S(1)} %collective-permute-done.6.refs_4_), channel_id=1, source_target_pairs={{0,8},{1,9},{2,26},{3,27},{4,12},{5,13},{6,30},{7,31},{8,16},{9,17... | collective-permute-start | bytes 3145736 | tf_op jit(solution)/shard_map/ppermute | solution.py:254
  32.3 3.9 %collective-permute-start.5 = (f32[8,1024]{1,0:T(8,128)S(1)}, f32[8,1024]{1,0:T(8,128)S(1)}, u32[]{:S(2)}, u32[]{:S(2)}) collective-permute-start(f32[8,1024]{1,0:T(8,128)S(1)} %merge.2.refs_0_), channel_id=1, source_target_pairs={{0,4},{1,5},{2,6},{3,7},{4,0},{5,1},{6,2},{7,3},{8,12},{9,13},{10,... | collective-permute-start | bytes 98312 | tf_op jit(solution)/shard_map/ppermute | solution.py:254
  38.1 11.6 %collective-permute-start.10 = (f32[256,256]{1,0:T(8,128)S(1)}, f32[256,256]{1,0:T(8,128)S(1)}, u32[]{:S(2)}, u32[]{:S(2)}) collective-permute-start(f32[256,256]{1,0:T(8,128)S(1)} %get-tuple-element.29), channel_id=1, source_target_pairs={{0,7},{1,5},{2,4},{3,6},{4,3},{5,1},{6,0},{7,2},{8,14},{9,12},{10,... | collective-permute-start | bytes 786440 | tf_op jit(solution)/shard_map/ppermute | solution.py:254
  42.2 8.7 %collective-permute-start.11 = (f32[256,256]{1,0:T(8,128)S(1)}, f32[256,256]{1,0:T(8,128)S(1)}, u32[]{:S(2)}, u32[]{:S(2)}) collective-permute-start(f32[256,256]{1,0:T(8,128)S(1)} %get-tuple-element.30), channel_id=1, source_target_pairs={{0,1},{1,3},{2,2},{3,0},{4,5},{5,7},{6,6},{7,4},{8,8},{9,10},{10,1... | collective-permute-start | bytes 786440 | tf_op jit(solution)/shard_map/ppermute | solution.py:254
  44.1 11.4 %collective-permute-start.12 = (f32[256,256]{1,0:T(8,128)S(1)}, f32[256,256]{1,0:T(8,128)S(1)}, u32[]{:S(2)}, u32[]{:S(2)}) collective-permute-start(f32[256,256]{1,0:T(8,128)S(1)} %get-tuple-element.31), channel_id=1, source_target_pairs={{0,3},{1,1},{2,0},{3,2},{4,7},{5,5},{6,4},{7,6},{8,10},{9,8},{10,9... | collective-permute-start | bytes 786440 | tf_op jit(solution)/shard_map/ppermute | solution.py:254
  47.8 11.0 %copy-start.2 = (s32[32,16]{1,0:T(8,128)S(1)}, s32[32,16]{1,0:T(8,128)}, u32[]{:S(2)}) copy-start(s32[32,16]{1,0:T(8,128)} %constant.19.clone.table_ref) | copy-start | bytes 6148
  47.8 8.7 %collective-permute-start.9 = (f32[256,256]{1,0:T(8,128)S(1)}, f32[256,256]{1,0:T(8,128)S(1)}, u32[]{:S(2)}, u32[]{:S(2)}) collective-permute-start(f32[256,256]{1,0:T(8,128)S(1)} %get-tuple-element.28), channel_id=1, source_target_pairs={{0,5},{1,7},{2,6},{3,4},{4,1},{5,3},{6,2},{7,0},{8,12},{9,14},{10,... | collective-permute-start | bytes 786440 | tf_op jit(solution)/shard_map/ppermute | solution.py:254
  56.5 26.0 %collective-permute-start.13 = (f32[256,1024]{1,0:T(8,128)S(1)}, f32[256,1024]{1,0:T(8,128)S(1)}, u32[]{:S(2)}, u32[]{:S(2)}) collective-permute-start(f32[256,1024]{1,0:T(8,128)S(1)} %copy-done.1), channel_id=1, source_target_pairs={{0,24},{1,25},{2,10},{3,11},{4,28},{5,29},{6,14},{7,15},{8,0},{9,1... | collective-permute-start | bytes 3145736 | tf_op jit(solution)/shard_map/ppermute | solution.py:254
  61.5 23.8 %collective-permute-start.19 = (f32[512,256]{1,0:T(8,128)S(1)}, f32[512,256]{1,0:T(8,128)S(1)}, u32[]{:S(2)}, u32[]{:S(2)}) collective-permute-start(f32[512,256]{1,0:T(8,128)S(1)} %get-tuple-element.42), channel_id=1, source_target_pairs={{0,1},{1,0},{2,3},{3,2},{4,5},{5,4},{6,7},{7,6},{8,9},{9,8},{10,11... | collective-permute-start | bytes 1572872 | tf_op jit(solution)/shard_map/ppermute | solution.py:254
  63.0 28.4 %collective-permute-start.20 = (f32[512,256]{1,0:T(8,128)S(1)}, f32[512,256]{1,0:T(8,128)S(1)}, u32[]{:S(2)}, u32[]{:S(2)}) collective-permute-start(f32[512,256]{1,0:T(8,128)S(1)} %get-tuple-element.44), channel_id=1, source_target_pairs={{0,4},{1,5},{2,6},{3,7},{4,0},{5,1},{6,2},{7,3},{8,12},{9,13},{10,... | collective-permute-start | bytes 1572872 | tf_op jit(solution)/shard_map/ppermute | solution.py:254
  64.5 28.8 %collective-permute-start.21 = (f32[512,256]{1,0:T(8,128)S(1)}, f32[512,256]{1,0:T(8,128)S(1)}, u32[]{:S(2)}, u32[]{:S(2)}) collective-permute-start(f32[512,256]{1,0:T(8,128)S(1)} %get-tuple-element.45), channel_id=1, source_target_pairs={{0,5},{1,4},{2,7},{3,6},{4,1},{5,0},{6,3},{7,2},{8,13},{9,12},{10,... | collective-permute-start | bytes 1572872 | tf_op jit(solution)/shard_map/ppermute | solution.py:254
  85.3 9.0 %collective-permute-start.14 = (f32[256,256]{1,0:T(8,128)S(1)}, f32[256,256]{1,0:T(8,128)S(1)}, u32[]{:S(2)}, u32[]{:S(2)}) collective-permute-start(f32[256,256]{1,0:T(8,128)S(1)} %get-tuple-element.36), channel_id=1, source_target_pairs={{0,4},{1,6},{2,7},{3,5},{4,0},{5,2},{6,3},{7,1},{8,13},{9,15},{10,... | collective-permute-start | bytes 786440 | tf_op jit(solution)/shard_map/ppermute | solution.py:254
  85.3 14.5 %collective-permute-start.15 = (f32[256,256]{1,0:T(8,128)}, f32[256,256]{1,0:T(8,128)}, u32[]{:S(2)}, u32[]{:S(2)}) collective-permute-start(f32[256,256]{1,0:T(8,128)} %get-tuple-element.37), channel_id=1, source_target_pairs={{0,6},{1,4},{2,5},{3,7},{4,2},{5,0},{6,1},{7,3},{8,15},{9,13},{10,... | collective-permute-start | bytes 786440 | tf_op jit(solution)/shard_map/ppermute | solution.py:254
  87.8 12.0 %collective-permute-start.16 = (f32[256,256]{1,0:T(8,128)}, f32[256,256]{1,0:T(8,128)}, u32[]{:S(2)}, u32[]{:S(2)}) collective-permute-start(f32[256,256]{1,0:T(8,128)} %get-tuple-element.38), channel_id=1, source_target_pairs={{0,0},{1,2},{2,3},{3,1},{4,4},{5,6},{6,7},{7,5},{8,9},{9,11},{10,1... | collective-permute-start | bytes 786440 | tf_op jit(solution)/shard_map/ppermute | solution.py:254
  91.4 10.6 %collective-permute-start.17 = (f32[256,256]{1,0:T(8,128)}, f32[256,256]{1,0:T(8,128)}, u32[]{:S(2)}, u32[]{:S(2)}) collective-permute-start(f32[256,256]{1,0:T(8,128)} %get-tuple-element.39), channel_id=1, source_target_pairs={{0,2},{1,0},{2,1},{3,3},{4,6},{5,4},{6,5},{7,7},{8,11},{9,9},{10,8... | collective-permute-start | bytes 786440 | tf_op jit(solution)/shard_map/ppermute | solution.py:254
  94.2 7.8 %collective-permute-start.22 = (f32[256,256]{1,0:T(8,128)}, f32[256,256]{1,0:T(8,128)}, u32[]{:S(2)}, u32[]{:S(2)}) collective-permute-start(f32[256,256]{1,0:T(8,128)} %get-tuple-element.46), channel_id=1, source_target_pairs={{0,2},{1,3},{2,0},{3,1},{4,6},{5,7},{6,4},{7,5},{8,10},{9,11},{10,... | collective-permute-start | bytes 786440 | tf_op jit(solution)/shard_map/ppermute | solution.py:254
  94.3 7.8 %collective-permute-start.23 = (f32[256,256]{1,0:T(8,128)}, f32[256,256]{1,0:T(8,128)}, u32[]{:S(2)}, u32[]{:S(2)}) collective-permute-start(f32[256,256]{1,0:T(8,128)} %get-tuple-element.47), channel_id=1, source_target_pairs={{0,2},{1,3},{2,0},{3,1},{4,6},{5,7},{6,4},{7,5},{8,10},{9,11},{10,... | collective-permute-start | bytes 786440 | tf_op jit(solution)/shard_map/ppermute | solution.py:254

commit v6 on v5

--- a/solution.py
+++ b/solution.py
@@ -258,10 +258,11 @@
     core_rows = send(log_derivs, over_core)
     one = send(log_derivs, ring)
 
-    side_rows = send(log_derivs, over_side)
 
     coefficients = coefficients[None, :]
-    stats = block_stats(log_derivs, core_rows, coefficients, send(coefficients, over_core))
+    other_coefficients = send(coefficients, over_core)
+    side_rows = send(after(log_derivs, other_coefficients), over_side)
+    stats = block_stats(log_derivs, core_rows, coefficients, other_coefficients)
     stats = merge(stats, *[send(stats, turn) for turn in turns])
     one, side_rows = lax.optimization_barrier((one, side_rows, stats))[:2]
     two = send(one, ring)
@@ -285,6 +286,7 @@
         *all_rows,
         after(log_derivs, out[0]),
     )
+    near = [after(piece, *near[1]) for piece in near[0]], near[1]
     three = send(after(log_derivs, *near[1], *near[0], *own_level), back)
     two = after(two, *near[1], *near[0], *own_level)
     keep_own, keep_side, sent_own, sent_side = kernel_call(

time: 105 us -> 104 us (level)
  no operation moved by 1% of the time
where the time goes in v6:
time: 104 us
  waiting for transfers between devices  50.2 us (48%)
  starting transfers between devices  34.9 us (34%)
  Pallas kernels  15.4 us (15%)
  local copies, waits for them, and re-layouts  1.94 us (2%)
    ppermute x24, waiting for transfers between devices, send(): return lax.ppermute(value, BOTH, pairs)  50.2 us
    ppermute x24, starting transfers between devices, send(): return lax.ppermute(value, BOTH, pairs)  34.9 us
    pallas_call x8, Pallas kernels, kernel_call(): pl.pallas_call(kernel, out_shape=[jax.ShapeDtypeStruct(s, jnp.float32) fo...  11.3 us
    pallas_call x2, Pallas kernels, place(): pl.pallas_call(functools.partial(place_kernel, planes, [len(terms) for te...  4.12 us
  transfers between devices with their start and end apart: 24, of which 10 were waited for; matrix products, arithmetic and copies ran while one was open for 1% of the time, Pallas kernels for 13%

profile of v6, /device:TPU:0, one launch (start us, length us, event | category | flops | bytes accessed | tf_op | source)
XLA Modules:
  0.0 103.8 jit_solution(3609661741398089544)
XLA Ops:
  1.2 3.0 %collective-permute-start.6 = (f32[256,1024]{1,0:T(8,128)}, f32[256,1024]{1,0:T(8,128)S(1)}, u32[]{:S(2)}, u32[]{:S(2)}) collective-permute-start(f32[256,1024]{1,0:T(8,128)} %refs_0_.7), channel_id=1, source_target_pairs={{0,8},{1,9},{2,26},{3,27},{4,12},{5,13},{6,30},{7,31},{8,16},{9,17... | collective-permute-start | bytes 3145736 | tf_op jit(solution)/shard_map/ppermute | solution.py:254
  4.2 2.3 %collective-permute-start.7 = (f32[256,1024]{1,0:T(8,128)}, f32[256,1024]{1,0:T(8,128)S(1)}, u32[]{:S(2)}, u32[]{:S(2)}) collective-permute-start(f32[256,1024]{1,0:T(8,128)} %refs_0_.7), channel_id=1, source_target_pairs={{0,4},{1,5},{2,6},{3,7},{4,0},{5,1},{6,2},{7,3},{8,12},{9,13},{10,... | collective-permute-start | bytes 3145736 | tf_op jit(solution)/shard_map/ppermute | solution.py:254
  6.5 1.3 %copy-done = f32[256,1024]{1,0:T(8,128)S(1)} copy-done((f32[256,1024]{1,0:T(8,128)S(1)}, f32[256,1024]{1,0:T(8,128)}, u32[]{:S(2)}) %copy-start) | copy-done | bytes 1048600
  8.4 1.2 %block_stats.1.refs_0_ = f32[8,1024]{1,0:T(8,128)S(1)} custom-call(f32[256,1024]{1,0:T(8,128)S(1)} %copy-done, f32[256,1024]{1,0:T(8,128)S(1)} %collective-permute-done.other_ref.refs_1_, f32[1,256]{1,0:T(1,128)S(1)} %bitcast.4, f32[1,256]{1,0:T(1,128)S(1)} %collective-permute-done.1.other_coef_ref), custom_call_target="tpu_custom_call" | custom-call | tf_op jit(solution)/shard_map/block_stats/pallas_call | solution.py:140
  9.6 1.6 %collective-permute-start.2 = (f32[8,1024]{1,0:T(8,128)S(1)}, f32[8,1024]{1,0:T(8,128)S(1)}, u32[]{:S(2)}, u32[]{:S(2)}) collective-permute-start(f32[8,1024]{1,0:T(8,128)S(1)} %block_stats.1.refs_0_), channel_id=1, source_target_pairs={{0,8},{1,9},{2,10},{3,11},{4,12},{5,13},{6,14},{7,15},{8,16},{9,17... | collective-permute-start | bytes 98312 | tf_op jit(solution)/shard_map/ppermute | solution.py:254
  11.2 2.6 %collective-permute-start.3 = (f32[8,1024]{1,0:T(8,128)S(1)}, f32[8,1024]{1,0:T(8,128)S(1)}, u32[]{:S(2)}, u32[]{:S(2)}) collective-permute-start(f32[8,1024]{1,0:T(8,128)S(1)} %block_stats.1.refs_0_), channel_id=1, source_target_pairs={{0,16},{1,17},{2,18},{3,19},{4,20},{5,21},{6,22},{7,23},{8,24},{9,... | collective-permute-start | bytes 98312 | tf_op jit(solution)/shard_map/ppermute | solution.py:254
  13.8 1.3 %collective-permute-start.4 = (f32[8,1024]{1,0:T(8,128)S(1)}, f32[8,1024]{1,0:T(8,128)S(1)}, u32[]{:S(2)}, u32[]{:S(2)}) collective-permute-start(f32[8,1024]{1,0:T(8,128)S(1)} %block_stats.1.refs_0_), channel_id=1, source_target_pairs={{0,24},{1,25},{2,26},{3,27},{4,28},{5,29},{6,30},{7,31},{8,0},{9,1... | collective-permute-start | bytes 98312 | tf_op jit(solution)/shard_map/ppermute | solution.py:254
  15.2 15.9 %collective-permute-done.2.refs_1_ = f32[8,1024]{1,0:T(8,128)S(1)} collective-permute-done((f32[8,1024]{1,0:T(8,128)S(1)}, f32[8,1024]{1,0:T(8,128)S(1)}, u32[]{:S(2)}, u32[]{:S(2)}) %collective-permute-start.2) | collective-permute-done | bytes 32800 | tf_op jit(solution)/shard_map/ppermute | solution.py:254
  31.3 1.3 %collective-permute-start.18 = (f32[256,1024]{1,0:T(8,128)S(1)}, f32[256,1024]{1,0:T(8,128)S(1)}, u32[]{:S(2)}, u32[]{:S(2)}) collective-permute-start(f32[256,1024]{1,0:T(8,128)S(1)} %collective-permute-done.6.refs_4_), channel_id=1, source_target_pairs={{0,8},{1,9},{2,26},{3,27},{4,12},{5,13},{6,30},{7,31},{8,16},{9,17... | collective-permute-start | bytes 3145736 | tf_op jit(solution)/shard_map/ppermute | solution.py:254
  32.6 1.5 %collective-permute-start.5 = (f32[8,1024]{1,0:T(8,128)S(1)}, f32[8,1024]{1,0:T(8,128)S(1)}, u32[]{:S(2)}, u32[]{:S(2)}) collective-permute-start(f32[8,1024]{1,0:T(8,128)S(1)} %merge.2.refs_0_), channel_id=1, source_target_pairs={{0,4},{1,5},{2,6},{3,7},{4,0},{5,1},{6,2},{7,3},{8,12},{9,13},{10,... | collective-permute-start | bytes 98312 | tf_op jit(solution)/shard_map/ppermute | solution.py:254
  34.1 2.4 %collective-permute-done.5.refs_1_ = f32[8,1024]{1,0:T(8,128)S(1)} collective-permute-done((f32[8,1024]{1,0:T(8,128)S(1)}, f32[8,1024]{1,0:T(8,128)S(1)}, u32[]{:S(2)}, u32[]{:S(2)}) %collective-permute-start.5) | collective-permute-done | bytes 32800 | tf_op jit(solution)/shard_map/ppermute | solution.py:254
  36.5 1.9 %products_near.1 = (f32[256,256]{1,0:T(8,128)S(1)}, f32[256,256]{1,0:T(8,128)S(1)}, f32[256,256]{1,0:T(8,128)S(1)}, f32[256,256]{1,0:T(8,128)S(1)}) custom-call(f32[8,1024]{1,0:T(8,128)S(1)} %merge.3.mean_ref, f32[256,1024]{1,0:T(8,128)S(1)} %copy-done.1, f32[256,1024]{1,0:T(8,128)S(1)} %collective-permute-done.other_ref.refs_1_, ...), custom_call_target="tpu_custom_call" | custom-call | tf_op jit(solution)/shard_map/products_near/pallas_call | solution.py:140
  38.4 4.2 %collective-permute-start.10 = (f32[256,256]{1,0:T(8,128)S(1)}, f32[256,256]{1,0:T(8,128)S(1)}, u32[]{:S(2)}, u32[]{:S(2)}) collective-permute-start(f32[256,256]{1,0:T(8,128)S(1)} %get-tuple-element.33), channel_id=1, source_target_pairs={{0,7},{1,5},{2,4},{3,6},{4,3},{5,1},{6,0},{7,2},{8,14},{9,12},{10,... | collective-permute-start | bytes 786440 | tf_op jit(solution)/shard_map/ppermute | solution.py:254
  42.7 2.1 %collective-permute-start.12 = (f32[256,256]{1,0:T(8,128)S(1)}, f32[256,256]{1,0:T(8,128)S(1)}, u32[]{:S(2)}, u32[]{:S(2)}) collective-permute-start(f32[256,256]{1,0:T(8,128)S(1)} %get-tuple-element.36), channel_id=1, source_target_pairs={{0,3},{1,1},{2,0},{3,2},{4,7},{5,5},{6,4},{7,6},{8,10},{9,8},{10,9... | collective-permute-start | bytes 786440 | tf_op jit(solution)/shard_map/ppermute | solution.py:254
  44.9 2.6 %collective-permute-start.11 = (f32[256,256]{1,0:T(8,128)S(1)}, f32[256,256]{1,0:T(8,128)S(1)}, u32[]{:S(2)}, u32[]{:S(2)}) collective-permute-start(f32[256,256]{1,0:T(8,128)S(1)} %get-tuple-element.34), channel_id=1, source_target_pairs={{0,1},{1,3},{2,2},{3,0},{4,5},{5,7},{6,6},{7,4},{8,8},{9,10},{10,1... | collective-permute-start | bytes 786440 | tf_op jit(solution)/shard_map/ppermute | solution.py:254
  47.5 1.9 %products_level.1 = (f32[512,256]{1,0:T(8,128)S(1)}, f32[512,256]{1,0:T(8,128)S(1)}) custom-call(f32[8,1024]{1,0:T(8,128)S(1)} %merge.3.mean_ref, f32[256,1024]{1,0:T(8,128)S(1)} %copy-done.1, f32[256,1024]{1,0:T(8,128)S(1)} %collective-permute-done.other_ref.refs_1_, f32[256,1024]{1,0:T(8,128)S(1)} %collective-permute-done.7.refs_2_, ...), custom_call_target="tpu_custom_call" | custom-call | tf_op jit(solution)/shard_map/products_level/pallas_call | solution.py:140
  49.4 2.8 %collective-permute-done.12.refs_1_ = f32[256,256]{1,0:T(8,128)S(1)} collective-permute-done((f32[256,256]{1,0:T(8,128)S(1)}, f32[256,256]{1,0:T(8,128)S(1)}, u32[]{:S(2)}, u32[]{:S(2)}) %collective-permute-start.12) | collective-permute-done | bytes 262176 | tf_op jit(solution)/shard_map/ppermute | solution.py:254
  52.2 2.1 %collective-permute-done.9.refs_2_ = f32[256,256]{1,0:T(8,128)S(1)} collective-permute-done((f32[256,256]{1,0:T(8,128)S(1)}, f32[256,256]{1,0:T(8,128)S(1)}, u32[]{:S(2)}, u32[]{:S(2)}) %collective-permute-start.9) | collective-permute-done | bytes 262176 | tf_op jit(solution)/shard_map/ppermute | solution.py:254
  54.3 2.0 %collective-permute-done.11.refs_0_ = f32[256,256]{1,0:T(8,128)S(1)} collective-permute-done((f32[256,256]{1,0:T(8,128)S(1)}, f32[256,256]{1,0:T(8,128)S(1)}, u32[]{:S(2)}, u32[]{:S(2)}) %collective-permute-start.11) | collective-permute-done | bytes 262176 | tf_op jit(solution)/shard_map/ppermute | solution.py:254
  56.3 3.2 %collective-permute-done.18.refs_4_ = f32[256,1024]{1,0:T(8,128)S(1)} collective-permute-done((f32[256,1024]{1,0:T(8,128)S(1)}, f32[256,1024]{1,0:T(8,128)S(1)}, u32[]{:S(2)}, u32[]{:S(2)}) %collective-permute-start.18) | collective-permute-done | bytes 1048608 | tf_op jit(solution)/shard_map/ppermute | solution.py:254
  59.5 2.7 %products_across.1 = (f32[512,256]{1,0:T(8,128)S(1)}, f32[512,256]{1,0:T(8,128)S(1)}, f32[512,256]{1,0:T(8,128)S(1)}, f32[512,256]{1,0:T(8,128)S(1)}) custom-call(s32[32,16]{1,0:T(8,128)S(1)} %copy-done.2, f32[8,1024]{1,0:T(8,128)S(1)} %merge.3.mean_ref, f32[256,1024]{1,0:T(8,128)S(1)} %copy-done.1, f32[256,1024]{1,0:T(8,128)S(1)} %collective-permute-done.other_ref.refs_1_, ...), custom_call_target="tpu_custom_call" | custom-call | flops 4000000000 | tf_op jit(solution)/shard_map/products_across/pallas_call | solution.py:140
  62.2 1.6 %collective-permute-start.19 = (f32[512,256]{1,0:T(8,128)S(1)}, f32[512,256]{1,0:T(8,128)S(1)}, u32[]{:S(2)}, u32[]{:S(2)}) collective-permute-start(f32[512,256]{1,0:T(8,128)S(1)} %get-tuple-element.48), channel_id=1, source_target_pairs={{0,1},{1,0},{2,3},{3,2},{4,5},{5,4},{6,7},{7,6},{8,9},{9,8},{10,11... | collective-permute-start | bytes 1572872 | tf_op jit(solution)/shard_map/ppermute | solution.py:254
  63.8 1.5 %collective-permute-start.20 = (f32[512,256]{1,0:T(8,128)S(1)}, f32[512,256]{1,0:T(8,128)S(1)}, u32[]{:S(2)}, u32[]{:S(2)}) collective-permute-start(f32[512,256]{1,0:T(8,128)S(1)} %get-tuple-element.50), channel_id=1, source_target_pairs={{0,4},{1,5},{2,6},{3,7},{4,0},{5,1},{6,2},{7,3},{8,12},{9,13},{10,... | collective-permute-start | bytes 1572872 | tf_op jit(solution)/shard_map/ppermute | solution.py:254
  65.8 16.1 %collective-permute-done.13.refs_4_ = f32[256,1024]{1,0:T(8,128)S(1)} collective-permute-done((f32[256,1024]{1,0:T(8,128)S(1)}, f32[256,1024]{1,0:T(8,128)S(1)}, u32[]{:S(2)}, u32[]{:S(2)}) %collective-permute-start.13) | collective-permute-done | bytes 1048608 | tf_op jit(solution)/shard_map/ppermute | solution.py:254
  81.8 2.7 %products_far.1 = (f32[256,256]{1,0:T(8,128)S(1)}, f32[256,256]{1,0:T(8,128)}, f32[256,256]{1,0:T(8,128)}, f32[256,256]{1,0:T(8,128)}) custom-call(f32[8,1024]{1,0:T(8,128)S(1)} %merge.3.mean_ref, f32[256,1024]{1,0:T(8,128)S(1)} %copy-done.1, f32[256,1024]{1,0:T(8,128)S(1)} %collective-permute-done.other_ref.refs_1_, ...), custom_call_target="tpu_custom_call" | custom-call | tf_op jit(solution)/shard_map/products_far/pallas_call | solution.py:140
  84.6 1.4 %collective-permute-start.14 = (f32[256,256]{1,0:T(8,128)S(1)}, f32[256,256]{1,0:T(8,128)S(1)}, u32[]{:S(2)}, u32[]{:S(2)}) collective-permute-start(f32[256,256]{1,0:T(8,128)S(1)} %get-tuple-element.42), channel_id=1, source_target_pairs={{0,4},{1,6},{2,7},{3,5},{4,0},{5,2},{6,3},{7,1},{8,13},{9,15},{10,... | collective-permute-start | bytes 786440 | tf_op jit(solution)/shard_map/ppermute | solution.py:254
  86.2 3.6 %collective-permute-start.16 = (f32[256,256]{1,0:T(8,128)}, f32[256,256]{1,0:T(8,128)}, u32[]{:S(2)}, u32[]{:S(2)}) collective-permute-start(f32[256,256]{1,0:T(8,128)} %get-tuple-element.44), channel_id=1, source_target_pairs={{0,0},{1,2},{2,3},{3,1},{4,4},{5,6},{6,7},{7,5},{8,9},{9,11},{10,1... | collective-permute-start | bytes 786440 | tf_op jit(solution)/shard_map/ppermute | solution.py:254
  89.8 2.0 %collective-permute-start.17 = (f32[256,256]{1,0:T(8,128)}, f32[256,256]{1,0:T(8,128)}, u32[]{:S(2)}, u32[]{:S(2)}) collective-permute-start(f32[256,256]{1,0:T(8,128)} %get-tuple-element.45), channel_id=1, source_target_pairs={{0,2},{1,0},{2,1},{3,3},{4,6},{5,4},{6,5},{7,7},{8,11},{9,9},{10,8... | collective-permute-start | bytes 786440 | tf_op jit(solution)/shard_map/ppermute | solution.py:254
  93.7 1.8 %place_most.1.refs_6_ = f32[256,2048]{1,0:T(8,128)} custom-call(s32[32,16]{1,0:T(8,128)S(1)} %copy-done.2, f32[256,256]{1,0:T(8,128)S(1)} %collective-permute-done.11.refs_0_, f32[256,256]{1,0:T(8,128)S(1)} %collective-permute-done.12.refs_1_, f32[256,256]{1,0:T(8,128)S(1)} %collective-permute-done.9.refs_2_, ...), custom_call_target="tpu_custom_call" | custom-call | tf_op jit(solution)/shard_map/place_most/pallas_call | solution.py:182
  96.1 3.3 %collective-permute-done.15.refs_1_ = f32[256,256]{1,0:T(8,128)} collective-permute-done((f32[256,256]{1,0:T(8,128)}, f32[256,256]{1,0:T(8,128)}, u32[]{:S(2)}, u32[]{:S(2)}) %collective-permute-start.15) | collective-permute-done | bytes 262176 | tf_op jit(solution)/shard_map/ppermute | solution.py:254
  99.4 2.1 %collective-permute-done.17.refs_3_ = f32[256,256]{1,0:T(8,128)} collective-permute-done((f32[256,256]{1,0:T(8,128)}, f32[256,256]{1,0:T(8,128)}, u32[]{:S(2)}, u32[]{:S(2)}) %collective-permute-start.17) | collective-permute-done | bytes 262176 | tf_op jit(solution)/shard_map/ppermute | solution.py:254
  101.5 2.3 %place_last.1 = f32[256,2048]{1,0:T(8,128)} custom-call(s32[32,16]{1,0:T(8,128)S(1)} %copy-done.2, f32[256,256]{1,0:T(8,128)S(1)} %collective-permute-done.14.refs_0_, f32[256,256]{1,0:T(8,128)} %collective-permute-done.15.refs_1_, f32[256,256]{1,0:T(8,128)} %collective-permute-done.16.refs_2_, ...), custom_call_target="tpu_custom_call", output_to_operand_aliasing={{}: (7, {})} | custom-call | tf_op jit(solution)/shard_map/place_last/pallas_call | solution.py:182
  (35 shorter events, 4.8 us)
Async XLA Ops:
  0.6 5.9 %collective-permute-start = (f32[256,1024]{1,0:T(8,128)}, f32[256,1024]{1,0:T(8,128)S(1)}, u32[]{:S(2)}, u32[]{:S(2)}) collective-permute-start(f32[256,1024]{1,0:T(8,128)} %refs_0_.7), channel_id=1, source_target_pairs={{0,2},{1,3},{2,0},{3,1},{4,6},{5,7},{6,4},{7,5},{8,10},{9,11},{10,... | collective-permute-start | bytes 3145736 | tf_op jit(solution)/shard_map/ppermute | solution.py:254
  1.1 3.1 %collective-permute-start.1 = (f32[1,256]{1,0:T(1,128)}, f32[1,256]{1,0:T(1,128)S(1)}, u32[]{:S(2)}, u32[]{:S(2)}) collective-permute-start(f32[1,256]{1,0:T(1,128)} %bitcast.3), channel_id=1, source_target_pairs={{0,2},{1,3},{2,0},{3,1},{4,6},{5,7},{6,4},{7,5},{8,10},{9,11},{10,... | collective-permute-start | bytes 3080 | tf_op jit(solution)/shard_map/ppermute | solution.py:254
  1.2 29.9 %collective-permute-start.6 = (f32[256,1024]{1,0:T(8,128)}, f32[256,1024]{1,0:T(8,128)S(1)}, u32[]{:S(2)}, u32[]{:S(2)}) collective-permute-start(f32[256,1024]{1,0:T(8,128)} %refs_0_.7), channel_id=1, source_target_pairs={{0,8},{1,9},{2,26},{3,27},{4,12},{5,13},{6,30},{7,31},{8,16},{9,17... | collective-permute-start | bytes 3145736 | tf_op jit(solution)/shard_map/ppermute | solution.py:254
  4.2 26.9 %collective-permute-start.7 = (f32[256,1024]{1,0:T(8,128)}, f32[256,1024]{1,0:T(8,128)S(1)}, u32[]{:S(2)}, u32[]{:S(2)}) collective-permute-start(f32[256,1024]{1,0:T(8,128)} %refs_0_.7), channel_id=1, source_target_pairs={{0,4},{1,5},{2,6},{3,7},{4,0},{5,1},{6,2},{7,3},{8,12},{9,13},{10,... | collective-permute-start | bytes 3145736 | tf_op jit(solution)/shard_map/ppermute | solution.py:254
  6.5 1.3 %copy-start = (f32[256,1024]{1,0:T(8,128)S(1)}, f32[256,1024]{1,0:T(8,128)}, u32[]{:S(2)}) copy-start(f32[256,1024]{1,0:T(8,128)} %refs_0_.7) | copy-start | bytes 3145732
  7.8 0.7 copy-start.3
  8.4 28.1 %copy-start.1 = (f32[256,1024]{1,0:T(8,128)S(1)}, f32[256,1024]{1,0:T(8,128)}, u32[]{:S(2)}) copy-start(f32[256,1024]{1,0:T(8,128)} %refs_0_.7) | copy-start | bytes 3145732
  9.6 21.5 %collective-permute-start.2 = (f32[8,1024]{1,0:T(8,128)S(1)}, f32[8,1024]{1,0:T(8,128)S(1)}, u32[]{:S(2)}, u32[]{:S(2)}) collective-permute-start(f32[8,1024]{1,0:T(8,128)S(1)} %block_stats.1.refs_0_), channel_id=1, source_target_pairs={{0,8},{1,9},{2,10},{3,11},{4,12},{5,13},{6,14},{7,15},{8,16},{9,17... | collective-permute-start | bytes 98312 | tf_op jit(solution)/shard_map/ppermute | solution.py:254
  11.2 19.9 %collective-permute-start.3 = (f32[8,1024]{1,0:T(8,128)S(1)}, f32[8,1024]{1,0:T(8,128)S(1)}, u32[]{:S(2)}, u32[]{:S(2)}) collective-permute-start(f32[8,1024]{1,0:T(8,128)S(1)} %block_stats.1.refs_0_), channel_id=1, source_target_pairs={{0,16},{1,17},{2,18},{3,19},{4,20},{5,21},{6,22},{7,23},{8,24},{9,... | collective-permute-start | bytes 98312 | tf_op jit(solution)/shard_map/ppermute | solution.py:254
  13.8 17.3 %collective-permute-start.4 = (f32[8,1024]{1,0:T(8,128)S(1)}, f32[8,1024]{1,0:T(8,128)S(1)}, u32[]{:S(2)}, u32[]{:S(2)}) collective-permute-start(f32[8,1024]{1,0:T(8,128)S(1)} %block_stats.1.refs_0_), channel_id=1, source_target_pairs={{0,24},{1,25},{2,26},{3,27},{4,28},{5,29},{6,30},{7,31},{8,0},{9,1... | collective-permute-start | bytes 98312 | tf_op jit(solution)/shard_map/ppermute | solution.py:254
  31.1 5.4 %collective-permute-start.8 = (f32[256,1024]{1,0:T(8,128)S(1)}, f32[256,1024]{1,0:T(8,128)S(1)}, u32[]{:S(2)}, u32[]{:S(2)}) collective-permute-start(f32[256,1024]{1,0:T(8,128)S(1)} %collective-permute-done.7.refs_2_), channel_id=1, source_target_pairs={{0,2},{1,3},{2,0},{3,1},{4,6},{5,7},{6,4},{7,5},{8,10},{9,11},{10,... | collective-permute-start | bytes 3145736 | tf_op jit(solution)/shard_map/ppermute | solution.py:254
  31.3 28.2 %collective-permute-start.18 = (f32[256,1024]{1,0:T(8,128)S(1)}, f32[256,1024]{1,0:T(8,128)S(1)}, u32[]{:S(2)}, u32[]{:S(2)}) collective-permute-start(f32[256,1024]{1,0:T(8,128)S(1)} %collective-permute-done.6.refs_4_), channel_id=1, source_target_pairs={{0,8},{1,9},{2,26},{3,27},{4,12},{5,13},{6,30},{7,31},{8,16},{9,17... | collective-permute-start | bytes 3145736 | tf_op jit(solution)/shard_map/ppermute | solution.py:254
  32.6 3.9 %collective-permute-start.5 = (f32[8,1024]{1,0:T(8,128)S(1)}, f32[8,1024]{1,0:T(8,128)S(1)}, u32[]{:S(2)}, u32[]{:S(2)}) collective-permute-start(f32[8,1024]{1,0:T(8,128)S(1)} %merge.2.refs_0_), channel_id=1, source_target_pairs={{0,4},{1,5},{2,6},{3,7},{4,0},{5,1},{6,2},{7,3},{8,12},{9,13},{10,... | collective-permute-start | bytes 98312 | tf_op jit(solution)/shard_map/ppermute | solution.py:254
  38.4 11.0 %collective-permute-start.10 = (f32[256,256]{1,0:T(8,128)S(1)}, f32[256,256]{1,0:T(8,128)S(1)}, u32[]{:S(2)}, u32[]{:S(2)}) collective-permute-start(f32[256,256]{1,0:T(8,128)S(1)} %get-tuple-element.33), channel_id=1, source_target_pairs={{0,7},{1,5},{2,4},{3,6},{4,3},{5,1},{6,0},{7,2},{8,14},{9,12},{10,... | collective-permute-start | bytes 786440 | tf_op jit(solution)/shard_map/ppermute | solution.py:254
  42.7 9.6 %collective-permute-start.12 = (f32[256,256]{1,0:T(8,128)S(1)}, f32[256,256]{1,0:T(8,128)S(1)}, u32[]{:S(2)}, u32[]{:S(2)}) collective-permute-start(f32[256,256]{1,0:T(8,128)S(1)} %get-tuple-element.36), channel_id=1, source_target_pairs={{0,3},{1,1},{2,0},{3,2},{4,7},{5,5},{6,4},{7,6},{8,10},{9,8},{10,9... | collective-permute-start | bytes 786440 | tf_op jit(solution)/shard_map/ppermute | solution.py:254
  44.8 9.5 %collective-permute-start.9 = (f32[256,256]{1,0:T(8,128)S(1)}, f32[256,256]{1,0:T(8,128)S(1)}, u32[]{:S(2)}, u32[]{:S(2)}) collective-permute-start(f32[256,256]{1,0:T(8,128)S(1)} %get-tuple-element.32), channel_id=1, source_target_pairs={{0,5},{1,7},{2,6},{3,4},{4,1},{5,3},{6,2},{7,0},{8,12},{9,14},{10,... | collective-permute-start | bytes 786440 | tf_op jit(solution)/shard_map/ppermute | solution.py:254
  44.9 14.6 %copy-start.2 = (s32[32,16]{1,0:T(8,128)S(1)}, s32[32,16]{1,0:T(8,128)}, u32[]{:S(2)}) copy-start(s32[32,16]{1,0:T(8,128)} %constant.19.clone.table_ref) | copy-start | bytes 6148
  44.9 11.4 %collective-permute-start.11 = (f32[256,256]{1,0:T(8,128)S(1)}, f32[256,256]{1,0:T(8,128)S(1)}, u32[]{:S(2)}, u32[]{:S(2)}) collective-permute-start(f32[256,256]{1,0:T(8,128)S(1)} %get-tuple-element.34), channel_id=1, source_target_pairs={{0,1},{1,3},{2,2},{3,0},{4,5},{5,7},{6,6},{7,4},{8,8},{9,10},{10,1... | collective-permute-start | bytes 786440 | tf_op jit(solution)/shard_map/ppermute | solution.py:254
  56.3 25.5 %collective-permute-start.13 = (f32[256,1024]{1,0:T(8,128)S(1)}, f32[256,1024]{1,0:T(8,128)S(1)}, u32[]{:S(2)}, u32[]{:S(2)}) collective-permute-start(f32[256,1024]{1,0:T(8,128)S(1)} %copy-done.1), channel_id=1, source_target_pairs={{0,24},{1,25},{2,10},{3,11},{4,28},{5,29},{6,14},{7,15},{8,0},{9,1... | collective-permute-start | bytes 3145736 | tf_op jit(solution)/shard_map/ppermute | solution.py:254
  62.2 23.7 %collective-permute-start.19 = (f32[512,256]{1,0:T(8,128)S(1)}, f32[512,256]{1,0:T(8,128)S(1)}, u32[]{:S(2)}, u32[]{:S(2)}) collective-permute-start(f32[512,256]{1,0:T(8,128)S(1)} %get-tuple-element.48), channel_id=1, source_target_pairs={{0,1},{1,0},{2,3},{3,2},{4,5},{5,4},{6,7},{7,6},{8,9},{9,8},{10,11... | collective-permute-start | bytes 1572872 | tf_op jit(solution)/shard_map/ppermute | solution.py:254
  63.8 26.0 %collective-permute-start.20 = (f32[512,256]{1,0:T(8,128)S(1)}, f32[512,256]{1,0:T(8,128)S(1)}, u32[]{:S(2)}, u32[]{:S(2)}) collective-permute-start(f32[512,256]{1,0:T(8,128)S(1)} %get-tuple-element.50), channel_id=1, source_target_pairs={{0,4},{1,5},{2,6},{3,7},{4,0},{5,1},{6,2},{7,3},{8,12},{9,13},{10,... | collective-permute-start | bytes 1572872 | tf_op jit(solution)/shard_map/ppermute | solution.py:254
  65.3 26.5 %collective-permute-start.21 = (f32[512,256]{1,0:T(8,128)S(1)}, f32[512,256]{1,0:T(8,128)S(1)}, u32[]{:S(2)}, u32[]{:S(2)}) collective-permute-start(f32[512,256]{1,0:T(8,128)S(1)} %get-tuple-element.51), channel_id=1, source_target_pairs={{0,5},{1,4},{2,7},{3,6},{4,1},{5,0},{6,3},{7,2},{8,13},{9,12},{10,... | collective-permute-start | bytes 1572872 | tf_op jit(solution)/shard_map/ppermute | solution.py:254
  84.6 9.1 %collective-permute-start.14 = (f32[256,256]{1,0:T(8,128)S(1)}, f32[256,256]{1,0:T(8,128)S(1)}, u32[]{:S(2)}, u32[]{:S(2)}) collective-permute-start(f32[256,256]{1,0:T(8,128)S(1)} %get-tuple-element.42), channel_id=1, source_target_pairs={{0,4},{1,6},{2,7},{3,5},{4,0},{5,2},{6,3},{7,1},{8,13},{9,15},{10,... | collective-permute-start | bytes 786440 | tf_op jit(solution)/shard_map/ppermute | solution.py:254
  85.9 13.5 %collective-permute-start.15 = (f32[256,256]{1,0:T(8,128)}, f32[256,256]{1,0:T(8,128)}, u32[]{:S(2)}, u32[]{:S(2)}) collective-permute-start(f32[256,256]{1,0:T(8,128)} %get-tuple-element.43), channel_id=1, source_target_pairs={{0,6},{1,4},{2,5},{3,7},{4,2},{5,0},{6,1},{7,3},{8,15},{9,13},{10,... | collective-permute-start | bytes 786440 | tf_op jit(solution)/shard_map/ppermute | solution.py:254
  86.2 13.2 %collective-permute-start.16 = (f32[256,256]{1,0:T(8,128)}, f32[256,256]{1,0:T(8,128)}, u32[]{:S(2)}, u32[]{:S(2)}) collective-permute-start(f32[256,256]{1,0:T(8,128)} %get-tuple-element.44), channel_id=1, source_target_pairs={{0,0},{1,2},{2,3},{3,1},{4,4},{5,6},{6,7},{7,5},{8,9},{9,11},{10,1... | collective-permute-start | bytes 786440 | tf_op jit(solution)/shard_map/ppermute | solution.py:254
  89.8 11.7 %collective-permute-start.17 = (f32[256,256]{1,0:T(8,128)}, f32[256,256]{1,0:T(8,128)}, u32[]{:S(2)}, u32[]{:S(2)}) collective-permute-start(f32[256,256]{1,0:T(8,128)} %get-tuple-element.45), channel_id=1, source_target_pairs={{0,2},{1,0},{2,1},{3,3},{4,6},{5,4},{6,5},{7,7},{8,11},{9,9},{10,8... | collective-permute-start | bytes 786440 | tf_op jit(solution)/shard_map/ppermute | solution.py:254
  92.7 8.8 %collective-permute-start.22 = (f32[256,256]{1,0:T(8,128)}, f32[256,256]{1,0:T(8,128)}, u32[]{:S(2)}, u32[]{:S(2)}) collective-permute-start(f32[256,256]{1,0:T(8,128)} %get-tuple-element.52), channel_id=1, source_target_pairs={{0,2},{1,3},{2,0},{3,1},{4,6},{5,7},{6,4},{7,5},{8,10},{9,11},{10,... | collective-permute-start | bytes 786440 | tf_op jit(solution)/shard_map/ppermute | solution.py:254
  93.7 7.8 %collective-permute-start.23 = (f32[256,256]{1,0:T(8,128)}, f32[256,256]{1,0:T(8,128)}, u32[]{:S(2)}, u32[]{:S(2)}) collective-permute-start(f32[256,256]{1,0:T(8,128)} %get-tuple-element.53), channel_id=1, source_target_pairs={{0,2},{1,3},{2,0},{3,1},{4,6},{5,7},{6,4},{7,5},{8,10},{9,11},{10,... | collective-permute-start | bytes 786440 | tf_op jit(solution)/shard_map/ppermute | solution.py:254

commit v7 on v6

--- a/solution.py
+++ b/solution.py
@@ -2,7 +2,6 @@
 
 import jax
 import jax.numpy as jnp
-import numpy as np
 from jax import lax
 from jax.experimental import pallas as pl
 from jax.experimental.pallas import tpu as pltpu
@@ -86,8 +85,31 @@
     return lax.dot_general(left, right, (((1,), (1,)), ((), ())), preferred_element_type=jnp.float32)
 
 
-def device_row(planes):
-    return lax.axis_index("smp") * planes + lax.axis_index("par")
+def entry(dims, which):
+    levels, planes, block = dims
+    per_plane = levels // planes
+    here, plane = lax.axis_index("smp"), lax.axis_index("par")
+    level, side, core = lax.div(here, 4), lax.rem(lax.div(here, 2), 2), lax.rem(here, 2)
+
+    def off(step, core):
+        return lax.rem(level - step * (1 - 2 * core) + levels, levels)
+
+    def held(z):
+        return lax.div(z, per_plane) == plane
+
+    if which == 0:
+        return held(level)
+    if which >= 9:
+        return held(off(1 if which == 9 else -1, core))
+    if which <= 4:
+        step = 1 if which <= 2 else -1
+        first = held(off(step, 0))
+        z, of_core = jnp.where(first, off(step, 0), off(step, 1)), jnp.where(first, 0, 1)
+    else:
+        z = jnp.where(held(level), level, lax.rem(level + levels // 2, levels))
+        of_core = core if which <= 6 else 1 - core
+    of_side = side if which % 2 == 1 else 1 - side
+    return ((lax.rem(z, per_plane) * 2 + of_side) * 2 + of_core) * block
 
 
 def product_of(row_ref, mean, high, low, scale):
@@ -95,11 +117,11 @@
     return (dot_nt(row_high, high) + (dot_nt(row_high, low) + dot_nt(row_low, high))) * scale
 
 
-def one_level_kernel(scale, mean_ref, *refs):
+def one_level_kernel(scale, dims, flag_at, mean_ref, *refs):
     rows, block, outs = refs[:4], refs[4], refs[5:]
     mean = mean_ref[0:1, :]
     high, low = split(block[...] - mean)
-    straight = lax.axis_index("par") == 0
+    straight = entry(dims, flag_at)
     for k, side in enumerate((1, 0)):
         same = product_of(rows[2 * side], mean, high, low, scale)
         other = product_of(rows[2 * side + 1], mean, high, low, scale)
@@ -116,10 +138,10 @@
         outs[k // 2][k % 2 * height : (k % 2 + 1) * height, :] = product_of(row, mean, high, low, scale)
 
 
-def across_level_kernel(scale, planes, flag_at, table_ref, mean_ref, *refs):
+def across_level_kernel(scale, dims, mean_ref, *refs):
     rows, block, level, outs = refs[:4], refs[4], refs[5:7], refs[7:]
     mean = mean_ref[0:1, :]
-    first = table_ref[device_row(planes), flag_at] == 1
+    first = entry(dims, 0)
     high, low = split(block[...] - mean)
     height = rows[0].shape[0]
     for k, row in enumerate(rows):
@@ -136,12 +158,11 @@
     side[...] = from_side[height:, :] + got_side[height:, :]
 
 
-def kernel_call(kernel, out_shapes, name, *args, smem=0, cost=FREE):
+def kernel_call(kernel, out_shapes, name, *args, cost=FREE):
     return pl.pallas_call(
         kernel,
         out_shape=[jax.ShapeDtypeStruct(s, jnp.float32) for s in out_shapes],
-        in_specs=[pl.BlockSpec(memory_space=pltpu.SMEM)] * smem
-        + [pl.BlockSpec(memory_space=pltpu.VMEM)] * (len(args) - smem),
+        in_specs=[pl.BlockSpec(memory_space=pltpu.VMEM)] * len(args),
         out_specs=[pl.BlockSpec(memory_space=pltpu.VMEM)] * len(out_shapes),
         compiler_params=pltpu.CompilerParams(vmem_limit_bytes=VMEM_LIMIT),
         cost_estimate=cost,
@@ -149,72 +170,62 @@
     )(*args)
 
 
-def place_kernel(planes, summands, columns, aliased, table_ref, *refs):
-    blocks = list(refs[: sum(summands)])
+def place_kernel(dims, apart, summands, columns, aliased, *refs):
+    blocks = list(refs[: sum(map(len, summands))])
     out = refs[len(blocks) + aliased]
-    *totals, sems = refs[len(blocks) + aliased + 1 :]
-    row = device_row(planes)
-    stores = []
-    for total, terms, places in zip(totals, summands, columns):
-        taken, blocks = blocks[:terms], blocks[terms:]
-        if terms > 1:
-            total[...] = taken[0][0 : total.shape[0], :] + taken[1][0 : total.shape[0], :]
-        else:
-            total = taken[0]
+    scratch = list(refs[len(blocks) + aliased + 1 :])
+    sems = scratch.pop()
+    if apart:
+        loads = []
+        for block in blocks:
+            here = scratch.pop(0)
+            loads.append(pltpu.make_async_copy(block.at[pl.ds(0, here.shape[0])], here, sems.at[len(loads)]))
+            loads[-1].start()
+        blocks = [load.dst_ref for load in loads]
+        for load in loads:
+            load.wait()
+    copies = []
+    for total, flags, places in zip(scratch, summands, columns):
+        taken, blocks = blocks[: len(flags)], blocks[len(flags) :]
+        value = 0.0
+        for block, flag_at in zip(taken, flags):
+            part = block[0 : total.shape[0], :]
+            value += part if flag_at is None else jnp.where(entry(dims, flag_at), part, 0.0)
+        total[...] = value
         width = total.shape[1] // len(places)
         for part, (where, offset) in enumerate(places):
-            column = pl.multiple_of((table_ref[row, where] + offset) * 128, 128)
-            stores.append(
-                pltpu.make_async_copy(
-                    total.at[:, pl.ds(part * width, width)], out.at[:, pl.ds(column, width)], sems.at[len(stores)]
-                )
+            column = pl.multiple_of((entry(dims, where) + offset) * 128, 128)
+            copy = pltpu.make_async_copy(
+                total.at[:, pl.ds(part * width, width)],
+                out.at[:, pl.ds(column, width)],
+                sems.at[apart * sum(map(len, summands)) + len(copies)],
             )
-            stores[-1].start()
-    for store in stores:
-        store.wait()
-
-
-def place(table, planes, pieces, shape, into, name):
-    blocks = [block for terms, _ in pieces for block in terms]
+            copy.start()
+            copies.append(copy)
+    for copy in copies:
+        copy.wait()
+
+
+def place(dims, pieces, shape, into, name, apart=False):
+    pieces = [([t if isinstance(t, tuple) else (t, None) for t in terms], places) for terms, places in pieces]
+    blocks = [block for terms, _ in pieces for block, _ in terms]
     columns = [places for _, places in pieces]
     aliased = 0 if into is None else 1
     near, far = pl.BlockSpec(memory_space=pltpu.VMEM), pl.BlockSpec(memory_space=pl.ANY)
+    buffers = [pltpu.VMEM((shape[0], block.shape[1]), jnp.float32) for block in blocks] if apart else []
     return pl.pallas_call(
-        functools.partial(place_kernel, planes, [len(terms) for terms, _ in pieces], columns, aliased),
+        functools.partial(place_kernel, dims, apart, [[flag for _, flag in terms] for terms, _ in pieces], columns, aliased),
         out_shape=jax.ShapeDtypeStruct(shape, jnp.float32),
-        in_specs=[pl.BlockSpec(memory_space=pltpu.SMEM)] + [near] * len(blocks) + [far] * aliased,
+        in_specs=[far if apart else near] * len(blocks) + [far] * aliased,
         out_specs=far,
-        scratch_shapes=[pltpu.VMEM((shape[0], terms[0].shape[1]), jnp.float32) for terms, _ in pieces]
-        + [pltpu.SemaphoreType.DMA((sum(map(len, columns)),))],
-        input_output_aliases={1 + len(blocks): 0} if aliased else {},
+        scratch_shapes=buffers
+        + [pltpu.VMEM((shape[0], terms[0][0].shape[1]), jnp.float32) for terms, _ in pieces]
+        + [pltpu.SemaphoreType.DMA((len(buffers) + sum(map(len, columns)),))],
+        input_output_aliases={len(blocks): 0} if aliased else {},
         compiler_params=pltpu.CompilerParams(vmem_limit_bytes=VMEM_LIMIT),
         cost_estimate=FREE,
         name=name,
-    )(table, *blocks, *([into] if aliased else []))
-
-
-def column_table(levels, planes, block):
-    per_plane = levels // planes
-    table = np.zeros((levels * 4 * planes, 16), np.int32)
-
-    def column(level, side, core):
-        return ((level % per_plane * 2 + side) * 2 + core) * block
-
-    for z in range(levels):
-        for x in range(2):
-            for c in range(2):
-                for y in range(planes):
-                    row = [int(z // per_plane == y)]
-                    for step in (-1, 1):
-                        for core in range(2):
-                            level = (z + step * (1 - 2 * core)) % levels
-                            if level // per_plane == y:
-                                row += [column(level, x, core), column(level, 1 - x, core)]
-                    level = z if row[0] else (z + levels // 2) % levels
-                    for core in (c, 1 - c):
-                        row += [column(level, x, core), column(level, 1 - x, core)]
-                    table[((z * 2 + x) * 2 + c) * planes + y, : len(row)] = row
-    return table
+    )(*blocks, *([into] if aliased else []))
 
 
 def ringed(log_derivs, coefficients):
@@ -248,12 +259,16 @@
     turns = [moves(lambda z, x, c, y, k=k: (z + k, x, c, y)) for k in range(1, levels)]
 
     def to_holder(step, side, swap):
-        return moves(lambda z, x, c, y: (z, x ^ side, c ^ y ^ swap, holder(z - step * (1 - 2 * c))))
+        def to(z, x, c, y):
+            plane = holder(z - step * (1 - 2 * c))
+            return z, x ^ side, c ^ swap ^ (plane != y), plane
+
+        return [(source, target) for source, target in moves(to) if source != target]
 
     def send(value, pairs):
         return lax.ppermute(value, BOTH, pairs)
 
-    table = jnp.asarray(column_table(levels, planes, rows // 128))
+    dims = levels, planes, rows // 128
 
     core_rows = send(log_derivs, over_core)
     one = send(log_derivs, ring)
@@ -271,9 +286,16 @@
     all_rows = (log_derivs, core_rows, side_rows, side_core_rows)
 
     def one_level(block, step, name):
-        out = kernel_call(functools.partial(one_level_kernel, scale), [(rows, rows)] * 4, name, stats, *all_rows, block)
+        out = kernel_call(
+            functools.partial(one_level_kernel, scale, dims, 9 if step == 1 else 10),
+            [(rows, rows)] * 4,
+            name,
+            stats,
+            *all_rows,
+            block,
+            )
         sent = [[send(out[2 * k + swap], to_holder(step, 1 - k, swap)) for swap in range(2)] for k in range(2)]
-        return out, sent[::-1]
+        return out, ([*sent[1], (out[2], 9 if step == 1 else 10)], sent[0])
 
     out, near = one_level(one, 1, "products_near")
     share = params // lax.axis_size("smp")
@@ -286,24 +308,25 @@
         *all_rows,
         after(log_derivs, out[0]),
     )
-    near = [after(piece, *near[1]) for piece in near[0]], near[1]
-    three = send(after(log_derivs, *near[1], *near[0], *own_level), back)
-    two = after(two, *near[1], *near[0], *own_level)
+    near = [*[after(piece, *near[1]) for piece in near[0][:2]], near[0][2]], near[1]
+    three = send(after(log_derivs, *near[1], *near[0][:2], *own_level), back)
+    two = after(two, *near[1], *near[0][:2], *own_level)
     keep_own, keep_side, sent_own, sent_side = kernel_call(
-        functools.partial(across_level_kernel, scale, planes, 0),
+        functools.partial(across_level_kernel, scale, dims),
         [(2 * rows, rows)] * 4,
         "products_across",
-        table,
         stats,
         *all_rows,
         two,
         *own_level,
-        smem=1,
         cost=LONG,
     )
     got_own = send(sent_own, over_plane)
     got_side = send(sent_side, diagonal)
     from_side = send(keep_side, over_side)
+
+    gram = place(dims, [(near[0], [(1, 0)]), (near[1], [(2, 0)])], shape, None, "place_near", apart=True)
+    three = after(three, gram)
 
     out, far = one_level(three, -1, "products_far")
 
@@ -313,17 +336,16 @@
     update = lax.dynamic_slice(after(stats, out[0]), (1, lax.axis_index("smp") * share), (1, share))[0]
     update = update / jnp.sqrt(jnp.float32(samples))
     gram = place(
-        table,
-        planes,
-        [(near[0], [(1, 0)]), (near[1], [(2, 0)]), ((keep_own, got_own), [(5, 0)]), ((from_side, got_side), [(6, 0)])],
+        dims,
+        [((keep_own, got_own), [(5, 0)]), ((from_side, got_side), [(6, 0)])],
         shape,
-        None,
+        gram,
         "place_most",
-    )
-    gram = after(gram, *far[1], *far[0])
+        apart=True,
+    )
+    gram = after(gram, *far[1], *far[0][:2])
     gram = place(
-        table,
-        planes,
+        dims,
         [(far[1], [(4, 0)]), (far[0], [(3, 0)]), ((across_own,), [(7, 0)]), ((across_side,), [(8, 0)])],
         shape,
         gram,

time: 104 us -> 103 us (level)
  waiting for transfers between devices: 50.2 us -> 52.6 us
  starting transfers between devices: 34.9 us -> 32.7 us
    ppermute x24, waiting for transfers between devices: 50.2 us -> 52.6 us  [send(): return lax.ppermute(value, BOTH, pairs)]
    ppermute x24, starting transfers between devices: 34.9 us -> 32.7 us  [send(): return lax.ppermute(value, BOTH, pairs)]
    pallas_call x2 -> x3, Pallas kernels: 4.12 us -> 4.01 us  [place(): pl.pallas_call(functools.partial(place_kernel, dims, apart, [[flag for _,...]
  transfers between devices with their start and end apart: 24 -> 24, of which waited for: 10 -> 10; matrix products, arithmetic and copies ran while one was open for 1% -> 1% of each run, Pallas kernels for 13% -> 12%
where the time goes in v7:
time: 103 us
  waiting for transfers between devices  52.6 us (51%)
  starting transfers between devices  32.7 us (32%)
  Pallas kernels  14.4 us (14%)
  local copies, waits for them, and re-layouts  1.94 us (2%)
    ppermute x24, waiting for transfers between devices, send(): return lax.ppermute(value, BOTH, pairs)  52.6 us
    ppermute x24, starting transfers between devices, send(): return lax.ppermute(value, BOTH, pairs)  32.7 us
    pallas_call x8, Pallas kernels, kernel_call(): pl.pallas_call(kernel, out_shape=[jax.ShapeDtypeStruct(s, jnp.float32) fo...  10.4 us
    pallas_call x3, Pallas kernels, place(): pl.pallas_call(functools.partial(place_kernel, dims, apart, [[flag for _,...  4.01 us
  transfers between devices with their start and end apart: 24, of which 10 were waited for; matrix products, arithmetic and copies ran while one was open for 1% of the time, Pallas kernels for 12%

profile of v7, /device:TPU:0, one launch (start us, length us, event | category | flops | bytes accessed | tf_op | source)
XLA Modules:
  0.0 103.0 jit_solution(17668395095106195250)
XLA Ops:
  1.2 3.0 %collective-permute-start.6 = (f32[256,1024]{1,0:T(8,128)}, f32[256,1024]{1,0:T(8,128)S(1)}, u32[]{:S(2)}, u32[]{:S(2)}) collective-permute-start(f32[256,1024]{1,0:T(8,128)} %refs_0_.7), channel_id=1, source_target_pairs={{0,8},{1,9},{2,26},{3,27},{4,12},{5,13},{6,30},{7,31},{8,16},{9,17... | collective-permute-start | bytes 3145736 | tf_op jit(solution)/shard_map/ppermute | solution.py:269
  4.2 2.3 %collective-permute-start.7 = (f32[256,1024]{1,0:T(8,128)}, f32[256,1024]{1,0:T(8,128)S(1)}, u32[]{:S(2)}, u32[]{:S(2)}) collective-permute-start(f32[256,1024]{1,0:T(8,128)} %refs_0_.7), channel_id=1, source_target_pairs={{0,4},{1,5},{2,6},{3,7},{4,0},{5,1},{6,2},{7,3},{8,12},{9,13},{10,... | collective-permute-start | bytes 3145736 | tf_op jit(solution)/shard_map/ppermute | solution.py:269
  6.5 1.3 %copy-done = f32[256,1024]{1,0:T(8,128)S(1)} copy-done((f32[256,1024]{1,0:T(8,128)S(1)}, f32[256,1024]{1,0:T(8,128)}, u32[]{:S(2)}) %copy-start) | copy-done | bytes 1048600
  8.4 1.2 %block_stats.1.refs_0_ = f32[8,1024]{1,0:T(8,128)S(1)} custom-call(f32[256,1024]{1,0:T(8,128)S(1)} %copy-done, f32[256,1024]{1,0:T(8,128)S(1)} %collective-permute-done.other_ref.refs_1_, f32[1,256]{1,0:T(1,128)S(1)} %bitcast.4, f32[1,256]{1,0:T(1,128)S(1)} %collective-permute-done.1.other_coef_ref), custom_call_target="tpu_custom_call" | custom-call | tf_op jit(solution)/shard_map/block_stats/pallas_call | solution.py:162
  9.6 1.6 %collective-permute-start.2 = (f32[8,1024]{1,0:T(8,128)S(1)}, f32[8,1024]{1,0:T(8,128)S(1)}, u32[]{:S(2)}, u32[]{:S(2)}) collective-permute-start(f32[8,1024]{1,0:T(8,128)S(1)} %block_stats.1.refs_0_), channel_id=1, source_target_pairs={{0,8},{1,9},{2,10},{3,11},{4,12},{5,13},{6,14},{7,15},{8,16},{9,17... | collective-permute-start | bytes 98312 | tf_op jit(solution)/shard_map/ppermute | solution.py:269
  11.2 2.6 %collective-permute-start.3 = (f32[8,1024]{1,0:T(8,128)S(1)}, f32[8,1024]{1,0:T(8,128)S(1)}, u32[]{:S(2)}, u32[]{:S(2)}) collective-permute-start(f32[8,1024]{1,0:T(8,128)S(1)} %block_stats.1.refs_0_), channel_id=1, source_target_pairs={{0,16},{1,17},{2,18},{3,19},{4,20},{5,21},{6,22},{7,23},{8,24},{9,... | collective-permute-start | bytes 98312 | tf_op jit(solution)/shard_map/ppermute | solution.py:269
  13.8 1.3 %collective-permute-start.4 = (f32[8,1024]{1,0:T(8,128)S(1)}, f32[8,1024]{1,0:T(8,128)S(1)}, u32[]{:S(2)}, u32[]{:S(2)}) collective-permute-start(f32[8,1024]{1,0:T(8,128)S(1)} %block_stats.1.refs_0_), channel_id=1, source_target_pairs={{0,24},{1,25},{2,26},{3,27},{4,28},{5,29},{6,30},{7,31},{8,0},{9,1... | collective-permute-start | bytes 98312 | tf_op jit(solution)/shard_map/ppermute | solution.py:269
  15.2 15.9 %collective-permute-done.2.refs_1_ = f32[8,1024]{1,0:T(8,128)S(1)} collective-permute-done((f32[8,1024]{1,0:T(8,128)S(1)}, f32[8,1024]{1,0:T(8,128)S(1)}, u32[]{:S(2)}, u32[]{:S(2)}) %collective-permute-start.2) | collective-permute-done | bytes 32800 | tf_op jit(solution)/shard_map/ppermute | solution.py:269
  31.3 1.3 %collective-permute-start.18 = (f32[256,1024]{1,0:T(8,128)S(1)}, f32[256,1024]{1,0:T(8,128)S(1)}, u32[]{:S(2)}, u32[]{:S(2)}) collective-permute-start(f32[256,1024]{1,0:T(8,128)S(1)} %collective-permute-done.6.refs_4_), channel_id=1, source_target_pairs={{0,8},{1,9},{2,26},{3,27},{4,12},{5,13},{6,30},{7,31},{8,16},{9,17... | collective-permute-start | bytes 3145736 | tf_op jit(solution)/shard_map/ppermute | solution.py:269
  32.6 1.5 %collective-permute-start.5 = (f32[8,1024]{1,0:T(8,128)S(1)}, f32[8,1024]{1,0:T(8,128)S(1)}, u32[]{:S(2)}, u32[]{:S(2)}) collective-permute-start(f32[8,1024]{1,0:T(8,128)S(1)} %merge.2.refs_0_), channel_id=1, source_target_pairs={{0,4},{1,5},{2,6},{3,7},{4,0},{5,1},{6,2},{7,3},{8,12},{9,13},{10,... | collective-permute-start | bytes 98312 | tf_op jit(solution)/shard_map/ppermute | solution.py:269
  34.1 2.4 %collective-permute-done.5.refs_1_ = f32[8,1024]{1,0:T(8,128)S(1)} collective-permute-done((f32[8,1024]{1,0:T(8,128)S(1)}, f32[8,1024]{1,0:T(8,128)S(1)}, u32[]{:S(2)}, u32[]{:S(2)}) %collective-permute-start.5) | collective-permute-done | bytes 32800 | tf_op jit(solution)/shard_map/ppermute | solution.py:269
  36.5 1.9 %products_near.1 = (f32[256,256]{1,0:T(8,128)S(1)}, f32[256,256]{1,0:T(8,128)S(1)}, f32[256,256]{1,0:T(8,128)S(1)}, f32[256,256]{1,0:T(8,128)S(1)}) custom-call(f32[8,1024]{1,0:T(8,128)S(1)} %merge.3.mean_ref, f32[256,1024]{1,0:T(8,128)S(1)} %copy-done.1, f32[256,1024]{1,0:T(8,128)S(1)} %collective-permute-done.other_ref.refs_1_, ...), custom_call_target="tpu_custom_call" | custom-call | tf_op jit(solution)/shard_map/products_near/pallas_call | solution.py:162
  38.4 2.5 %collective-permute-start.10 = (f32[256,256]{1,0:T(8,128)S(1)}, f32[256,256]{1,0:T(8,128)S(1)}, u32[]{:S(2)}, u32[]{:S(2)}) collective-permute-start(f32[256,256]{1,0:T(8,128)S(1)} %get-tuple-element.34), channel_id=1, source_target_pairs={{0,5},{1,7},{2,4},{3,6},{4,1},{5,3},{6,0},{7,2},{8,14},{9,12},{10,... | collective-permute-start | bytes 786440 | tf_op jit(solution)/shard_map/ppermute | solution.py:269
  40.9 2.3 %collective-permute-start.12 = (f32[256,256]{1,0:T(8,128)S(1)}, f32[256,256]{1,0:T(8,128)S(1)}, u32[]{:S(2)}, u32[]{:S(2)}) collective-permute-start(f32[256,256]{1,0:T(8,128)S(1)} %get-tuple-element.37), channel_id=1, source_target_pairs={{0,1},{1,3},{2,0},{3,2},{4,5},{5,7},{6,4},{7,6},{8,10},{9,8},{10,1... | collective-permute-start | bytes 786440 | tf_op jit(solution)/shard_map/ppermute | solution.py:269
  43.2 3.6 %collective-permute-start.11 = (f32[256,256]{1,0:T(8,128)S(1)}, f32[256,256]{1,0:T(8,128)S(1)}, u32[]{:S(2)}, u32[]{:S(2)}) collective-permute-start(f32[256,256]{1,0:T(8,128)S(1)} %get-tuple-element.35.refs_2_), channel_id=1, source_target_pairs={{0,3},{3,0},{4,7},{7,4},{9,10},{10,9},{13,14},{14,13},{17,18},{18,... | collective-permute-start | bytes 786440 | tf_op jit(solution)/shard_map/ppermute | solution.py:269
  46.8 1.9 %products_level.1 = (f32[512,256]{1,0:T(8,128)S(1)}, f32[512,256]{1,0:T(8,128)S(1)}) custom-call(f32[8,1024]{1,0:T(8,128)S(1)} %merge.3.mean_ref, f32[256,1024]{1,0:T(8,128)S(1)} %copy-done.1, f32[256,1024]{1,0:T(8,128)S(1)} %collective-permute-done.other_ref.refs_1_, f32[256,1024]{1,0:T(8,128)S(1)} %collective-permute-done.7.refs_2_, ...), custom_call_target="tpu_custom_call" | custom-call | tf_op jit(solution)/shard_map/products_level/pallas_call | solution.py:162
  48.8 1.0 collective-permute-done.12.refs_1_
  49.8 5.0 %collective-permute-done.9.refs_3_ = f32[256,256]{1,0:T(8,128)S(1)} collective-permute-done((f32[256,256]{1,0:T(8,128)S(1)}, f32[256,256]{1,0:T(8,128)S(1)}, u32[]{:S(2)}, u32[]{:S(2)}) %collective-permute-start.9) | collective-permute-done | bytes 262176 | tf_op jit(solution)/shard_map/ppermute | solution.py:269
  56.2 3.4 %collective-permute-done.18.refs_4_ = f32[256,1024]{1,0:T(8,128)S(1)} collective-permute-done((f32[256,1024]{1,0:T(8,128)S(1)}, f32[256,1024]{1,0:T(8,128)S(1)}, u32[]{:S(2)}, u32[]{:S(2)}) %collective-permute-start.18) | collective-permute-done | bytes 1048608 | tf_op jit(solution)/shard_map/ppermute | solution.py:269
  59.6 1.9 %products_across.1 = (f32[512,256]{1,0:T(8,128)S(1)}, f32[512,256]{1,0:T(8,128)S(1)}, f32[512,256]{1,0:T(8,128)S(1)}, f32[512,256]{1,0:T(8,128)S(1)}) custom-call(f32[8,1024]{1,0:T(8,128)S(1)} %merge.3.mean_ref, f32[256,1024]{1,0:T(8,128)S(1)} %copy-done.1, f32[256,1024]{1,0:T(8,128)S(1)} %collective-permute-done.other_ref.refs_1_, ...), custom_call_target="tpu_custom_call" | custom-call | flops 4000000000 | tf_op jit(solution)/shard_map/products_across/pallas_call | solution.py:162
  61.5 1.3 %collective-permute-start.19 = (f32[512,256]{1,0:T(8,128)S(1)}, f32[512,256]{1,0:T(8,128)S(1)}, u32[]{:S(2)}, u32[]{:S(2)}) collective-permute-start(f32[512,256]{1,0:T(8,128)S(1)} %get-tuple-element.50), channel_id=1, source_target_pairs={{0,1},{1,0},{2,3},{3,2},{4,5},{5,4},{6,7},{7,6},{8,9},{9,8},{10,11... | collective-permute-start | bytes 1572872 | tf_op jit(solution)/shard_map/ppermute | solution.py:269
  62.8 1.5 %collective-permute-start.20 = (f32[512,256]{1,0:T(8,128)S(1)}, f32[512,256]{1,0:T(8,128)S(1)}, u32[]{:S(2)}, u32[]{:S(2)}) collective-permute-start(f32[512,256]{1,0:T(8,128)S(1)} %get-tuple-element.52), channel_id=1, source_target_pairs={{0,4},{1,5},{2,6},{3,7},{4,0},{5,1},{6,2},{7,3},{8,12},{9,13},{10,... | collective-permute-start | bytes 1572872 | tf_op jit(solution)/shard_map/ppermute | solution.py:269
  65.1 1.0 place_near.1.refs_4_
  66.1 15.5 %collective-permute-done.13.refs_4_ = f32[256,1024]{1,0:T(8,128)S(1)} collective-permute-done((f32[256,1024]{1,0:T(8,128)S(1)}, f32[256,1024]{1,0:T(8,128)S(1)}, u32[]{:S(2)}, u32[]{:S(2)}) %collective-permute-start.13) | collective-permute-done | bytes 1048608 | tf_op jit(solution)/shard_map/ppermute | solution.py:269
  81.6 2.6 %products_far.1 = (f32[256,256]{1,0:T(8,128)S(1)}, f32[256,256]{1,0:T(8,128)}, f32[256,256]{1,0:T(8,128)S(1)}, f32[256,256]{1,0:T(8,128)}) custom-call(f32[8,1024]{1,0:T(8,128)S(1)} %merge.3.mean_ref, f32[256,1024]{1,0:T(8,128)S(1)} %copy-done.1, f32[256,1024]{1,0:T(8,128)S(1)} %collective-permute-done.other_ref.refs_1_, ...), custom_call_target="tpu_custom_call" | custom-call | tf_op jit(solution)/shard_map/products_far/pallas_call | solution.py:162
  84.2 1.2 %collective-permute-start.14 = (f32[256,256]{1,0:T(8,128)S(1)}, f32[256,256]{1,0:T(8,128)S(1)}, u32[]{:S(2)}, u32[]{:S(2)}) collective-permute-start(f32[256,256]{1,0:T(8,128)S(1)} %get-tuple-element.44), channel_id=1, source_target_pairs={{0,4},{1,6},{2,5},{3,7},{4,0},{5,2},{6,1},{7,3},{8,15},{9,13},{10,... | collective-permute-start | bytes 786440 | tf_op jit(solution)/shard_map/ppermute | solution.py:269
  86.1 3.7 %collective-permute-start.17 = (f32[256,256]{1,0:T(8,128)}, f32[256,256]{1,0:T(8,128)S(1)}, u32[]{:S(2)}, u32[]{:S(2)}) collective-permute-start(f32[256,256]{1,0:T(8,128)} %get-tuple-element.47), channel_id=1, source_target_pairs={{0,2},{1,0},{2,3},{3,1},{4,6},{5,4},{6,7},{7,5},{8,9},{9,11},{10,8... | collective-permute-start | bytes 786440 | tf_op jit(solution)/shard_map/ppermute | solution.py:269
  90.7 2.7 %collective-permute-done.14.refs_0_ = f32[256,256]{1,0:T(8,128)S(1)} collective-permute-done((f32[256,256]{1,0:T(8,128)S(1)}, f32[256,256]{1,0:T(8,128)S(1)}, u32[]{:S(2)}, u32[]{:S(2)}) %collective-permute-start.14) | collective-permute-done | bytes 262176 | tf_op jit(solution)/shard_map/ppermute | solution.py:269
  93.5 0.9 place_most.1.refs_7_
  95.0 3.9 %collective-permute-done.15.refs_1_ = f32[256,256]{1,0:T(8,128)S(1)} collective-permute-done((f32[256,256]{1,0:T(8,128)}, f32[256,256]{1,0:T(8,128)S(1)}, u32[]{:S(2)}, u32[]{:S(2)}) %collective-permute-start.15) | collective-permute-done | bytes 262176 | tf_op jit(solution)/shard_map/ppermute | solution.py:269
  98.9 2.0 %collective-permute-done.17.refs_3_ = f32[256,256]{1,0:T(8,128)S(1)} collective-permute-done((f32[256,256]{1,0:T(8,128)}, f32[256,256]{1,0:T(8,128)S(1)}, u32[]{:S(2)}, u32[]{:S(2)}) %collective-permute-start.17) | collective-permute-done | bytes 262176 | tf_op jit(solution)/shard_map/ppermute | solution.py:269
  100.9 2.1 %place_last.1 = f32[256,2048]{1,0:T(8,128)} custom-call(f32[256,256]{1,0:T(8,128)S(1)} %collective-permute-done.14.refs_0_, f32[256,256]{1,0:T(8,128)S(1)} %collective-permute-done.15.refs_1_, f32[256,256]{1,0:T(8,128)S(1)} %collective-permute-done.16.refs_2_, f32[256,256]{1,0:T(8,128)S(1)} %collective-permute-done.17.refs_3_, ...), custom_call_target="tpu_custom_call", output_to_operand_aliasing={{}: (7, {})} | custom-call | tf_op jit(solution)/shard_map/place_last/pallas_call | solution.py:216
  (34 shorter events, 5.9 us)
Async XLA Ops:
  0.6 5.9 %collective-permute-start = (f32[256,1024]{1,0:T(8,128)}, f32[256,1024]{1,0:T(8,128)S(1)}, u32[]{:S(2)}, u32[]{:S(2)}) collective-permute-start(f32[256,1024]{1,0:T(8,128)} %refs_0_.7), channel_id=1, source_target_pairs={{0,2},{1,3},{2,0},{3,1},{4,6},{5,7},{6,4},{7,5},{8,10},{9,11},{10,... | collective-permute-start | bytes 3145736 | tf_op jit(solution)/shard_map/ppermute | solution.py:269
  1.1 3.1 %collective-permute-start.1 = (f32[1,256]{1,0:T(1,128)}, f32[1,256]{1,0:T(1,128)S(1)}, u32[]{:S(2)}, u32[]{:S(2)}) collective-permute-start(f32[1,256]{1,0:T(1,128)} %bitcast.3), channel_id=1, source_target_pairs={{0,2},{1,3},{2,0},{3,1},{4,6},{5,7},{6,4},{7,5},{8,10},{9,11},{10,... | collective-permute-start | bytes 3080 | tf_op jit(solution)/shard_map/ppermute | solution.py:269
  1.2 29.9 %collective-permute-start.6 = (f32[256,1024]{1,0:T(8,128)}, f32[256,1024]{1,0:T(8,128)S(1)}, u32[]{:S(2)}, u32[]{:S(2)}) collective-permute-start(f32[256,1024]{1,0:T(8,128)} %refs_0_.7), channel_id=1, source_target_pairs={{0,8},{1,9},{2,26},{3,27},{4,12},{5,13},{6,30},{7,31},{8,16},{9,17... | collective-permute-start | bytes 3145736 | tf_op jit(solution)/shard_map/ppermute | solution.py:269
  4.2 26.9 %collective-permute-start.7 = (f32[256,1024]{1,0:T(8,128)}, f32[256,1024]{1,0:T(8,128)S(1)}, u32[]{:S(2)}, u32[]{:S(2)}) collective-permute-start(f32[256,1024]{1,0:T(8,128)} %refs_0_.7), channel_id=1, source_target_pairs={{0,4},{1,5},{2,6},{3,7},{4,0},{5,1},{6,2},{7,3},{8,12},{9,13},{10,... | collective-permute-start | bytes 3145736 | tf_op jit(solution)/shard_map/ppermute | solution.py:269
  6.5 1.3 %copy-start = (f32[256,1024]{1,0:T(8,128)S(1)}, f32[256,1024]{1,0:T(8,128)}, u32[]{:S(2)}) copy-start(f32[256,1024]{1,0:T(8,128)} %refs_0_.7) | copy-start | bytes 3145732
  7.8 0.7 copy-start.2
  8.4 28.1 %copy-start.1 = (f32[256,1024]{1,0:T(8,128)S(1)}, f32[256,1024]{1,0:T(8,128)}, u32[]{:S(2)}) copy-start(f32[256,1024]{1,0:T(8,128)} %refs_0_.7) | copy-start | bytes 3145732
  9.6 21.5 %collective-permute-start.2 = (f32[8,1024]{1,0:T(8,128)S(1)}, f32[8,1024]{1,0:T(8,128)S(1)}, u32[]{:S(2)}, u32[]{:S(2)}) collective-permute-start(f32[8,1024]{1,0:T(8,128)S(1)} %block_stats.1.refs_0_), channel_id=1, source_target_pairs={{0,8},{1,9},{2,10},{3,11},{4,12},{5,13},{6,14},{7,15},{8,16},{9,17... | collective-permute-start | bytes 98312 | tf_op jit(solution)/shard_map/ppermute | solution.py:269
  11.2 19.9 %collective-permute-start.3 = (f32[8,1024]{1,0:T(8,128)S(1)}, f32[8,1024]{1,0:T(8,128)S(1)}, u32[]{:S(2)}, u32[]{:S(2)}) collective-permute-start(f32[8,1024]{1,0:T(8,128)S(1)} %block_stats.1.refs_0_), channel_id=1, source_target_pairs={{0,16},{1,17},{2,18},{3,19},{4,20},{5,21},{6,22},{7,23},{8,24},{9,... | collective-permute-start | bytes 98312 | tf_op jit(solution)/shard_map/ppermute | solution.py:269
  13.8 17.3 %collective-permute-start.4 = (f32[8,1024]{1,0:T(8,128)S(1)}, f32[8,1024]{1,0:T(8,128)S(1)}, u32[]{:S(2)}, u32[]{:S(2)}) collective-permute-start(f32[8,1024]{1,0:T(8,128)S(1)} %block_stats.1.refs_0_), channel_id=1, source_target_pairs={{0,24},{1,25},{2,26},{3,27},{4,28},{5,29},{6,30},{7,31},{8,0},{9,1... | collective-permute-start | bytes 98312 | tf_op jit(solution)/shard_map/ppermute | solution.py:269
  31.1 5.4 %collective-permute-start.8 = (f32[256,1024]{1,0:T(8,128)S(1)}, f32[256,1024]{1,0:T(8,128)S(1)}, u32[]{:S(2)}, u32[]{:S(2)}) collective-permute-start(f32[256,1024]{1,0:T(8,128)S(1)} %collective-permute-done.7.refs_2_), channel_id=1, source_target_pairs={{0,2},{1,3},{2,0},{3,1},{4,6},{5,7},{6,4},{7,5},{8,10},{9,11},{10,... | collective-permute-start | bytes 3145736 | tf_op jit(solution)/shard_map/ppermute | solution.py:269
  31.3 28.3 %collective-permute-start.18 = (f32[256,1024]{1,0:T(8,128)S(1)}, f32[256,1024]{1,0:T(8,128)S(1)}, u32[]{:S(2)}, u32[]{:S(2)}) collective-permute-start(f32[256,1024]{1,0:T(8,128)S(1)} %collective-permute-done.6.refs_4_), channel_id=1, source_target_pairs={{0,8},{1,9},{2,26},{3,27},{4,12},{5,13},{6,30},{7,31},{8,16},{9,17... | collective-permute-start | bytes 3145736 | tf_op jit(solution)/shard_map/ppermute | solution.py:269
  32.6 3.9 %collective-permute-start.5 = (f32[8,1024]{1,0:T(8,128)S(1)}, f32[8,1024]{1,0:T(8,128)S(1)}, u32[]{:S(2)}, u32[]{:S(2)}) collective-permute-start(f32[8,1024]{1,0:T(8,128)S(1)} %merge.2.refs_0_), channel_id=1, source_target_pairs={{0,4},{1,5},{2,6},{3,7},{4,0},{5,1},{6,2},{7,3},{8,12},{9,13},{10,... | collective-permute-start | bytes 98312 | tf_op jit(solution)/shard_map/ppermute | solution.py:269
  38.4 10.3 %collective-permute-start.10 = (f32[256,256]{1,0:T(8,128)S(1)}, f32[256,256]{1,0:T(8,128)S(1)}, u32[]{:S(2)}, u32[]{:S(2)}) collective-permute-start(f32[256,256]{1,0:T(8,128)S(1)} %get-tuple-element.34), channel_id=1, source_target_pairs={{0,5},{1,7},{2,4},{3,6},{4,1},{5,3},{6,0},{7,2},{8,14},{9,12},{10,... | collective-permute-start | bytes 786440 | tf_op jit(solution)/shard_map/ppermute | solution.py:269
  40.9 8.8 %collective-permute-start.12 = (f32[256,256]{1,0:T(8,128)S(1)}, f32[256,256]{1,0:T(8,128)S(1)}, u32[]{:S(2)}, u32[]{:S(2)}) collective-permute-start(f32[256,256]{1,0:T(8,128)S(1)} %get-tuple-element.37), channel_id=1, source_target_pairs={{0,1},{1,3},{2,0},{3,2},{4,5},{5,7},{6,4},{7,6},{8,10},{9,8},{10,1... | collective-permute-start | bytes 786440 | tf_op jit(solution)/shard_map/ppermute | solution.py:269
  43.2 11.5 %collective-permute-start.9 = (f32[256,256]{1,0:T(8,128)S(1)}, f32[256,256]{1,0:T(8,128)S(1)}, u32[]{:S(2)}, u32[]{:S(2)}) collective-permute-start(f32[256,256]{1,0:T(8,128)S(1)} %get-tuple-element.33), channel_id=1, source_target_pairs={{0,7},{1,5},{2,6},{3,4},{4,3},{5,1},{6,2},{7,0},{8,12},{9,14},{10,... | collective-permute-start | bytes 786440 | tf_op jit(solution)/shard_map/ppermute | solution.py:269
  43.2 12.1 %collective-permute-start.11 = (f32[256,256]{1,0:T(8,128)S(1)}, f32[256,256]{1,0:T(8,128)S(1)}, u32[]{:S(2)}, u32[]{:S(2)}) collective-permute-start(f32[256,256]{1,0:T(8,128)S(1)} %get-tuple-element.35.refs_2_), channel_id=1, source_target_pairs={{0,3},{3,0},{4,7},{7,4},{9,10},{10,9},{13,14},{14,13},{17,18},{18,... | collective-permute-start | bytes 786440 | tf_op jit(solution)/shard_map/ppermute | solution.py:269
  55.3 26.3 %collective-permute-start.13 = (f32[256,1024]{1,0:T(8,128)S(1)}, f32[256,1024]{1,0:T(8,128)S(1)}, u32[]{:S(2)}, u32[]{:S(2)}) collective-permute-start(f32[256,1024]{1,0:T(8,128)S(1)} %copy-done.1), channel_id=1, source_target_pairs={{0,24},{1,25},{2,10},{3,11},{4,28},{5,29},{6,14},{7,15},{8,0},{9,1... | collective-permute-start | bytes 3145736 | tf_op jit(solution)/shard_map/ppermute | solution.py:269
  61.5 23.9 %collective-permute-start.19 = (f32[512,256]{1,0:T(8,128)S(1)}, f32[512,256]{1,0:T(8,128)S(1)}, u32[]{:S(2)}, u32[]{:S(2)}) collective-permute-start(f32[512,256]{1,0:T(8,128)S(1)} %get-tuple-element.50), channel_id=1, source_target_pairs={{0,1},{1,0},{2,3},{3,2},{4,5},{5,4},{6,7},{7,6},{8,9},{9,8},{10,11... | collective-permute-start | bytes 1572872 | tf_op jit(solution)/shard_map/ppermute | solution.py:269
  62.8 23.3 %collective-permute-start.20 = (f32[512,256]{1,0:T(8,128)S(1)}, f32[512,256]{1,0:T(8,128)S(1)}, u32[]{:S(2)}, u32[]{:S(2)}) collective-permute-start(f32[512,256]{1,0:T(8,128)S(1)} %get-tuple-element.52), channel_id=1, source_target_pairs={{0,4},{1,5},{2,6},{3,7},{4,0},{5,1},{6,2},{7,3},{8,12},{9,13},{10,... | collective-permute-start | bytes 1572872 | tf_op jit(solution)/shard_map/ppermute | solution.py:269
  64.3 25.6 %collective-permute-start.21 = (f32[512,256]{1,0:T(8,128)S(1)}, f32[512,256]{1,0:T(8,128)S(1)}, u32[]{:S(2)}, u32[]{:S(2)}) collective-permute-start(f32[512,256]{1,0:T(8,128)S(1)} %get-tuple-element.53), channel_id=1, source_target_pairs={{0,5},{1,4},{2,7},{3,6},{4,1},{5,0},{6,3},{7,2},{8,13},{9,12},{10,... | collective-permute-start | bytes 1572872 | tf_op jit(solution)/shard_map/ppermute | solution.py:269
  84.2 9.2 %collective-permute-start.14 = (f32[256,256]{1,0:T(8,128)S(1)}, f32[256,256]{1,0:T(8,128)S(1)}, u32[]{:S(2)}, u32[]{:S(2)}) collective-permute-start(f32[256,256]{1,0:T(8,128)S(1)} %get-tuple-element.44), channel_id=1, source_target_pairs={{0,4},{1,6},{2,5},{3,7},{4,0},{5,2},{6,1},{7,3},{8,15},{9,13},{10,... | collective-permute-start | bytes 786440 | tf_op jit(solution)/shard_map/ppermute | solution.py:269
  85.4 13.5 %collective-permute-start.15 = (f32[256,256]{1,0:T(8,128)}, f32[256,256]{1,0:T(8,128)S(1)}, u32[]{:S(2)}, u32[]{:S(2)}) collective-permute-start(f32[256,256]{1,0:T(8,128)} %get-tuple-element.45), channel_id=1, source_target_pairs={{0,6},{1,4},{2,7},{3,5},{4,2},{5,0},{6,3},{7,1},{8,13},{9,15},{10,... | collective-permute-start | bytes 786440 | tf_op jit(solution)/shard_map/ppermute | solution.py:269
  85.4 13.5 %collective-permute-start.16 = (f32[256,256]{1,0:T(8,128)S(1)}, f32[256,256]{1,0:T(8,128)S(1)}, u32[]{:S(2)}, u32[]{:S(2)}) collective-permute-start(f32[256,256]{1,0:T(8,128)S(1)} %get-tuple-element.46.refs_4_), channel_id=1, source_target_pairs={{1,2},{2,1},{5,6},{6,5},{8,11},{11,8},{12,15},{15,12},{16,19},{19,... | collective-permute-start | bytes 786440 | tf_op jit(solution)/shard_map/ppermute | solution.py:269
  86.1 14.8 %collective-permute-start.17 = (f32[256,256]{1,0:T(8,128)}, f32[256,256]{1,0:T(8,128)S(1)}, u32[]{:S(2)}, u32[]{:S(2)}) collective-permute-start(f32[256,256]{1,0:T(8,128)} %get-tuple-element.47), channel_id=1, source_target_pairs={{0,2},{1,0},{2,3},{3,1},{4,6},{5,4},{6,7},{7,5},{8,9},{9,11},{10,8... | collective-permute-start | bytes 786440 | tf_op jit(solution)/shard_map/ppermute | solution.py:269
  90.7 10.2 %collective-permute-start.22 = (f32[256,256]{1,0:T(8,128)}, f32[256,256]{1,0:T(8,128)}, u32[]{:S(2)}, u32[]{:S(2)}) collective-permute-start(f32[256,256]{1,0:T(8,128)} %get-tuple-element.54), channel_id=1, source_target_pairs={{0,2},{1,3},{2,0},{3,1},{4,6},{5,7},{6,4},{7,5},{8,10},{9,11},{10,... | collective-permute-start | bytes 786440 | tf_op jit(solution)/shard_map/ppermute | solution.py:269
  93.5 7.5 %collective-permute-start.23 = (f32[256,256]{1,0:T(8,128)}, f32[256,256]{1,0:T(8,128)}, u32[]{:S(2)}, u32[]{:S(2)}) collective-permute-start(f32[256,256]{1,0:T(8,128)} %get-tuple-element.55), channel_id=1, source_target_pairs={{0,2},{1,3},{2,0},{3,1},{4,6},{5,7},{6,4},{7,5},{8,10},{9,11},{10,... | collective-permute-start | bytes 786440 | tf_op jit(solution)/shard_map/ppermute | solution.py:269

commit v8 on v7

--- a/solution.py
+++ b/solution.py
@@ -270,12 +270,12 @@
 
     dims = levels, planes, rows // 128
 
-    core_rows = send(log_derivs, over_core)
     one = send(log_derivs, ring)
 
 
     coefficients = coefficients[None, :]
     other_coefficients = send(coefficients, over_core)
+    core_rows = send(after(log_derivs, other_coefficients), over_core)
     side_rows = send(after(log_derivs, other_coefficients), over_side)
     stats = block_stats(log_derivs, core_rows, coefficients, other_coefficients)
     stats = merge(stats, *[send(stats, turn) for turn in turns])

time: 103 us -> 104 us (level)
  waiting for transfers between devices: 52.6 us -> 54.5 us
    ppermute x24, waiting for transfers between devices: 52.6 us -> 54.5 us  [send(): return lax.ppermute(value, BOTH, pairs)]
  transfers between devices with their start and end apart: 24 -> 24, of which waited for: 10 -> 11; matrix products, arithmetic and copies ran while one was open for 1% -> 1% of each run, Pallas kernels for 12% -> 12%
where the time goes in v8:
time: 104 us
  waiting for transfers between devices  54.5 us (52%)
  starting transfers between devices  31.8 us (31%)
  Pallas kernels  14.4 us (14%)
  local copies, waits for them, and re-layouts  1.94 us (2%)
    ppermute x24, waiting for transfers between devices, send(): return lax.ppermute(value, BOTH, pairs)  54.5 us
    ppermute x24, starting transfers between devices, send(): return lax.ppermute(value, BOTH, pairs)  31.8 us
    pallas_call x8, Pallas kernels, kernel_call(): pl.pallas_call(kernel, out_shape=[jax.ShapeDtypeStruct(s, jnp.float32) fo...  10.4 us
    pallas_call x3, Pallas kernels, place(): pl.pallas_call(functools.partial(place_kernel, dims, apart, [[flag for _,...  4.01 us
  transfers between devices with their start and end apart: 24, of which 11 were waited for; matrix products, arithmetic and copies ran while one was open for 1% of the time, Pallas kernels for 12%

profile of v8, /device:TPU:0, one launch (start us, length us, event | category | flops | bytes accessed | tf_op | source)
XLA Modules:
  0.0 104.0 jit_solution(6842596458663857138)
XLA Ops:
  1.1 1.0 collective-permute-done.other_coef_ref
  2.5 2.8 %collective-permute-start.6 = (f32[256,1024]{1,0:T(8,128)}, f32[256,1024]{1,0:T(8,128)S(1)}, u32[]{:S(2)}, u32[]{:S(2)}) collective-permute-start(f32[256,1024]{1,0:T(8,128)} %refs_0_.7), channel_id=1, source_target_pairs={{0,8},{1,9},{2,26},{3,27},{4,12},{5,13},{6,30},{7,31},{8,16},{9,17... | collective-permute-start | bytes 3145736 | tf_op jit(solution)/shard_map/ppermute | solution.py:269
  5.3 1.5 %collective-permute-start.7 = (f32[256,1024]{1,0:T(8,128)}, f32[256,1024]{1,0:T(8,128)S(1)}, u32[]{:S(2)}, u32[]{:S(2)}) collective-permute-start(f32[256,1024]{1,0:T(8,128)} %refs_0_.7), channel_id=1, source_target_pairs={{0,4},{1,5},{2,6},{3,7},{4,0},{5,1},{6,2},{7,3},{8,12},{9,13},{10,... | collective-permute-start | bytes 3145736 | tf_op jit(solution)/shard_map/ppermute | solution.py:269
  6.8 1.3 %copy-done = f32[256,1024]{1,0:T(8,128)S(1)} copy-done((f32[256,1024]{1,0:T(8,128)S(1)}, f32[256,1024]{1,0:T(8,128)}, u32[]{:S(2)}) %copy-start) | copy-done | bytes 1048600
  8.7 1.2 %block_stats.1.refs_0_ = f32[8,1024]{1,0:T(8,128)S(1)} custom-call(f32[256,1024]{1,0:T(8,128)S(1)} %copy-done, f32[256,1024]{1,0:T(8,128)S(1)} %collective-permute-done.1.other_ref.refs_1_, f32[1,256]{1,0:T(1,128)S(1)} %bitcast.4, f32[1,256]{1,0:T(1,128)S(1)} %collective-permute-done.other_coef_ref), custom_call_target="tpu_custom_call" | custom-call | tf_op jit(solution)/shard_map/block_stats/pallas_call | solution.py:162
  9.9 1.6 %collective-permute-start.2 = (f32[8,1024]{1,0:T(8,128)S(1)}, f32[8,1024]{1,0:T(8,128)S(1)}, u32[]{:S(2)}, u32[]{:S(2)}) collective-permute-start(f32[8,1024]{1,0:T(8,128)S(1)} %block_stats.1.refs_0_), channel_id=1, source_target_pairs={{0,8},{1,9},{2,10},{3,11},{4,12},{5,13},{6,14},{7,15},{8,16},{9,17... | collective-permute-start | bytes 98312 | tf_op jit(solution)/shard_map/ppermute | solution.py:269
  11.5 2.2 %collective-permute-start.3 = (f32[8,1024]{1,0:T(8,128)S(1)}, f32[8,1024]{1,0:T(8,128)S(1)}, u32[]{:S(2)}, u32[]{:S(2)}) collective-permute-start(f32[8,1024]{1,0:T(8,128)S(1)} %block_stats.1.refs_0_), channel_id=1, source_target_pairs={{0,16},{1,17},{2,18},{3,19},{4,20},{5,21},{6,22},{7,23},{8,24},{9,... | collective-permute-start | bytes 98312 | tf_op jit(solution)/shard_map/ppermute | solution.py:269
  13.6 1.8 %collective-permute-start.4 = (f32[8,1024]{1,0:T(8,128)S(1)}, f32[8,1024]{1,0:T(8,128)S(1)}, u32[]{:S(2)}, u32[]{:S(2)}) collective-permute-start(f32[8,1024]{1,0:T(8,128)S(1)} %block_stats.1.refs_0_), channel_id=1, source_target_pairs={{0,24},{1,25},{2,26},{3,27},{4,28},{5,29},{6,30},{7,31},{8,0},{9,1... | collective-permute-start | bytes 98312 | tf_op jit(solution)/shard_map/ppermute | solution.py:269
  15.4 16.9 %collective-permute-done.2.refs_1_ = f32[8,1024]{1,0:T(8,128)S(1)} collective-permute-done((f32[8,1024]{1,0:T(8,128)S(1)}, f32[8,1024]{1,0:T(8,128)S(1)}, u32[]{:S(2)}, u32[]{:S(2)}) %collective-permute-start.2) | collective-permute-done | bytes 32800 | tf_op jit(solution)/shard_map/ppermute | solution.py:269
  32.4 1.3 %collective-permute-start.18 = (f32[256,1024]{1,0:T(8,128)S(1)}, f32[256,1024]{1,0:T(8,128)S(1)}, u32[]{:S(2)}, u32[]{:S(2)}) collective-permute-start(f32[256,1024]{1,0:T(8,128)S(1)} %collective-permute-done.6.refs_4_), channel_id=1, source_target_pairs={{0,8},{1,9},{2,26},{3,27},{4,12},{5,13},{6,30},{7,31},{8,16},{9,17... | collective-permute-start | bytes 3145736 | tf_op jit(solution)/shard_map/ppermute | solution.py:269
  33.7 1.6 %collective-permute-start.5 = (f32[8,1024]{1,0:T(8,128)S(1)}, f32[8,1024]{1,0:T(8,128)S(1)}, u32[]{:S(2)}, u32[]{:S(2)}) collective-permute-start(f32[8,1024]{1,0:T(8,128)S(1)} %merge.2.refs_0_), channel_id=1, source_target_pairs={{0,4},{1,5},{2,6},{3,7},{4,0},{5,1},{6,2},{7,3},{8,12},{9,13},{10,... | collective-permute-start | bytes 98312 | tf_op jit(solution)/shard_map/ppermute | solution.py:269
  35.3 2.3 %collective-permute-done.5.refs_1_ = f32[8,1024]{1,0:T(8,128)S(1)} collective-permute-done((f32[8,1024]{1,0:T(8,128)S(1)}, f32[8,1024]{1,0:T(8,128)S(1)}, u32[]{:S(2)}, u32[]{:S(2)}) %collective-permute-start.5) | collective-permute-done | bytes 32800 | tf_op jit(solution)/shard_map/ppermute | solution.py:269
  37.7 1.9 %products_near.1 = (f32[256,256]{1,0:T(8,128)S(1)}, f32[256,256]{1,0:T(8,128)S(1)}, f32[256,256]{1,0:T(8,128)S(1)}, f32[256,256]{1,0:T(8,128)S(1)}) custom-call(f32[8,1024]{1,0:T(8,128)S(1)} %merge.3.mean_ref, f32[256,1024]{1,0:T(8,128)S(1)} %copy-done.1, f32[256,1024]{1,0:T(8,128)S(1)} %collective-permute-done.1.other_ref.refs_1_, ...), custom_call_target="tpu_custom_call" | custom-call | tf_op jit(solution)/shard_map/products_near/pallas_call | solution.py:162
  39.6 2.6 %collective-permute-start.10 = (f32[256,256]{1,0:T(8,128)S(1)}, f32[256,256]{1,0:T(8,128)S(1)}, u32[]{:S(2)}, u32[]{:S(2)}) collective-permute-start(f32[256,256]{1,0:T(8,128)S(1)} %get-tuple-element.34), channel_id=1, source_target_pairs={{0,5},{1,7},{2,4},{3,6},{4,1},{5,3},{6,0},{7,2},{8,14},{9,12},{10,... | collective-permute-start | bytes 786440 | tf_op jit(solution)/shard_map/ppermute | solution.py:269
  42.2 2.0 %collective-permute-start.12 = (f32[256,256]{1,0:T(8,128)S(1)}, f32[256,256]{1,0:T(8,128)S(1)}, u32[]{:S(2)}, u32[]{:S(2)}) collective-permute-start(f32[256,256]{1,0:T(8,128)S(1)} %get-tuple-element.37), channel_id=1, source_target_pairs={{0,1},{1,3},{2,0},{3,2},{4,5},{5,7},{6,4},{7,6},{8,10},{9,8},{10,1... | collective-permute-start | bytes 786440 | tf_op jit(solution)/shard_map/ppermute | solution.py:269
  44.3 3.6 %collective-permute-start.11 = (f32[256,256]{1,0:T(8,128)S(1)}, f32[256,256]{1,0:T(8,128)S(1)}, u32[]{:S(2)}, u32[]{:S(2)}) collective-permute-start(f32[256,256]{1,0:T(8,128)S(1)} %get-tuple-element.35.refs_2_), channel_id=1, source_target_pairs={{0,3},{3,0},{4,7},{7,4},{9,10},{10,9},{13,14},{14,13},{17,18},{18,... | collective-permute-start | bytes 786440 | tf_op jit(solution)/shard_map/ppermute | solution.py:269
  47.9 1.9 %products_level.1 = (f32[512,256]{1,0:T(8,128)S(1)}, f32[512,256]{1,0:T(8,128)S(1)}) custom-call(f32[8,1024]{1,0:T(8,128)S(1)} %merge.3.mean_ref, f32[256,1024]{1,0:T(8,128)S(1)} %copy-done.1, f32[256,1024]{1,0:T(8,128)S(1)} %collective-permute-done.1.other_ref.refs_1_, f32[256,1024]{1,0:T(8,128)S(1)} %collective-permute-done.7.refs_2_, ...), custom_call_target="tpu_custom_call" | custom-call | tf_op jit(solution)/shard_map/products_level/pallas_call | solution.py:162
  49.8 1.0 collective-permute-done.12.refs_1_
  50.8 5.0 %collective-permute-done.9.refs_3_ = f32[256,256]{1,0:T(8,128)S(1)} collective-permute-done((f32[256,256]{1,0:T(8,128)S(1)}, f32[256,256]{1,0:T(8,128)S(1)}, u32[]{:S(2)}, u32[]{:S(2)}) %collective-permute-start.9) | collective-permute-done | bytes 262176 | tf_op jit(solution)/shard_map/ppermute | solution.py:269
  57.2 3.4 %collective-permute-done.18.refs_4_ = f32[256,1024]{1,0:T(8,128)S(1)} collective-permute-done((f32[256,1024]{1,0:T(8,128)S(1)}, f32[256,1024]{1,0:T(8,128)S(1)}, u32[]{:S(2)}, u32[]{:S(2)}) %collective-permute-start.18) | collective-permute-done | bytes 1048608 | tf_op jit(solution)/shard_map/ppermute | solution.py:269
  60.6 1.9 %products_across.1 = (f32[512,256]{1,0:T(8,128)S(1)}, f32[512,256]{1,0:T(8,128)S(1)}, f32[512,256]{1,0:T(8,128)S(1)}, f32[512,256]{1,0:T(8,128)S(1)}) custom-call(f32[8,1024]{1,0:T(8,128)S(1)} %merge.3.mean_ref, f32[256,1024]{1,0:T(8,128)S(1)} %copy-done.1, f32[256,1024]{1,0:T(8,128)S(1)} %collective-permute-done.1.other_ref.refs_1_, ...), custom_call_target="tpu_custom_call" | custom-call | flops 4000000000 | tf_op jit(solution)/shard_map/products_across/pallas_call | solution.py:162
  62.5 1.3 %collective-permute-start.19 = (f32[512,256]{1,0:T(8,128)S(1)}, f32[512,256]{1,0:T(8,128)S(1)}, u32[]{:S(2)}, u32[]{:S(2)}) collective-permute-start(f32[512,256]{1,0:T(8,128)S(1)} %get-tuple-element.50), channel_id=1, source_target_pairs={{0,1},{1,0},{2,3},{3,2},{4,5},{5,4},{6,7},{7,6},{8,9},{9,8},{10,11... | collective-permute-start | bytes 1572872 | tf_op jit(solution)/shard_map/ppermute | solution.py:269
  63.8 1.5 %collective-permute-start.20 = (f32[512,256]{1,0:T(8,128)S(1)}, f32[512,256]{1,0:T(8,128)S(1)}, u32[]{:S(2)}, u32[]{:S(2)}) collective-permute-start(f32[512,256]{1,0:T(8,128)S(1)} %get-tuple-element.52), channel_id=1, source_target_pairs={{0,4},{1,5},{2,6},{3,7},{4,0},{5,1},{6,2},{7,3},{8,12},{9,13},{10,... | collective-permute-start | bytes 1572872 | tf_op jit(solution)/shard_map/ppermute | solution.py:269
  66.1 1.0 place_near.1.refs_4_
  67.1 15.5 %collective-permute-done.13.refs_4_ = f32[256,1024]{1,0:T(8,128)S(1)} collective-permute-done((f32[256,1024]{1,0:T(8,128)S(1)}, f32[256,1024]{1,0:T(8,128)S(1)}, u32[]{:S(2)}, u32[]{:S(2)}) %collective-permute-start.13) | collective-permute-done | bytes 1048608 | tf_op jit(solution)/shard_map/ppermute | solution.py:269
  82.6 2.6 %products_far.1 = (f32[256,256]{1,0:T(8,128)S(1)}, f32[256,256]{1,0:T(8,128)}, f32[256,256]{1,0:T(8,128)S(1)}, f32[256,256]{1,0:T(8,128)}) custom-call(f32[8,1024]{1,0:T(8,128)S(1)} %merge.3.mean_ref, f32[256,1024]{1,0:T(8,128)S(1)} %copy-done.1, f32[256,1024]{1,0:T(8,128)S(1)} %collective-permute-done.1.other_ref.refs_1_, ...), custom_call_target="tpu_custom_call" | custom-call | tf_op jit(solution)/shard_map/products_far/pallas_call | solution.py:162
  85.3 1.2 %collective-permute-start.14 = (f32[256,256]{1,0:T(8,128)S(1)}, f32[256,256]{1,0:T(8,128)S(1)}, u32[]{:S(2)}, u32[]{:S(2)}) collective-permute-start(f32[256,256]{1,0:T(8,128)S(1)} %get-tuple-element.44), channel_id=1, source_target_pairs={{0,4},{1,6},{2,5},{3,7},{4,0},{5,2},{6,1},{7,3},{8,15},{9,13},{10,... | collective-permute-start | bytes 786440 | tf_op jit(solution)/shard_map/ppermute | solution.py:269
  87.1 3.7 %collective-permute-start.17 = (f32[256,256]{1,0:T(8,128)}, f32[256,256]{1,0:T(8,128)S(1)}, u32[]{:S(2)}, u32[]{:S(2)}) collective-permute-start(f32[256,256]{1,0:T(8,128)} %get-tuple-element.47), channel_id=1, source_target_pairs={{0,2},{1,0},{2,3},{3,1},{4,6},{5,4},{6,7},{7,5},{8,9},{9,11},{10,8... | collective-permute-start | bytes 786440 | tf_op jit(solution)/shard_map/ppermute | solution.py:269
  91.7 2.8 %collective-permute-done.14.refs_0_ = f32[256,256]{1,0:T(8,128)S(1)} collective-permute-done((f32[256,256]{1,0:T(8,128)S(1)}, f32[256,256]{1,0:T(8,128)S(1)}, u32[]{:S(2)}, u32[]{:S(2)}) %collective-permute-start.14) | collective-permute-done | bytes 262176 | tf_op jit(solution)/shard_map/ppermute | solution.py:269
  96.0 3.9 %collective-permute-done.15.refs_1_ = f32[256,256]{1,0:T(8,128)S(1)} collective-permute-done((f32[256,256]{1,0:T(8,128)}, f32[256,256]{1,0:T(8,128)S(1)}, u32[]{:S(2)}, u32[]{:S(2)}) %collective-permute-start.15) | collective-permute-done | bytes 262176 | tf_op jit(solution)/shard_map/ppermute | solution.py:269
  100.0 2.0 %collective-permute-done.17.refs_3_ = f32[256,256]{1,0:T(8,128)S(1)} collective-permute-done((f32[256,256]{1,0:T(8,128)}, f32[256,256]{1,0:T(8,128)S(1)}, u32[]{:S(2)}, u32[]{:S(2)}) %collective-permute-start.17) | collective-permute-done | bytes 262176 | tf_op jit(solution)/shard_map/ppermute | solution.py:269
  102.0 2.1 %place_last.1 = f32[256,2048]{1,0:T(8,128)} custom-call(f32[256,256]{1,0:T(8,128)S(1)} %collective-permute-done.14.refs_0_, f32[256,256]{1,0:T(8,128)S(1)} %collective-permute-done.15.refs_1_, f32[256,256]{1,0:T(8,128)S(1)} %collective-permute-done.16.refs_2_, f32[256,256]{1,0:T(8,128)S(1)} %collective-permute-done.17.refs_3_, ...), custom_call_target="tpu_custom_call", output_to_operand_aliasing={{}: (7, {})} | custom-call | tf_op jit(solution)/shard_map/place_last/pallas_call | solution.py:216
  (34 shorter events, 7.0 us)
Async XLA Ops:
  0.6 1.5 %collective-permute-start = (f32[1,256]{1,0:T(1,128)}, f32[1,256]{1,0:T(1,128)S(1)}, u32[]{:S(2)}, u32[]{:S(2)}) collective-permute-start(f32[1,256]{1,0:T(1,128)} %bitcast.3), channel_id=1, source_target_pairs={{0,2},{1,3},{2,0},{3,1},{4,6},{5,7},{6,4},{7,5},{8,10},{9,11},{10,... | collective-permute-start | bytes 3080 | tf_op jit(solution)/shard_map/ppermute | solution.py:269
  2.2 4.6 %collective-permute-start.1 = (f32[256,1024]{1,0:T(8,128)}, f32[256,1024]{1,0:T(8,128)S(1)}, u32[]{:S(2)}, u32[]{:S(2)}) collective-permute-start(f32[256,1024]{1,0:T(8,128)} %refs_0_.7), channel_id=1, source_target_pairs={{0,2},{1,3},{2,0},{3,1},{4,6},{5,7},{6,4},{7,5},{8,10},{9,11},{10,... | collective-permute-start | bytes 3145736 | tf_op jit(solution)/shard_map/ppermute | solution.py:269
  2.5 29.8 %collective-permute-start.6 = (f32[256,1024]{1,0:T(8,128)}, f32[256,1024]{1,0:T(8,128)S(1)}, u32[]{:S(2)}, u32[]{:S(2)}) collective-permute-start(f32[256,1024]{1,0:T(8,128)} %refs_0_.7), channel_id=1, source_target_pairs={{0,8},{1,9},{2,26},{3,27},{4,12},{5,13},{6,30},{7,31},{8,16},{9,17... | collective-permute-start | bytes 3145736 | tf_op jit(solution)/shard_map/ppermute | solution.py:269
  5.3 27.1 %collective-permute-start.7 = (f32[256,1024]{1,0:T(8,128)}, f32[256,1024]{1,0:T(8,128)S(1)}, u32[]{:S(2)}, u32[]{:S(2)}) collective-permute-start(f32[256,1024]{1,0:T(8,128)} %refs_0_.7), channel_id=1, source_target_pairs={{0,4},{1,5},{2,6},{3,7},{4,0},{5,1},{6,2},{7,3},{8,12},{9,13},{10,... | collective-permute-start | bytes 3145736 | tf_op jit(solution)/shard_map/ppermute | solution.py:269
  6.8 1.3 %copy-start = (f32[256,1024]{1,0:T(8,128)S(1)}, f32[256,1024]{1,0:T(8,128)}, u32[]{:S(2)}) copy-start(f32[256,1024]{1,0:T(8,128)} %refs_0_.7) | copy-start | bytes 3145732
  8.0 0.7 copy-start.2
  8.7 29.0 %copy-start.1 = (f32[256,1024]{1,0:T(8,128)S(1)}, f32[256,1024]{1,0:T(8,128)}, u32[]{:S(2)}) copy-start(f32[256,1024]{1,0:T(8,128)} %refs_0_.7) | copy-start | bytes 3145732
  9.9 22.4 %collective-permute-start.2 = (f32[8,1024]{1,0:T(8,128)S(1)}, f32[8,1024]{1,0:T(8,128)S(1)}, u32[]{:S(2)}, u32[]{:S(2)}) collective-permute-start(f32[8,1024]{1,0:T(8,128)S(1)} %block_stats.1.refs_0_), channel_id=1, source_target_pairs={{0,8},{1,9},{2,10},{3,11},{4,12},{5,13},{6,14},{7,15},{8,16},{9,17... | collective-permute-start | bytes 98312 | tf_op jit(solution)/shard_map/ppermute | solution.py:269
  11.5 20.8 %collective-permute-start.3 = (f32[8,1024]{1,0:T(8,128)S(1)}, f32[8,1024]{1,0:T(8,128)S(1)}, u32[]{:S(2)}, u32[]{:S(2)}) collective-permute-start(f32[8,1024]{1,0:T(8,128)S(1)} %block_stats.1.refs_0_), channel_id=1, source_target_pairs={{0,16},{1,17},{2,18},{3,19},{4,20},{5,21},{6,22},{7,23},{8,24},{9,... | collective-permute-start | bytes 98312 | tf_op jit(solution)/shard_map/ppermute | solution.py:269
  13.6 18.7 %collective-permute-start.4 = (f32[8,1024]{1,0:T(8,128)S(1)}, f32[8,1024]{1,0:T(8,128)S(1)}, u32[]{:S(2)}, u32[]{:S(2)}) collective-permute-start(f32[8,1024]{1,0:T(8,128)S(1)} %block_stats.1.refs_0_), channel_id=1, source_target_pairs={{0,24},{1,25},{2,26},{3,27},{4,28},{5,29},{6,30},{7,31},{8,0},{9,1... | collective-permute-start | bytes 98312 | tf_op jit(solution)/shard_map/ppermute | solution.py:269
  32.4 5.3 %collective-permute-start.8 = (f32[256,1024]{1,0:T(8,128)S(1)}, f32[256,1024]{1,0:T(8,128)S(1)}, u32[]{:S(2)}, u32[]{:S(2)}) collective-permute-start(f32[256,1024]{1,0:T(8,128)S(1)} %collective-permute-done.7.refs_2_), channel_id=1, source_target_pairs={{0,2},{1,3},{2,0},{3,1},{4,6},{5,7},{6,4},{7,5},{8,10},{9,11},{10,... | collective-permute-start | bytes 3145736 | tf_op jit(solution)/shard_map/ppermute | solution.py:269
  32.4 28.2 %collective-permute-start.18 = (f32[256,1024]{1,0:T(8,128)S(1)}, f32[256,1024]{1,0:T(8,128)S(1)}, u32[]{:S(2)}, u32[]{:S(2)}) collective-permute-start(f32[256,1024]{1,0:T(8,128)S(1)} %collective-permute-done.6.refs_4_), channel_id=1, source_target_pairs={{0,8},{1,9},{2,26},{3,27},{4,12},{5,13},{6,30},{7,31},{8,16},{9,17... | collective-permute-start | bytes 3145736 | tf_op jit(solution)/shard_map/ppermute | solution.py:269
  33.7 3.9 %collective-permute-start.5 = (f32[8,1024]{1,0:T(8,128)S(1)}, f32[8,1024]{1,0:T(8,128)S(1)}, u32[]{:S(2)}, u32[]{:S(2)}) collective-permute-start(f32[8,1024]{1,0:T(8,128)S(1)} %merge.2.refs_0_), channel_id=1, source_target_pairs={{0,4},{1,5},{2,6},{3,7},{4,0},{5,1},{6,2},{7,3},{8,12},{9,13},{10,... | collective-permute-start | bytes 98312 | tf_op jit(solution)/shard_map/ppermute | solution.py:269
  39.6 10.2 %collective-permute-start.10 = (f32[256,256]{1,0:T(8,128)S(1)}, f32[256,256]{1,0:T(8,128)S(1)}, u32[]{:S(2)}, u32[]{:S(2)}) collective-permute-start(f32[256,256]{1,0:T(8,128)S(1)} %get-tuple-element.34), channel_id=1, source_target_pairs={{0,5},{1,7},{2,4},{3,6},{4,1},{5,3},{6,0},{7,2},{8,14},{9,12},{10,... | collective-permute-start | bytes 786440 | tf_op jit(solution)/shard_map/ppermute | solution.py:269
  42.2 8.6 %collective-permute-start.12 = (f32[256,256]{1,0:T(8,128)S(1)}, f32[256,256]{1,0:T(8,128)S(1)}, u32[]{:S(2)}, u32[]{:S(2)}) collective-permute-start(f32[256,256]{1,0:T(8,128)S(1)} %get-tuple-element.37), channel_id=1, source_target_pairs={{0,1},{1,3},{2,0},{3,2},{4,5},{5,7},{6,4},{7,6},{8,10},{9,8},{10,1... | collective-permute-start | bytes 786440 | tf_op jit(solution)/shard_map/ppermute | solution.py:269
  44.3 11.5 %collective-permute-start.9 = (f32[256,256]{1,0:T(8,128)S(1)}, f32[256,256]{1,0:T(8,128)S(1)}, u32[]{:S(2)}, u32[]{:S(2)}) collective-permute-start(f32[256,256]{1,0:T(8,128)S(1)} %get-tuple-element.33), channel_id=1, source_target_pairs={{0,7},{1,5},{2,6},{3,4},{4,3},{5,1},{6,2},{7,0},{8,12},{9,14},{10,... | collective-permute-start | bytes 786440 | tf_op jit(solution)/shard_map/ppermute | solution.py:269
  44.3 12.1 %collective-permute-start.11 = (f32[256,256]{1,0:T(8,128)S(1)}, f32[256,256]{1,0:T(8,128)S(1)}, u32[]{:S(2)}, u32[]{:S(2)}) collective-permute-start(f32[256,256]{1,0:T(8,128)S(1)} %get-tuple-element.35.refs_2_), channel_id=1, source_target_pairs={{0,3},{3,0},{4,7},{7,4},{9,10},{10,9},{13,14},{14,13},{17,18},{18,... | collective-permute-start | bytes 786440 | tf_op jit(solution)/shard_map/ppermute | solution.py:269
  56.4 26.3 %collective-permute-start.13 = (f32[256,1024]{1,0:T(8,128)S(1)}, f32[256,1024]{1,0:T(8,128)S(1)}, u32[]{:S(2)}, u32[]{:S(2)}) collective-permute-start(f32[256,1024]{1,0:T(8,128)S(1)} %copy-done.1), channel_id=1, source_target_pairs={{0,24},{1,25},{2,10},{3,11},{4,28},{5,29},{6,14},{7,15},{8,0},{9,1... | collective-permute-start | bytes 3145736 | tf_op jit(solution)/shard_map/ppermute | solution.py:269
  62.5 23.9 %collective-permute-start.19 = (f32[512,256]{1,0:T(8,128)S(1)}, f32[512,256]{1,0:T(8,128)S(1)}, u32[]{:S(2)}, u32[]{:S(2)}) collective-permute-start(f32[512,256]{1,0:T(8,128)S(1)} %get-tuple-element.50), channel_id=1, source_target_pairs={{0,1},{1,0},{2,3},{3,2},{4,5},{5,4},{6,7},{7,6},{8,9},{9,8},{10,11... | collective-permute-start | bytes 1572872 | tf_op jit(solution)/shard_map/ppermute | solution.py:269
  63.8 23.3 %collective-permute-start.20 = (f32[512,256]{1,0:T(8,128)S(1)}, f32[512,256]{1,0:T(8,128)S(1)}, u32[]{:S(2)}, u32[]{:S(2)}) collective-permute-start(f32[512,256]{1,0:T(8,128)S(1)} %get-tuple-element.52), channel_id=1, source_target_pairs={{0,4},{1,5},{2,6},{3,7},{4,0},{5,1},{6,2},{7,3},{8,12},{9,13},{10,... | collective-permute-start | bytes 1572872 | tf_op jit(solution)/shard_map/ppermute | solution.py:269
  65.3 25.6 %collective-permute-start.21 = (f32[512,256]{1,0:T(8,128)S(1)}, f32[512,256]{1,0:T(8,128)S(1)}, u32[]{:S(2)}, u32[]{:S(2)}) collective-permute-start(f32[512,256]{1,0:T(8,128)S(1)} %get-tuple-element.53), channel_id=1, source_target_pairs={{0,5},{1,4},{2,7},{3,6},{4,1},{5,0},{6,3},{7,2},{8,13},{9,12},{10,... | collective-permute-start | bytes 1572872 | tf_op jit(solution)/shard_map/ppermute | solution.py:269
  85.3 9.2 %collective-permute-start.14 = (f32[256,256]{1,0:T(8,128)S(1)}, f32[256,256]{1,0:T(8,128)S(1)}, u32[]{:S(2)}, u32[]{:S(2)}) collective-permute-start(f32[256,256]{1,0:T(8,128)S(1)} %get-tuple-element.44), channel_id=1, source_target_pairs={{0,4},{1,6},{2,5},{3,7},{4,0},{5,2},{6,1},{7,3},{8,15},{9,13},{10,... | collective-permute-start | bytes 786440 | tf_op jit(solution)/shard_map/ppermute | solution.py:269
  86.4 13.5 %collective-permute-start.15 = (f32[256,256]{1,0:T(8,128)}, f32[256,256]{1,0:T(8,128)S(1)}, u32[]{:S(2)}, u32[]{:S(2)}) collective-permute-start(f32[256,256]{1,0:T(8,128)} %get-tuple-element.45), channel_id=1, source_target_pairs={{0,6},{1,4},{2,7},{3,5},{4,2},{5,0},{6,3},{7,1},{8,13},{9,15},{10,... | collective-permute-start | bytes 786440 | tf_op jit(solution)/shard_map/ppermute | solution.py:269
  86.4 13.5 %collective-permute-start.16 = (f32[256,256]{1,0:T(8,128)S(1)}, f32[256,256]{1,0:T(8,128)S(1)}, u32[]{:S(2)}, u32[]{:S(2)}) collective-permute-start(f32[256,256]{1,0:T(8,128)S(1)} %get-tuple-element.46.refs_4_), channel_id=1, source_target_pairs={{1,2},{2,1},{5,6},{6,5},{8,11},{11,8},{12,15},{15,12},{16,19},{19,... | collective-permute-start | bytes 786440 | tf_op jit(solution)/shard_map/ppermute | solution.py:269
  87.1 14.8 %collective-permute-start.17 = (f32[256,256]{1,0:T(8,128)}, f32[256,256]{1,0:T(8,128)S(1)}, u32[]{:S(2)}, u32[]{:S(2)}) collective-permute-start(f32[256,256]{1,0:T(8,128)} %get-tuple-element.47), channel_id=1, source_target_pairs={{0,2},{1,0},{2,3},{3,1},{4,6},{5,4},{6,7},{7,5},{8,9},{9,11},{10,8... | collective-permute-start | bytes 786440 | tf_op jit(solution)/shard_map/ppermute | solution.py:269
  91.7 10.2 %collective-permute-start.22 = (f32[256,256]{1,0:T(8,128)}, f32[256,256]{1,0:T(8,128)}, u32[]{:S(2)}, u32[]{:S(2)}) collective-permute-start(f32[256,256]{1,0:T(8,128)} %get-tuple-element.54), channel_id=1, source_target_pairs={{0,2},{1,3},{2,0},{3,1},{4,6},{5,7},{6,4},{7,5},{8,10},{9,11},{10,... | collective-permute-start | bytes 786440 | tf_op jit(solution)/shard_map/ppermute | solution.py:269
  94.5 7.5 %collective-permute-start.23 = (f32[256,256]{1,0:T(8,128)}, f32[256,256]{1,0:T(8,128)}, u32[]{:S(2)}, u32[]{:S(2)}) collective-permute-start(f32[256,256]{1,0:T(8,128)} %get-tuple-element.55), channel_id=1, source_target_pairs={{0,2},{1,3},{2,0},{3,1},{4,6},{5,7},{6,4},{7,5},{8,10},{9,11},{10,... | collective-permute-start | bytes 786440 | tf_op jit(solution)/shard_map/ppermute | solution.py:269

commit v9 on v7

--- a/solution.py
+++ b/solution.py
@@ -8,7 +8,7 @@
 from jax.sharding import PartitionSpec as P
 
 BOTH = ("smp", "par")
-VMEM_LIMIT = 16 * 1024 * 1024
+VMEM_LIMIT = 10 * 1024 * 1024
 LONG = pl.CostEstimate(flops=4_000_000_000, bytes_accessed=0, transcendentals=0)
 FREE = pl.CostEstimate(flops=0, bytes_accessed=0, transcendentals=0)
 

time: 103 us -> 103 us (level)
  no operation moved by 1% of the time
where the time goes in v9:
time: 103 us
  waiting for transfers between devices  52.6 us (51%)
  starting transfers between devices  32.7 us (32%)
  Pallas kernels  14.4 us (14%)
  local copies, waits for them, and re-layouts  1.94 us (2%)
    ppermute x24, waiting for transfers between devices, send(): return lax.ppermute(value, BOTH, pairs)  52.6 us
    ppermute x24, starting transfers between devices, send(): return lax.ppermute(value, BOTH, pairs)  32.7 us
    pallas_call x8, Pallas kernels, kernel_call(): pl.pallas_call(kernel, out_shape=[jax.ShapeDtypeStruct(s, jnp.float32) fo...  10.4 us
    pallas_call x3, Pallas kernels, place(): pl.pallas_call(functools.partial(place_kernel, dims, apart, [[flag for _,...  4.01 us
  transfers between devices with their start and end apart: 24, of which 10 were waited for; matrix products, arithmetic and copies ran while one was open for 1% of the time, Pallas kernels for 12%

profile of v9, /device:TPU:0, one launch (start us, length us, event | category | flops | bytes accessed | tf_op | source)
XLA Modules:
  0.0 103.0 jit_solution(15862900509948457656)
XLA Ops:
  1.2 3.0 %collective-permute-start.6 = (f32[256,1024]{1,0:T(8,128)}, f32[256,1024]{1,0:T(8,128)S(1)}, u32[]{:S(2)}, u32[]{:S(2)}) collective-permute-start(f32[256,1024]{1,0:T(8,128)} %refs_0_.7), channel_id=1, source_target_pairs={{0,8},{1,9},{2,26},{3,27},{4,12},{5,13},{6,30},{7,31},{8,16},{9,17... | collective-permute-start | bytes 3145736 | tf_op jit(solution)/shard_map/ppermute | solution.py:269
  4.2 2.3 %collective-permute-start.7 = (f32[256,1024]{1,0:T(8,128)}, f32[256,1024]{1,0:T(8,128)S(1)}, u32[]{:S(2)}, u32[]{:S(2)}) collective-permute-start(f32[256,1024]{1,0:T(8,128)} %refs_0_.7), channel_id=1, source_target_pairs={{0,4},{1,5},{2,6},{3,7},{4,0},{5,1},{6,2},{7,3},{8,12},{9,13},{10,... | collective-permute-start | bytes 3145736 | tf_op jit(solution)/shard_map/ppermute | solution.py:269
  6.5 1.3 %copy-done = f32[256,1024]{1,0:T(8,128)S(1)} copy-done((f32[256,1024]{1,0:T(8,128)S(1)}, f32[256,1024]{1,0:T(8,128)}, u32[]{:S(2)}) %copy-start) | copy-done | bytes 1048600
  8.4 1.2 %block_stats.1.refs_0_ = f32[8,1024]{1,0:T(8,128)S(1)} custom-call(f32[256,1024]{1,0:T(8,128)S(1)} %copy-done, f32[256,1024]{1,0:T(8,128)S(1)} %collective-permute-done.other_ref.refs_1_, f32[1,256]{1,0:T(1,128)S(1)} %bitcast.4, f32[1,256]{1,0:T(1,128)S(1)} %collective-permute-done.1.other_coef_ref), custom_call_target="tpu_custom_call" | custom-call | tf_op jit(solution)/shard_map/block_stats/pallas_call | solution.py:162
  9.6 1.6 %collective-permute-start.2 = (f32[8,1024]{1,0:T(8,128)S(1)}, f32[8,1024]{1,0:T(8,128)S(1)}, u32[]{:S(2)}, u32[]{:S(2)}) collective-permute-start(f32[8,1024]{1,0:T(8,128)S(1)} %block_stats.1.refs_0_), channel_id=1, source_target_pairs={{0,8},{1,9},{2,10},{3,11},{4,12},{5,13},{6,14},{7,15},{8,16},{9,17... | collective-permute-start | bytes 98312 | tf_op jit(solution)/shard_map/ppermute | solution.py:269
  11.2 2.6 %collective-permute-start.3 = (f32[8,1024]{1,0:T(8,128)S(1)}, f32[8,1024]{1,0:T(8,128)S(1)}, u32[]{:S(2)}, u32[]{:S(2)}) collective-permute-start(f32[8,1024]{1,0:T(8,128)S(1)} %block_stats.1.refs_0_), channel_id=1, source_target_pairs={{0,16},{1,17},{2,18},{3,19},{4,20},{5,21},{6,22},{7,23},{8,24},{9,... | collective-permute-start | bytes 98312 | tf_op jit(solution)/shard_map/ppermute | solution.py:269
  13.8 1.3 %collective-permute-start.4 = (f32[8,1024]{1,0:T(8,128)S(1)}, f32[8,1024]{1,0:T(8,128)S(1)}, u32[]{:S(2)}, u32[]{:S(2)}) collective-permute-start(f32[8,1024]{1,0:T(8,128)S(1)} %block_stats.1.refs_0_), channel_id=1, source_target_pairs={{0,24},{1,25},{2,26},{3,27},{4,28},{5,29},{6,30},{7,31},{8,0},{9,1... | collective-permute-start | bytes 98312 | tf_op jit(solution)/shard_map/ppermute | solution.py:269
  15.2 15.9 %collective-permute-done.2.refs_1_ = f32[8,1024]{1,0:T(8,128)S(1)} collective-permute-done((f32[8,1024]{1,0:T(8,128)S(1)}, f32[8,1024]{1,0:T(8,128)S(1)}, u32[]{:S(2)}, u32[]{:S(2)}) %collective-permute-start.2) | collective-permute-done | bytes 32800 | tf_op jit(solution)/shard_map/ppermute | solution.py:269
  31.3 1.3 %collective-permute-start.18 = (f32[256,1024]{1,0:T(8,128)S(1)}, f32[256,1024]{1,0:T(8,128)S(1)}, u32[]{:S(2)}, u32[]{:S(2)}) collective-permute-start(f32[256,1024]{1,0:T(8,128)S(1)} %collective-permute-done.6.refs_4_), channel_id=1, source_target_pairs={{0,8},{1,9},{2,26},{3,27},{4,12},{5,13},{6,30},{7,31},{8,16},{9,17... | collective-permute-start | bytes 3145736 | tf_op jit(solution)/shard_map/ppermute | solution.py:269
  32.6 1.5 %collective-permute-start.5 = (f32[8,1024]{1,0:T(8,128)S(1)}, f32[8,1024]{1,0:T(8,128)S(1)}, u32[]{:S(2)}, u32[]{:S(2)}) collective-permute-start(f32[8,1024]{1,0:T(8,128)S(1)} %merge.2.refs_0_), channel_id=1, source_target_pairs={{0,4},{1,5},{2,6},{3,7},{4,0},{5,1},{6,2},{7,3},{8,12},{9,13},{10,... | collective-permute-start | bytes 98312 | tf_op jit(solution)/shard_map/ppermute | solution.py:269
  34.1 2.4 %collective-permute-done.5.refs_1_ = f32[8,1024]{1,0:T(8,128)S(1)} collective-permute-done((f32[8,1024]{1,0:T(8,128)S(1)}, f32[8,1024]{1,0:T(8,128)S(1)}, u32[]{:S(2)}, u32[]{:S(2)}) %collective-permute-start.5) | collective-permute-done | bytes 32800 | tf_op jit(solution)/shard_map/ppermute | solution.py:269
  36.5 1.9 %products_near.1 = (f32[256,256]{1,0:T(8,128)S(1)}, f32[256,256]{1,0:T(8,128)S(1)}, f32[256,256]{1,0:T(8,128)S(1)}, f32[256,256]{1,0:T(8,128)S(1)}) custom-call(f32[8,1024]{1,0:T(8,128)S(1)} %merge.3.mean_ref, f32[256,1024]{1,0:T(8,128)S(1)} %copy-done.1, f32[256,1024]{1,0:T(8,128)S(1)} %collective-permute-done.other_ref.refs_1_, ...), custom_call_target="tpu_custom_call" | custom-call | tf_op jit(solution)/shard_map/products_near/pallas_call | solution.py:162
  38.4 2.5 %collective-permute-start.10 = (f32[256,256]{1,0:T(8,128)S(1)}, f32[256,256]{1,0:T(8,128)S(1)}, u32[]{:S(2)}, u32[]{:S(2)}) collective-permute-start(f32[256,256]{1,0:T(8,128)S(1)} %get-tuple-element.34), channel_id=1, source_target_pairs={{0,5},{1,7},{2,4},{3,6},{4,1},{5,3},{6,0},{7,2},{8,14},{9,12},{10,... | collective-permute-start | bytes 786440 | tf_op jit(solution)/shard_map/ppermute | solution.py:269
  40.9 2.3 %collective-permute-start.12 = (f32[256,256]{1,0:T(8,128)S(1)}, f32[256,256]{1,0:T(8,128)S(1)}, u32[]{:S(2)}, u32[]{:S(2)}) collective-permute-start(f32[256,256]{1,0:T(8,128)S(1)} %get-tuple-element.37), channel_id=1, source_target_pairs={{0,1},{1,3},{2,0},{3,2},{4,5},{5,7},{6,4},{7,6},{8,10},{9,8},{10,1... | collective-permute-start | bytes 786440 | tf_op jit(solution)/shard_map/ppermute | solution.py:269
  43.2 3.6 %collective-permute-start.11 = (f32[256,256]{1,0:T(8,128)S(1)}, f32[256,256]{1,0:T(8,128)S(1)}, u32[]{:S(2)}, u32[]{:S(2)}) collective-permute-start(f32[256,256]{1,0:T(8,128)S(1)} %get-tuple-element.35.refs_2_), channel_id=1, source_target_pairs={{0,3},{3,0},{4,7},{7,4},{9,10},{10,9},{13,14},{14,13},{17,18},{18,... | collective-permute-start | bytes 786440 | tf_op jit(solution)/shard_map/ppermute | solution.py:269
  46.8 1.9 %products_level.1 = (f32[512,256]{1,0:T(8,128)S(1)}, f32[512,256]{1,0:T(8,128)S(1)}) custom-call(f32[8,1024]{1,0:T(8,128)S(1)} %merge.3.mean_ref, f32[256,1024]{1,0:T(8,128)S(1)} %copy-done.1, f32[256,1024]{1,0:T(8,128)S(1)} %collective-permute-done.other_ref.refs_1_, f32[256,1024]{1,0:T(8,128)S(1)} %collective-permute-done.7.refs_2_, ...), custom_call_target="tpu_custom_call" | custom-call | tf_op jit(solution)/shard_map/products_level/pallas_call | solution.py:162
  48.8 1.0 collective-permute-done.12.refs_1_
  49.8 5.0 %collective-permute-done.9.refs_3_ = f32[256,256]{1,0:T(8,128)S(1)} collective-permute-done((f32[256,256]{1,0:T(8,128)S(1)}, f32[256,256]{1,0:T(8,128)S(1)}, u32[]{:S(2)}, u32[]{:S(2)}) %collective-permute-start.9) | collective-permute-done | bytes 262176 | tf_op jit(solution)/shard_map/ppermute | solution.py:269
  56.2 3.4 %collective-permute-done.18.refs_4_ = f32[256,1024]{1,0:T(8,128)S(1)} collective-permute-done((f32[256,1024]{1,0:T(8,128)S(1)}, f32[256,1024]{1,0:T(8,128)S(1)}, u32[]{:S(2)}, u32[]{:S(2)}) %collective-permute-start.18) | collective-permute-done | bytes 1048608 | tf_op jit(solution)/shard_map/ppermute | solution.py:269
  59.6 1.9 %products_across.1 = (f32[512,256]{1,0:T(8,128)S(1)}, f32[512,256]{1,0:T(8,128)S(1)}, f32[512,256]{1,0:T(8,128)S(1)}, f32[512,256]{1,0:T(8,128)S(1)}) custom-call(f32[8,1024]{1,0:T(8,128)S(1)} %merge.3.mean_ref, f32[256,1024]{1,0:T(8,128)S(1)} %copy-done.1, f32[256,1024]{1,0:T(8,128)S(1)} %collective-permute-done.other_ref.refs_1_, ...), custom_call_target="tpu_custom_call" | custom-call | flops 4000000000 | tf_op jit(solution)/shard_map/products_across/pallas_call | solution.py:162
  61.5 1.3 %collective-permute-start.19 = (f32[512,256]{1,0:T(8,128)S(1)}, f32[512,256]{1,0:T(8,128)S(1)}, u32[]{:S(2)}, u32[]{:S(2)}) collective-permute-start(f32[512,256]{1,0:T(8,128)S(1)} %get-tuple-element.50), channel_id=1, source_target_pairs={{0,1},{1,0},{2,3},{3,2},{4,5},{5,4},{6,7},{7,6},{8,9},{9,8},{10,11... | collective-permute-start | bytes 1572872 | tf_op jit(solution)/shard_map/ppermute | solution.py:269
  62.8 1.5 %collective-permute-start.20 = (f32[512,256]{1,0:T(8,128)S(1)}, f32[512,256]{1,0:T(8,128)S(1)}, u32[]{:S(2)}, u32[]{:S(2)}) collective-permute-start(f32[512,256]{1,0:T(8,128)S(1)} %get-tuple-element.52), channel_id=1, source_target_pairs={{0,4},{1,5},{2,6},{3,7},{4,0},{5,1},{6,2},{7,3},{8,12},{9,13},{10,... | collective-permute-start | bytes 1572872 | tf_op jit(solution)/shard_map/ppermute | solution.py:269
  65.1 1.0 place_near.1.refs_4_
  66.1 15.5 %collective-permute-done.13.refs_4_ = f32[256,1024]{1,0:T(8,128)S(1)} collective-permute-done((f32[256,1024]{1,0:T(8,128)S(1)}, f32[256,1024]{1,0:T(8,128)S(1)}, u32[]{:S(2)}, u32[]{:S(2)}) %collective-permute-start.13) | collective-permute-done | bytes 1048608 | tf_op jit(solution)/shard_map/ppermute | solution.py:269
  81.6 2.6 %products_far.1 = (f32[256,256]{1,0:T(8,128)S(1)}, f32[256,256]{1,0:T(8,128)}, f32[256,256]{1,0:T(8,128)S(1)}, f32[256,256]{1,0:T(8,128)}) custom-call(f32[8,1024]{1,0:T(8,128)S(1)} %merge.3.mean_ref, f32[256,1024]{1,0:T(8,128)S(1)} %copy-done.1, f32[256,1024]{1,0:T(8,128)S(1)} %collective-permute-done.other_ref.refs_1_, ...), custom_call_target="tpu_custom_call" | custom-call | tf_op jit(solution)/shard_map/products_far/pallas_call | solution.py:162
  84.2 1.2 %collective-permute-start.14 = (f32[256,256]{1,0:T(8,128)S(1)}, f32[256,256]{1,0:T(8,128)S(1)}, u32[]{:S(2)}, u32[]{:S(2)}) collective-permute-start(f32[256,256]{1,0:T(8,128)S(1)} %get-tuple-element.44), channel_id=1, source_target_pairs={{0,4},{1,6},{2,5},{3,7},{4,0},{5,2},{6,1},{7,3},{8,15},{9,13},{10,... | collective-permute-start | bytes 786440 | tf_op jit(solution)/shard_map/ppermute | solution.py:269
  86.1 3.7 %collective-permute-start.17 = (f32[256,256]{1,0:T(8,128)}, f32[256,256]{1,0:T(8,128)S(1)}, u32[]{:S(2)}, u32[]{:S(2)}) collective-permute-start(f32[256,256]{1,0:T(8,128)} %get-tuple-element.47), channel_id=1, source_target_pairs={{0,2},{1,0},{2,3},{3,1},{4,6},{5,4},{6,7},{7,5},{8,9},{9,11},{10,8... | collective-permute-start | bytes 786440 | tf_op jit(solution)/shard_map/ppermute | solution.py:269
  90.7 2.7 %collective-permute-done.14.refs_0_ = f32[256,256]{1,0:T(8,128)S(1)} collective-permute-done((f32[256,256]{1,0:T(8,128)S(1)}, f32[256,256]{1,0:T(8,128)S(1)}, u32[]{:S(2)}, u32[]{:S(2)}) %collective-permute-start.14) | collective-permute-done | bytes 262176 | tf_op jit(solution)/shard_map/ppermute | solution.py:269
  93.5 0.9 place_most.1.refs_7_
  95.0 3.9 %collective-permute-done.15.refs_1_ = f32[256,256]{1,0:T(8,128)S(1)} collective-permute-done((f32[256,256]{1,0:T(8,128)}, f32[256,256]{1,0:T(8,128)S(1)}, u32[]{:S(2)}, u32[]{:S(2)}) %collective-permute-start.15) | collective-permute-done | bytes 262176 | tf_op jit(solution)/shard_map/ppermute | solution.py:269
  98.9 2.0 %collective-permute-done.17.refs_3_ = f32[256,256]{1,0:T(8,128)S(1)} collective-permute-done((f32[256,256]{1,0:T(8,128)}, f32[256,256]{1,0:T(8,128)S(1)}, u32[]{:S(2)}, u32[]{:S(2)}) %collective-permute-start.17) | collective-permute-done | bytes 262176 | tf_op jit(solution)/shard_map/ppermute | solution.py:269
  100.9 2.1 %place_last.1 = f32[256,2048]{1,0:T(8,128)} custom-call(f32[256,256]{1,0:T(8,128)S(1)} %collective-permute-done.14.refs_0_, f32[256,256]{1,0:T(8,128)S(1)} %collective-permute-done.15.refs_1_, f32[256,256]{1,0:T(8,128)S(1)} %collective-permute-done.16.refs_2_, f32[256,256]{1,0:T(8,128)S(1)} %collective-permute-done.17.refs_3_, ...), custom_call_target="tpu_custom_call", output_to_operand_aliasing={{}: (7, {})} | custom-call | tf_op jit(solution)/shard_map/place_last/pallas_call | solution.py:216
  (34 shorter events, 5.9 us)
Async XLA Ops:
  0.6 5.9 %collective-permute-start = (f32[256,1024]{1,0:T(8,128)}, f32[256,1024]{1,0:T(8,128)S(1)}, u32[]{:S(2)}, u32[]{:S(2)}) collective-permute-start(f32[256,1024]{1,0:T(8,128)} %refs_0_.7), channel_id=1, source_target_pairs={{0,2},{1,3},{2,0},{3,1},{4,6},{5,7},{6,4},{7,5},{8,10},{9,11},{10,... | collective-permute-start | bytes 3145736 | tf_op jit(solution)/shard_map/ppermute | solution.py:269
  1.1 3.1 %collective-permute-start.1 = (f32[1,256]{1,0:T(1,128)}, f32[1,256]{1,0:T(1,128)S(1)}, u32[]{:S(2)}, u32[]{:S(2)}) collective-permute-start(f32[1,256]{1,0:T(1,128)} %bitcast.3), channel_id=1, source_target_pairs={{0,2},{1,3},{2,0},{3,1},{4,6},{5,7},{6,4},{7,5},{8,10},{9,11},{10,... | collective-permute-start | bytes 3080 | tf_op jit(solution)/shard_map/ppermute | solution.py:269
  1.2 29.9 %collective-permute-start.6 = (f32[256,1024]{1,0:T(8,128)}, f32[256,1024]{1,0:T(8,128)S(1)}, u32[]{:S(2)}, u32[]{:S(2)}) collective-permute-start(f32[256,1024]{1,0:T(8,128)} %refs_0_.7), channel_id=1, source_target_pairs={{0,8},{1,9},{2,26},{3,27},{4,12},{5,13},{6,30},{7,31},{8,16},{9,17... | collective-permute-start | bytes 3145736 | tf_op jit(solution)/shard_map/ppermute | solution.py:269
  4.2 26.9 %collective-permute-start.7 = (f32[256,1024]{1,0:T(8,128)}, f32[256,1024]{1,0:T(8,128)S(1)}, u32[]{:S(2)}, u32[]{:S(2)}) collective-permute-start(f32[256,1024]{1,0:T(8,128)} %refs_0_.7), channel_id=1, source_target_pairs={{0,4},{1,5},{2,6},{3,7},{4,0},{5,1},{6,2},{7,3},{8,12},{9,13},{10,... | collective-permute-start | bytes 3145736 | tf_op jit(solution)/shard_map/ppermute | solution.py:269
  6.5 1.3 %copy-start = (f32[256,1024]{1,0:T(8,128)S(1)}, f32[256,1024]{1,0:T(8,128)}, u32[]{:S(2)}) copy-start(f32[256,1024]{1,0:T(8,128)} %refs_0_.7) | copy-start | bytes 3145732
  7.8 0.7 copy-start.2
  8.4 28.1 %copy-start.1 = (f32[256,1024]{1,0:T(8,128)S(1)}, f32[256,1024]{1,0:T(8,128)}, u32[]{:S(2)}) copy-start(f32[256,1024]{1,0:T(8,128)} %refs_0_.7) | copy-start | bytes 3145732
  9.6 21.5 %collective-permute-start.2 = (f32[8,1024]{1,0:T(8,128)S(1)}, f32[8,1024]{1,0:T(8,128)S(1)}, u32[]{:S(2)}, u32[]{:S(2)}) collective-permute-start(f32[8,1024]{1,0:T(8,128)S(1)} %block_stats.1.refs_0_), channel_id=1, source_target_pairs={{0,8},{1,9},{2,10},{3,11},{4,12},{5,13},{6,14},{7,15},{8,16},{9,17... | collective-permute-start | bytes 98312 | tf_op jit(solution)/shard_map/ppermute | solution.py:269
  11.2 19.9 %collective-permute-start.3 = (f32[8,1024]{1,0:T(8,128)S(1)}, f32[8,1024]{1,0:T(8,128)S(1)}, u32[]{:S(2)}, u32[]{:S(2)}) collective-permute-start(f32[8,1024]{1,0:T(8,128)S(1)} %block_stats.1.refs_0_), channel_id=1, source_target_pairs={{0,16},{1,17},{2,18},{3,19},{4,20},{5,21},{6,22},{7,23},{8,24},{9,... | collective-permute-start | bytes 98312 | tf_op jit(solution)/shard_map/ppermute | solution.py:269
  13.8 17.3 %collective-permute-start.4 = (f32[8,1024]{1,0:T(8,128)S(1)}, f32[8,1024]{1,0:T(8,128)S(1)}, u32[]{:S(2)}, u32[]{:S(2)}) collective-permute-start(f32[8,1024]{1,0:T(8,128)S(1)} %block_stats.1.refs_0_), channel_id=1, source_target_pairs={{0,24},{1,25},{2,26},{3,27},{4,28},{5,29},{6,30},{7,31},{8,0},{9,1... | collective-permute-start | bytes 98312 | tf_op jit(solution)/shard_map/ppermute | solution.py:269
  31.1 5.4 %collective-permute-start.8 = (f32[256,1024]{1,0:T(8,128)S(1)}, f32[256,1024]{1,0:T(8,128)S(1)}, u32[]{:S(2)}, u32[]{:S(2)}) collective-permute-start(f32[256,1024]{1,0:T(8,128)S(1)} %collective-permute-done.7.refs_2_), channel_id=1, source_target_pairs={{0,2},{1,3},{2,0},{3,1},{4,6},{5,7},{6,4},{7,5},{8,10},{9,11},{10,... | collective-permute-start | bytes 3145736 | tf_op jit(solution)/shard_map/ppermute | solution.py:269
  31.3 28.3 %collective-permute-start.18 = (f32[256,1024]{1,0:T(8,128)S(1)}, f32[256,1024]{1,0:T(8,128)S(1)}, u32[]{:S(2)}, u32[]{:S(2)}) collective-permute-start(f32[256,1024]{1,0:T(8,128)S(1)} %collective-permute-done.6.refs_4_), channel_id=1, source_target_pairs={{0,8},{1,9},{2,26},{3,27},{4,12},{5,13},{6,30},{7,31},{8,16},{9,17... | collective-permute-start | bytes 3145736 | tf_op jit(solution)/shard_map/ppermute | solution.py:269
  32.6 3.9 %collective-permute-start.5 = (f32[8,1024]{1,0:T(8,128)S(1)}, f32[8,1024]{1,0:T(8,128)S(1)}, u32[]{:S(2)}, u32[]{:S(2)}) collective-permute-start(f32[8,1024]{1,0:T(8,128)S(1)} %merge.2.refs_0_), channel_id=1, source_target_pairs={{0,4},{1,5},{2,6},{3,7},{4,0},{5,1},{6,2},{7,3},{8,12},{9,13},{10,... | collective-permute-start | bytes 98312 | tf_op jit(solution)/shard_map/ppermute | solution.py:269
  38.4 10.3 %collective-permute-start.10 = (f32[256,256]{1,0:T(8,128)S(1)}, f32[256,256]{1,0:T(8,128)S(1)}, u32[]{:S(2)}, u32[]{:S(2)}) collective-permute-start(f32[256,256]{1,0:T(8,128)S(1)} %get-tuple-element.34), channel_id=1, source_target_pairs={{0,5},{1,7},{2,4},{3,6},{4,1},{5,3},{6,0},{7,2},{8,14},{9,12},{10,... | collective-permute-start | bytes 786440 | tf_op jit(solution)/shard_map/ppermute | solution.py:269
  40.9 8.8 %collective-permute-start.12 = (f32[256,256]{1,0:T(8,128)S(1)}, f32[256,256]{1,0:T(8,128)S(1)}, u32[]{:S(2)}, u32[]{:S(2)}) collective-permute-start(f32[256,256]{1,0:T(8,128)S(1)} %get-tuple-element.37), channel_id=1, source_target_pairs={{0,1},{1,3},{2,0},{3,2},{4,5},{5,7},{6,4},{7,6},{8,10},{9,8},{10,1... | collective-permute-start | bytes 786440 | tf_op jit(solution)/shard_map/ppermute | solution.py:269
  43.2 11.5 %collective-permute-start.9 = (f32[256,256]{1,0:T(8,128)S(1)}, f32[256,256]{1,0:T(8,128)S(1)}, u32[]{:S(2)}, u32[]{:S(2)}) collective-permute-start(f32[256,256]{1,0:T(8,128)S(1)} %get-tuple-element.33), channel_id=1, source_target_pairs={{0,7},{1,5},{2,6},{3,4},{4,3},{5,1},{6,2},{7,0},{8,12},{9,14},{10,... | collective-permute-start | bytes 786440 | tf_op jit(solution)/shard_map/ppermute | solution.py:269
  43.2 12.1 %collective-permute-start.11 = (f32[256,256]{1,0:T(8,128)S(1)}, f32[256,256]{1,0:T(8,128)S(1)}, u32[]{:S(2)}, u32[]{:S(2)}) collective-permute-start(f32[256,256]{1,0:T(8,128)S(1)} %get-tuple-element.35.refs_2_), channel_id=1, source_target_pairs={{0,3},{3,0},{4,7},{7,4},{9,10},{10,9},{13,14},{14,13},{17,18},{18,... | collective-permute-start | bytes 786440 | tf_op jit(solution)/shard_map/ppermute | solution.py:269
  55.3 26.3 %collective-permute-start.13 = (f32[256,1024]{1,0:T(8,128)S(1)}, f32[256,1024]{1,0:T(8,128)S(1)}, u32[]{:S(2)}, u32[]{:S(2)}) collective-permute-start(f32[256,1024]{1,0:T(8,128)S(1)} %copy-done.1), channel_id=1, source_target_pairs={{0,24},{1,25},{2,10},{3,11},{4,28},{5,29},{6,14},{7,15},{8,0},{9,1... | collective-permute-start | bytes 3145736 | tf_op jit(solution)/shard_map/ppermute | solution.py:269
  61.5 23.9 %collective-permute-start.19 = (f32[512,256]{1,0:T(8,128)S(1)}, f32[512,256]{1,0:T(8,128)S(1)}, u32[]{:S(2)}, u32[]{:S(2)}) collective-permute-start(f32[512,256]{1,0:T(8,128)S(1)} %get-tuple-element.50), channel_id=1, source_target_pairs={{0,1},{1,0},{2,3},{3,2},{4,5},{5,4},{6,7},{7,6},{8,9},{9,8},{10,11... | collective-permute-start | bytes 1572872 | tf_op jit(solution)/shard_map/ppermute | solution.py:269
  62.8 23.3 %collective-permute-start.20 = (f32[512,256]{1,0:T(8,128)S(1)}, f32[512,256]{1,0:T(8,128)S(1)}, u32[]{:S(2)}, u32[]{:S(2)}) collective-permute-start(f32[512,256]{1,0:T(8,128)S(1)} %get-tuple-element.52), channel_id=1, source_target_pairs={{0,4},{1,5},{2,6},{3,7},{4,0},{5,1},{6,2},{7,3},{8,12},{9,13},{10,... | collective-permute-start | bytes 1572872 | tf_op jit(solution)/shard_map/ppermute | solution.py:269
  64.3 25.6 %collective-permute-start.21 = (f32[512,256]{1,0:T(8,128)S(1)}, f32[512,256]{1,0:T(8,128)S(1)}, u32[]{:S(2)}, u32[]{:S(2)}) collective-permute-start(f32[512,256]{1,0:T(8,128)S(1)} %get-tuple-element.53), channel_id=1, source_target_pairs={{0,5},{1,4},{2,7},{3,6},{4,1},{5,0},{6,3},{7,2},{8,13},{9,12},{10,... | collective-permute-start | bytes 1572872 | tf_op jit(solution)/shard_map/ppermute | solution.py:269
  84.2 9.2 %collective-permute-start.14 = (f32[256,256]{1,0:T(8,128)S(1)}, f32[256,256]{1,0:T(8,128)S(1)}, u32[]{:S(2)}, u32[]{:S(2)}) collective-permute-start(f32[256,256]{1,0:T(8,128)S(1)} %get-tuple-element.44), channel_id=1, source_target_pairs={{0,4},{1,6},{2,5},{3,7},{4,0},{5,2},{6,1},{7,3},{8,15},{9,13},{10,... | collective-permute-start | bytes 786440 | tf_op jit(solution)/shard_map/ppermute | solution.py:269
  85.4 13.5 %collective-permute-start.15 = (f32[256,256]{1,0:T(8,128)}, f32[256,256]{1,0:T(8,128)S(1)}, u32[]{:S(2)}, u32[]{:S(2)}) collective-permute-start(f32[256,256]{1,0:T(8,128)} %get-tuple-element.45), channel_id=1, source_target_pairs={{0,6},{1,4},{2,7},{3,5},{4,2},{5,0},{6,3},{7,1},{8,13},{9,15},{10,... | collective-permute-start | bytes 786440 | tf_op jit(solution)/shard_map/ppermute | solution.py:269
  85.4 13.5 %collective-permute-start.16 = (f32[256,256]{1,0:T(8,128)S(1)}, f32[256,256]{1,0:T(8,128)S(1)}, u32[]{:S(2)}, u32[]{:S(2)}) collective-permute-start(f32[256,256]{1,0:T(8,128)S(1)} %get-tuple-element.46.refs_4_), channel_id=1, source_target_pairs={{1,2},{2,1},{5,6},{6,5},{8,11},{11,8},{12,15},{15,12},{16,19},{19,... | collective-permute-start | bytes 786440 | tf_op jit(solution)/shard_map/ppermute | solution.py:269
  86.1 14.8 %collective-permute-start.17 = (f32[256,256]{1,0:T(8,128)}, f32[256,256]{1,0:T(8,128)S(1)}, u32[]{:S(2)}, u32[]{:S(2)}) collective-permute-start(f32[256,256]{1,0:T(8,128)} %get-tuple-element.47), channel_id=1, source_target_pairs={{0,2},{1,0},{2,3},{3,1},{4,6},{5,4},{6,7},{7,5},{8,9},{9,11},{10,8... | collective-permute-start | bytes 786440 | tf_op jit(solution)/shard_map/ppermute | solution.py:269
  90.7 10.2 %collective-permute-start.22 = (f32[256,256]{1,0:T(8,128)}, f32[256,256]{1,0:T(8,128)}, u32[]{:S(2)}, u32[]{:S(2)}) collective-permute-start(f32[256,256]{1,0:T(8,128)} %get-tuple-element.54), channel_id=1, source_target_pairs={{0,2},{1,3},{2,0},{3,1},{4,6},{5,7},{6,4},{7,5},{8,10},{9,11},{10,... | collective-permute-start | bytes 786440 | tf_op jit(solution)/shard_map/ppermute | solution.py:269
  93.5 7.5 %collective-permute-start.23 = (f32[256,256]{1,0:T(8,128)}, f32[256,256]{1,0:T(8,128)}, u32[]{:S(2)}, u32[]{:S(2)}) collective-permute-start(f32[256,256]{1,0:T(8,128)} %get-tuple-element.55), channel_id=1, source_target_pairs={{0,2},{1,3},{2,0},{3,1},{4,6},{5,7},{6,4},{7,5},{8,10},{9,11},{10,... | collective-permute-start | bytes 786440 | tf_op jit(solution)/shard_map/ppermute | solution.py:269
